TPU v7x, 256 devices: a whole 4x4x8 slice. The times are simulated.
256 devices in a mesh: lat: 16 (over y, x_hi, core), lon: 16 (over x_lo, z).
Axes of the slice: x: 4 (x_hi: 2, x_lo: 2; x = x_hi * 2 + x_lo), y: 4, z: 8, core: 2. Of those that a mesh axis runs over, the one named last changes fastest.
Arguments:
- field: bfloat16 [256, 512, 512], P('lat', 'lon'), may hold values from -6 to 6
- filter_values: bfloat16 [4, 256, 4, 4], replicated, may hold values from -1.5 to 1.5
- block_lat: int32 [256, 4], replicated, may hold values from -2 to 2, as said below
- block_lon: int32 [256, 4], replicated, may hold values from -16 to 13, as said below
- mixing: bfloat16 [4, 512, 512], replicated, may hold values from -0.125 to 0.125
- cotangent: bfloat16 [256, 512, 512], P('lat', 'lon'), may hold values from -6 to 6
Outputs:
- output: bfloat16 [256, 512, 512], P('lat', 'lon')
- field_grad: bfloat16 [256, 512, 512], P('lat', 'lon')
- mixing_grad: float32 [4, 512, 512], P(None, 'lat')
Inputs may be any that keep to these rules, and one draw needn't show every extreme that they name: Block b of output cycle i reads input cycle i + block_lat[i, b]; the latitude reach of a cycle grows toward the poles, and every cycle has blocks at both ends of its reach. Block b of output cycle i covers longitude offsets block_lon[i, b] to block_lon[i, b] + 3; the longitude reach of a cycle grows toward the poles, and every cycle has blocks at both ends of its reach.
All inputs are finite; a program needn't handle non-finite values.
Results may differ from a plain program's by a relative error of at most 0.0049.
Values may be sent and summed in bfloat16 or wider, within the bound.
No kernel may reach another device: no remote copies, remote signals or barrier semaphores. Data moves between devices by JAX's collectives and lax.ppermute only.
A program may use at most 128 MiB of HBM per device.

v0:
```python
import math

import jax
import jax.numpy as jnp
from jax import lax
from jax.sharding import PartitionSpec as P

HL = 2
WL = 16


def extended_2(cells, sides, width, closed):
    for axis, dim in sides:
        count = lax.axis_size(axis)
        ends = count if closed else count - 1
        head = lax.slice_in_dim(cells, 0, width, axis=dim)
        tail = lax.slice_in_dim(cells, cells.shape[dim] - width, cells.shape[dim], axis=dim)
        cells = jnp.concatenate(
            [
                lax.ppermute(tail, axis, [(i, (i + 1) % count) for i in range(ends)]),
                cells,
                lax.ppermute(head, axis, [((i + 1) % count, i) for i in range(ends)]),
            ],
            axis=dim,
        )
    return cells


def tap_matrix(psi_row, lat_row, lon_row, cols_out, cols_in, direction):
    block_width = psi_row.shape[2]
    lat_hot = (lat_row[:, None] + HL == jnp.arange(2 * HL + 1, dtype=jnp.int32)[None, :]).astype(
        jnp.float32
    )
    shift = direction * (lon_row[:, None] + jnp.arange(block_width, dtype=jnp.int32)[None, :])
    out_ids = jnp.arange(cols_out, dtype=jnp.int32)[:, None]
    in_ids = jnp.arange(cols_in, dtype=jnp.int32)[None, :]
    col_hot = (in_ids[None, None] == out_ids[None, None] + WL + shift[:, :, None, None]).astype(
        jnp.float32
    )
    return jnp.einsum(
        "kbw,bl,bwjq->kljq",
        psi_row.astype(jnp.float32),
        lat_hot,
        col_hot,
        precision=lax.Precision.HIGHEST,
    )


def forward_filter(extended, psi_local, lat_local, lon_local, band_rows, sector_cols):
    cols_in = extended.shape[1]

    def forward_one_cycle(row_index):
        taps = tap_matrix(
            psi_local[:, row_index],
            lat_local[row_index],
            lon_local[row_index],
            sector_cols,
            cols_in,
            1,
        )
        slab = lax.dynamic_slice_in_dim(extended, row_index, 2 * HL + 1, 0).astype(jnp.float32)
        return jnp.einsum("kljq,lqc->kjc", taps, slab, precision=lax.Precision.HIGHEST).astype(
            jnp.bfloat16
        )

    return lax.map(forward_one_cycle, jnp.arange(band_rows, dtype=jnp.int32))


def adjoint_push(back_mixed, psi_local, lat_local, lon_local, band_rows, sector_cols):
    cols_in = sector_cols + 2 * WL

    def adjoint_one_cycle(row_index):
        taps = tap_matrix(
            psi_local[:, row_index],
            lat_local[row_index],
            lon_local[row_index],
            sector_cols,
            cols_in,
            1,
        )
        slab = back_mixed[row_index].astype(jnp.float32)
        return jnp.einsum("kljq,kjc->lqc", taps, slab, precision=lax.Precision.HIGHEST)

    placed = lax.map(adjoint_one_cycle, jnp.arange(band_rows, dtype=jnp.int32))
    buffer = jnp.pad(placed[:, 0], ((0, 2 * HL), (0, 0), (0, 0)))
    for lat_step in range(1, 2 * HL + 1):
        buffer = buffer + jnp.pad(
            placed[:, lat_step], ((lat_step, 2 * HL - lat_step), (0, 0), (0, 0))
        )
    return buffer


def fold_rims(buffer, band_rows, sector_cols):
    west_east = jnp.concatenate([buffer[:, :WL], buffer[:, WL + sector_cols :]], axis=1)
    arrived = extended_2(west_east, (("lon", 1),), WL, True)
    interior = buffer[:, WL : WL + sector_cols]
    interior = interior.at[:, :WL].add(arrived[:, :WL])
    interior = interior.at[:, sector_cols - WL :].add(arrived[:, 3 * WL :])
    north_south = jnp.concatenate([interior[:HL], interior[HL + band_rows :]], axis=0)
    landed = extended_2(north_south, (("lat", 0),), HL, False)
    middle = interior[HL : HL + band_rows]
    middle = middle.at[:HL].add(landed[:HL])
    middle = middle.at[band_rows - HL :].add(landed[3 * HL :])
    return middle


def local(field, filter_values, block_lat, block_lon, mixing, cotangent):
    band_rows, sector_cols, channels = field.shape
    first_cycle = lax.axis_index("lat") * band_rows
    psi_local = lax.dynamic_slice_in_dim(filter_values, first_cycle, band_rows, 1)
    lat_local = lax.dynamic_slice_in_dim(block_lat, first_cycle, band_rows, 0)
    lon_local = lax.dynamic_slice_in_dim(block_lon, first_cycle, band_rows, 0)
    field_band = extended_2(field, (("lat", 0),), HL, False)
    extended = extended_2(field_band, (("lon", 1),), WL, True)
    filtered = forward_filter(extended, psi_local, lat_local, lon_local, band_rows, sector_cols)
    output = jnp.einsum(
        "rkjc,kcd->rjd", filtered, mixing, preferred_element_type=jnp.float32
    ).astype(jnp.bfloat16)
    weight_terms = jnp.einsum(
        "rkjc,rjd->kcd", filtered, cotangent, preferred_element_type=jnp.float32
    )
    back_mixed = jnp.einsum(
        "rjd,kcd->rkjc", cotangent, mixing, preferred_element_type=jnp.float32
    ).astype(jnp.bfloat16)
    buffer = adjoint_push(back_mixed, psi_local, lat_local, lon_local, band_rows, sector_cols)
    gradient = fold_rims(buffer, band_rows, sector_cols)
    field_grad = gradient.astype(jnp.bfloat16)
    sector_total = lax.psum(weight_terms, "lon")
    summed = lax.psum_scatter(sector_total, "lat", scatter_dimension=1, tiled=True)
    normalizer = 1.0 / math.sqrt(
        band_rows * lax.axis_size("lat") * sector_cols * lax.axis_size("lon")
    )
    mixing_grad = summed * normalizer
    return (output, field_grad, mixing_grad)


def solution(mesh):
    return jax.shard_map(
        local,
        mesh=mesh,
        in_specs=(P("lat", "lon", None), P(), P(), P(), P(), P("lat", "lon", None)),
        out_specs=(P("lat", "lon", None), P("lat", "lon", None), P(None, "lat", None)),
        check_vma=False,
    )
```

profile of v0, /device:TPU:2, one launch (start us, length us, event | category | flops | bytes accessed | tf_op | source)
XLA Modules:
  0.0 427.0 jit_solution(2171400840934537817)
XLA Ops:
  7.2 1.0 fusion.53
  8.3 1.7 collective-permute-start
  10.0 1.3 collective-permute-start.1
  11.3 0.8 constant_dynamic-slice_fusion.4
  12.3 0.8 constant_dynamic-slice_fusion.5
  13.3 1.1 constant_dynamic-update-slice_fusion.1
  14.4 0.7 collective-permute-done.1
  15.1 2.0 collective-permute-start.2
  17.1 4.9 %collective-permute-start.3 = (bf16[20,16,512]{2,1,0:T(8,128)(2,1)S(1)}, bf16[20,16,512]{2,1,0:T(8,128)(2,1)S(1)}, u32[]{:S(2)}, u32[]{:S(2)}) collective-permute-start(bf16[20,16,512]{2,1,0:T(8,128)(2,1)S(1)} %get-tuple-element.197), channel_id=1, source_target_pairs={{1,0},{2,1},{3,2},{4,3},{5,4},{6,5},{7,6},{8,7},{9,8},{10,9},{11,1... | collective-permute-start | bytes 983048 | tf_op jit(solution)/shard_map/ppermute | solution.py:22
  22.0 2.6 convert_bitcast_fusion
  24.6 2.4 collective-permute-done.2
  27.0 1.2 pad_maximum_fusion
  28.2 113.0 %while.24 = (s32[]{:T(128)}, bf16[16,4,32,512]{3,2,1,0:T(8,128)(2,1)}, s32[16]{0:T(128)S(1)}, s32[16,4]{1,0:T(8,128)S(1)}, bf16[4,16,4,4]{3,2,0,1:T(4,128)(2,1)S...) while((s32[]{:T(128)}, ...), condition=%wide.region_1.2_spmd, body=%wide.region_0.1_spmd.sunk | while | flops 253985360 | bytes 1054240 | solution.py:66
  33.1 2.1 fusion.79
  40.2 2.1 fusion.79
  47.2 2.1 fusion.79
  54.3 2.1 fusion.79
  61.3 2.2 fusion.79
  68.4 2.2 fusion.79
  75.5 2.1 fusion.79
  80.7 0.6 convolution_bitcast_fusion.7
  82.6 2.1 fusion.79
  89.6 2.2 fusion.79
  94.8 0.6 convolution_bitcast_fusion.7
  96.7 2.1 fusion.79
  103.7 2.2 fusion.79
  110.8 2.1 fusion.79
  117.9 2.2 fusion.79
  124.9 2.1 fusion.79
  132.0 2.1 fusion.79
  139.1 2.1 fusion.79
  141.2 4.9 %convolution_bitcast_fusion.4 = f32[4,512,512]{2,1,0:T(8,128)} fusion(bf16[16,4,32,512]{3,2,1,0:T(8,128)(2,1)} %get-tuple-element.125, bf16[16,32,512]{2,1,0:T(8,128)(2,1)S(1)} %copy-done.2), kind=kOutput, calls=%fused_computation.51 | convolution fusion | flops 1073741824 | bytes 6815744 | tf_op jit(solution)/shard_map/rkjc,rjd->kcd/dot_general | solution.py:119
  146.2 95.5 %while.25 = (s32[]{:T(128)}, f32[16,5,64,512]{3,2,0,1:T(8,128)}, s32[16]{0:T(128)S(1)}, s32[16,4]{1,0:T(8,128)S(1)}, bf16[4,16,4,4]{3,2,0,1:T(4,128)(2,1)S(1)}, ...) while((s32[]{:T(128)}, f32[16,5,64,512]{3,2,0,1:T(8,128)}, ...), condition=%wide.region_3.4_spmd, body=%wide.region_2.3_spmd.sunk | while | flops 253919824 | bytes 1381887 | solution.py:84
  149.9 2.3 fusion.87
  155.8 2.3 fusion.87
  161.8 2.4 fusion.87
  167.8 2.3 fusion.87
  173.8 2.4 fusion.87
  179.7 2.4 fusion.87
  185.7 2.3 fusion.87
  191.7 2.3 fusion.87
  197.7 2.3 fusion.87
  203.6 2.3 fusion.87
  209.6 2.4 fusion.87
  215.5 2.3 fusion.87
  221.5 2.4 fusion.87
  227.5 2.3 fusion.87
  233.4 2.3 fusion.87
  239.4 2.4 fusion.87
  241.8 5.5 %slice_bitcast_fusion.4 = (f32[16,64,512]{2,1,0:T(8,128)S(1)}, f32[16,64,512]{2,1,0:T(8,128)S(1)}, f32[16,64,512]{2,1,0:T(8,128)S(1)}, f32[16,64,512]{2,1,0:T(8,128)S(1)}, f32[16,64,512]{2,1,0:T(8,128)S(1)}) fusion(f32[16,5,64,512]{3,2,0,1:T(8,128)} %get-tuple-element.126), kind=kLoop, calls=%fused_computation.60 | loop fusion | bytes 20971520 | tf_op jit(solution)/shard_map/squeeze | solution.py:85
  247.2 1.4 pad_add_fusion
  248.9 4.3 %collective-permute-start.5 = (f32[20,16,512]{2,1,0:T(8,128)S(1)}, f32[20,16,512]{2,1,0:T(8,128)S(1)}, u32[]{:S(2)}, u32[]{:S(2)}) collective-permute-start(f32[20,16,512]{2,1,0:T(8,128)S(1)} %get-tuple-element.192), channel_id=1, source_target_pairs={{1,0},{2,1},{3,2},{4,3},{5,4},{6,5},{7,6},{8,7},{9,8},{10,9},{11,1... | collective-permute-start | bytes 1966088 | tf_op jit(solution)/shard_map/ppermute | solution.py:22
  253.3 12.7 %collective-permute-done.4 = f32[20,16,512]{2,1,0:T(8,128)S(1)} collective-permute-done((f32[20,16,512]{2,1,0:T(8,128)S(1)}, f32[20,16,512]{2,1,0:T(8,128)S(1)}, u32[]{:S(2)}, u32[]{:S(2)}) %collective-permute-start.4) | collective-permute-done | bytes 655392 | tf_op jit(solution)/shard_map/ppermute | solution.py:20
  266.3 0.7 fusion.51
  267.0 4.4 %collective-permute-start.6 = (f32[2,32,512]{2,1,0:T(8,128)}, f32[2,32,512]{2,1,0:T(8,128)S(1)}, u32[]{:S(2)}, u32[]{:S(2)}) collective-permute-start(f32[2,32,512]{2,1,0:T(8,128)} %get-tuple-element.195), channel_id=1, source_target_pairs={{0,16},{16,32},{32,48},{48,64},{64,80},{80,96},{96,112},{112,128},... | collective-permute-start | bytes 393224 | tf_op jit(solution)/shard_map/ppermute | solution.py:20
  271.5 2.0 fusion.41
  273.5 1.1 slice.169
  274.6 1.3 collective-permute-start.7
  275.9 0.7 fusion.49
  276.6 8.9 %collective-permute-done.7 = f32[2,32,512]{2,1,0:T(8,128)} collective-permute-done((f32[2,32,512]{2,1,0:T(8,128)}, f32[2,32,512]{2,1,0:T(8,128)}, u32[]{:S(2)}, u32[]{:S(2)}) %collective-permute-start.7) | collective-permute-done | bytes 131104 | tf_op jit(solution)/shard_map/ppermute | solution.py:22
  285.5 1.6 fusion.48
  287.1 2.1 convert_element_type.36
  289.2 129.3 %all-reduce.7.cloned.1.call-done = f32[4,32,512]{2,1,0:T(8,128)} async-done(((f32[4,32,512]{2,1,0:T(8,128)}), f32[4,32,512]{2,1,0:T(8,128)}) %all-reduce.7.cloned.1.call-update) | async-done | bytes 262160 | tf_op jit(solution)/shard_map/psum | solution.py:128
  418.5 1.7 broadcast_multiply_fusion
  (284 shorter events, 53.0 us)
Async XLA Ops:
  7.2 14.9 %copy-start = (bf16[4,512,512]{2,1,0:T(8,128)(2,1)S(1)}, bf16[4,512,512]{2,1,0:T(8,128)(2,1)}, u32[]{:S(2)}) copy-start(bf16[4,512,512]{2,1,0:T(8,128)(2,1)} %param.22) | copy-start | bytes 6291460
  7.2 14.9 %copy-start.2 = (bf16[16,32,512]{2,1,0:T(8,128)(2,1)S(1)}, bf16[16,32,512]{2,1,0:T(8,128)(2,1)}, u32[]{:S(2)}) copy-start(bf16[16,32,512]{2,1,0:T(8,128)(2,1)} %param.23) | copy-start | bytes 1572868
  7.2 268.7 %reduce-scatter.2.cloned.1.call-start = ((), (), s32[]{:S(2)}) async-start(), calls=%async_computation.1 | async-start | bytes 4456448 | tf_op jit(solution)/shard_map/reduce_scatter | solution.py:129
  8.3 5.0 %collective-permute-start = (bf16[2,32,512]{2,1,0:T(8,128)(2,1)S(1)}, bf16[2,32,512]{2,1,0:T(8,128)(2,1)S(1)}, u32[]{:S(2)}, u32[]{:S(2)}) collective-permute-start(bf16[2,32,512]{2,1,0:T(8,128)(2,1)S(1)} %get-tuple-element.199), channel_id=1, source_target_pairs={{0,16},{16,32},{32,48},{48,64},{64,80},{80,96},{96,112},{112,128},... | collective-permute-start | bytes 196616 | tf_op jit(solution)/shard_map/ppermute | solution.py:20
  10.0 5.1 %collective-permute-start.1 = (bf16[2,32,512]{2,1,0:T(8,128)(2,1)S(1)}, bf16[2,32,512]{2,1,0:T(8,128)(2,1)S(1)}, u32[]{:S(2)}, u32[]{:S(2)}) collective-permute-start(bf16[2,32,512]{2,1,0:T(8,128)(2,1)S(1)} %get-tuple-element.198), channel_id=1, source_target_pairs={{16,0},{32,16},{48,32},{64,48},{80,64},{96,80},{112,96},{128,112},... | collective-permute-start | bytes 196616 | tf_op jit(solution)/shard_map/ppermute | solution.py:22
  15.1 11.9 %collective-permute-start.2 = (bf16[20,16,512]{2,1,0:T(8,128)(2,1)S(1)}, bf16[20,16,512]{2,1,0:T(8,128)(2,1)S(1)}, u32[]{:S(2)}, u32[]{:S(2)}) collective-permute-start(bf16[20,16,512]{2,1,0:T(8,128)(2,1)S(1)} %get-tuple-element.196), channel_id=1, source_target_pairs={{0,1},{1,2},{2,3},{3,4},{4,5},{5,6},{6,7},{7,8},{8,9},{9,10},{10,1... | collective-permute-start | bytes 983048 | tf_op jit(solution)/shard_map/ppermute | solution.py:20
  17.1 9.9 %collective-permute-start.3 = (bf16[20,16,512]{2,1,0:T(8,128)(2,1)S(1)}, bf16[20,16,512]{2,1,0:T(8,128)(2,1)S(1)}, u32[]{:S(2)}, u32[]{:S(2)}) collective-permute-start(bf16[20,16,512]{2,1,0:T(8,128)(2,1)S(1)} %get-tuple-element.197), channel_id=1, source_target_pairs={{1,0},{2,1},{3,2},{4,3},{5,4},{6,5},{7,6},{8,7},{9,8},{10,9},{11,1... | collective-permute-start | bytes 983048 | tf_op jit(solution)/shard_map/ppermute | solution.py:22
  146.2 272.3 %all-reduce.7.cloned.1.call-start = ((), (), s32[]{:S(2)}) async-start(), calls=%async_computation.2 | async-start | bytes 524288 | tf_op jit(solution)/shard_map/psum | solution.py:128
  248.8 17.2 %collective-permute-start.4 = (f32[20,16,512]{2,1,0:T(8,128)S(1)}, f32[20,16,512]{2,1,0:T(8,128)S(1)}, u32[]{:S(2)}, u32[]{:S(2)}) collective-permute-start(f32[20,16,512]{2,1,0:T(8,128)S(1)} %get-tuple-element.193), channel_id=1, source_target_pairs={{0,1},{1,2},{2,3},{3,4},{4,5},{5,6},{6,7},{7,8},{8,9},{9,10},{10,1... | collective-permute-start | bytes 1966088 | tf_op jit(solution)/shard_map/ppermute | solution.py:20
  248.9 17.3 %collective-permute-start.5 = (f32[20,16,512]{2,1,0:T(8,128)S(1)}, f32[20,16,512]{2,1,0:T(8,128)S(1)}, u32[]{:S(2)}, u32[]{:S(2)}) collective-permute-start(f32[20,16,512]{2,1,0:T(8,128)S(1)} %get-tuple-element.192), channel_id=1, source_target_pairs={{1,0},{2,1},{3,2},{4,3},{5,4},{6,5},{7,6},{8,7},{9,8},{10,9},{11,1... | collective-permute-start | bytes 1966088 | tf_op jit(solution)/shard_map/ppermute | solution.py:22
  253.3 18.1 %copy-start.1 = (bf16[16,4,32,512]{3,2,1,0:T(8,128)(2,1)S(1)}, bf16[16,4,32,512]{3,2,1,0:T(8,128)(2,1)}, u32[]{:S(2)}) copy-start(bf16[16,4,32,512]{3,2,1,0:T(8,128)(2,1)} %get-tuple-element.125) | copy-start | bytes 6291460
  267.0 8.9 %collective-permute-start.6 = (f32[2,32,512]{2,1,0:T(8,128)}, f32[2,32,512]{2,1,0:T(8,128)S(1)}, u32[]{:S(2)}, u32[]{:S(2)}) collective-permute-start(f32[2,32,512]{2,1,0:T(8,128)} %get-tuple-element.195), channel_id=1, source_target_pairs={{0,16},{16,32},{32,48},{48,64},{64,80},{80,96},{96,112},{112,128},... | collective-permute-start | bytes 393224 | tf_op jit(solution)/shard_map/ppermute | solution.py:20
  274.6 10.9 %collective-permute-start.7 = (f32[2,32,512]{2,1,0:T(8,128)}, f32[2,32,512]{2,1,0:T(8,128)}, u32[]{:S(2)}, u32[]{:S(2)}) collective-permute-start(f32[2,32,512]{2,1,0:T(8,128)} %get-tuple-element.194), channel_id=1, source_target_pairs={{16,0},{32,16},{48,32},{64,48},{80,64},{96,80},{112,96},{128,112},... | collective-permute-start | bytes 393224 | tf_op jit(solution)/shard_map/ppermute | solution.py:22
Sparse Core Ops, SparseCore 0:
  146.3 93.9 reduce-scatter.1
  276.0 142.4 all-reduce.6
where the time goes:
time: 430 us; the launch traced here: 427 us
  waiting for transfers between devices  154 us (36%)
  matrix products  110 us (26%)
  loops' own time  83.7 us (19%)
  local copies, waits for them, and re-layouts  30.4 us (7%)
  starting transfers between devices  20.1 us (5%)
  between operations  14.3 us (3%)
  other arithmetic  14.1 us (3%)
    psum x1, waiting for transfers between devices, local(): sector_total = lax.psum(weight_terms, 'lon')  129 us
    another operation x1, loops' own time, forward_filter(): return lax.map(forward_one_cycle, jnp.arange(band_rows, dtype=jnp.int32))  52.2 us
    dot_general x16, matrix products, adjoint_one_cycle(): jnp.einsum('kljq,kjc->lqc', taps, slab, precision=lax.Precision.HIGHEST)  37.5 us
    dot_general x16, matrix products, forward_one_cycle(): jnp.einsum('kljq,lqc->kjc', taps, slab, precision=lax.Precision.HIGHEST)  34.3 us
    another operation x1, loops' own time, adjoint_push(): placed = lax.map(adjoint_one_cycle, jnp.arange(band_rows, dtype=jnp.int32))  31.5 us
    dot_general x64, matrix products, tap_matrix(): jnp.einsum('kbw,bl,bwjq->kljq', psi_row.astype(jnp.float32), lat_hot, col...  29 us
    dynamic_slice x32, local copies, waits for them, and re-layouts, forward_filter(): return lax.map(forward_one_cycle, jnp.arange(band_rows, dtype=jnp.int32))  18.6 us
    ppermute x4, waiting for transfers between devices, extended_2(): lax.ppermute(tail, axis, [(i, (i + 1) % count) for i in range(ends)])  15 us
  transfers between devices with their start and end apart: 10, of which 5 were waited for; matrix products, arithmetic and copies ran while one was open for 20% of the time, Pallas kernels for 0%

commit v1 on v0

v1 whole, which is shorter than its diff:
```python
import math

import jax
import jax.numpy as jnp
from jax import lax
from jax.experimental import pallas as pl
from jax.experimental.pallas import tpu as pltpu
from jax.sharding import Mesh
from jax.sharding import PartitionSpec as P

HL = 2
WL = 16
BW = 4
SPAN = 2 * HL + 1
F32 = jnp.float32
BF16 = jnp.bfloat16
VMEM = pl.BlockSpec(memory_space=pltpu.VMEM)
SMEM = pl.BlockSpec(memory_space=pltpu.SMEM)
PARAMS = pltpu.CompilerParams(vmem_limit_bytes=48 * 1024 * 1024)


def picked(distance, weights, basis, taps):
    value = jnp.zeros(distance.shape, F32)
    for tap in range(taps):
        row = weights[basis * taps + tap : basis * taps + tap + 1, :]
        value = jnp.where(distance == tap, row, value)
    return value


def taps_kernel(first, bank, fwd_out, adj_out):
    rows, basis_rows, _ = fwd_out.shape
    blocks, lines, cycles = bank.shape
    taps = BW
    basis_count = (lines - 2) // taps
    cols = basis_rows // basis_count
    wide = cols + 2 * WL
    near = 128 // blocks

    def iota(shape, axis):
        return lax.broadcasted_iota(jnp.int32, shape, axis)

    cycle = iota((cycles, 128), 0) - first[0] + HL
    slot = iota((cycles, 128), 1)
    fwd_bank = jnp.zeros((lines, 128), F32)
    adj_banks = []
    for block in range(blocks):
        lines_here = bank[block]
        hot = (slot == cycle + block * near) & (cycle >= 0) & (cycle < near)
        fwd_bank += jnp.dot(lines_here, hot.astype(BF16), preferred_element_type=F32)
        hot = (slot == cycle) & (cycle < near)
        adj_banks.append(jnp.dot(lines_here, hot.astype(BF16), preferred_element_type=F32))
    fwd_bank = fwd_bank.astype(BF16)
    adj_banks = [adj_bank.astype(BF16) for adj_bank in adj_banks]
    fwd_wide = blocks * wide
    adj_wide = SPAN * wide
    fwd_slot = iota((128, fwd_wide), 0) - (iota((128, fwd_wide), 1) // wide) * near - HL
    adj_slot = iota((128, adj_wide), 0) - iota((128, adj_wide), 1) // wide
    fwd_base = iota((cols, fwd_wide), 1) % wide - iota((cols, fwd_wide), 0) - WL
    adj_base = iota((cols, adj_wide), 0) - iota((cols, adj_wide), 1) % wide + WL
    adj_turn = HL - iota((1, adj_wide), 1) // wide

    def one_row(row, carry):
        hot = (fwd_slot == row).astype(BF16)
        weights = jnp.dot(fwd_bank, hot, preferred_element_type=F32)
        shift = weights[lines - 2 : lines - 1, :].astype(jnp.int32)
        distance = fwd_base - shift
        for basis in range(basis_count):
            value = picked(distance, weights, basis, taps)
            fwd_out[row, basis * cols : (basis + 1) * cols, :] = value.astype(BF16)
        hot = (adj_slot == row).astype(BF16)
        totals = [None] * basis_count
        for block in range(blocks):
            weights = jnp.dot(adj_banks[block], hot, preferred_element_type=F32)
            shift = weights[lines - 2 : lines - 1, :].astype(jnp.int32)
            turn = weights[lines - 1 : lines, :].astype(jnp.int32)
            distance = jnp.where(turn == adj_turn, adj_base - shift, -1)
            for basis in range(basis_count):
                value = picked(distance, weights, basis, taps)
                totals[basis] = value if block == 0 else totals[basis] + value
        for basis in range(basis_count):
            adj_out[row, basis * cols : (basis + 1) * cols, :] = totals[basis].astype(BF16)
        return carry

    lax.fori_loop(0, rows, one_row, 0, unroll=2)


def assemble(extended, center, west, east, north, south):
    rows, cols, _ = center.shape
    extended[HL : HL + rows, 0:WL] = west[...]
    extended[HL : HL + rows, WL : WL + cols] = center[...]
    extended[HL : HL + rows, WL + cols :] = east[...]
    extended[0:HL] = north[...]
    extended[HL + rows :] = south[...]


def filter_kernel(first, lat, taps, center, west, east, north, south, cot, weight_out, filt_out, extended):
    rows, cols, channels = center.shape
    basis_count = filt_out.shape[0]
    blocks = lat.shape[0]
    assemble(extended, center, west, east, north, south)

    def one_row(row, carry):
        slabs = [extended[row + HL + lat[block, first[0] + row]] for block in range(blocks)]
        slab = jnp.concatenate(slabs, axis=0)
        filtered = jnp.dot(taps[row], slab, preferred_element_type=F32).astype(BF16)
        filt_out[:, row] = filtered.reshape(basis_count, cols, channels)
        return carry

    lax.fori_loop(0, rows, one_row, 0, unroll=4)
    cot_flat = cot[...].reshape(rows * cols, channels)
    shares = weight_out.shape[0]
    for basis in range(basis_count):
        filtered = filt_out[basis].reshape(rows * cols, channels)
        terms = lax.dot_general(
            filtered, cot_flat, (((0,), (0,)), ((), ())), preferred_element_type=F32
        )
        weight_out[:, basis] = terms.reshape(shares, channels // shares, channels).astype(
            weight_out.dtype
        )


def output_kernel(filt, mixing, out):
    basis_count, rows, cols, channels = filt.shape
    total = None
    for basis in range(basis_count):
        part = jnp.dot(
            filt[basis].reshape(rows * cols, channels), mixing[basis], preferred_element_type=F32
        )
        total = part if total is None else total + part
    out[...] = total.reshape(rows, cols, channels).astype(BF16)


def adjoint_kernel(taps, center, west, east, north, south, mixing, out, extended, spread):
    rows, cols, channels = center.shape
    basis_count = mixing.shape[0]
    assemble(extended, center, west, east, north, south)

    def one_row(row, carry):
        slab = extended[pl.ds(row, SPAN)].reshape(SPAN * (cols + 2 * WL), channels)
        pulled = jnp.dot(taps[row], slab, preferred_element_type=F32).astype(BF16)
        spread[:, row] = pulled.reshape(basis_count, cols, channels)
        return carry

    lax.fori_loop(0, rows, one_row, 0, unroll=4)
    total = None
    for basis in range(basis_count):
        part = lax.dot_general(
            spread[basis].reshape(rows * cols, channels),
            mixing[basis],
            (((1,), (1,)), ((), ())),
            preferred_element_type=F32,
        )
        total = part if total is None else total + part
    out[...] = total.reshape(rows, cols, channels).astype(BF16)


def ring(step, count):
    return [(i, (i + step) % count) for i in range(count)]


def halo(cells):
    rows, cols, _ = cells.shape
    lons = lax.axis_size("lon")
    lats = lax.axis_size("lat")
    west = lax.ppermute(cells[:, cols - WL :], "lon", ring(1, lons))
    east = lax.ppermute(cells[:, :WL], "lon", ring(-1, lons))
    tail = jnp.concatenate([a[rows - HL :] for a in (west, cells, east)], axis=1)
    head = jnp.concatenate([a[:HL] for a in (west, cells, east)], axis=1)
    north = lax.ppermute(tail, "lat", [(i, i + 1) for i in range(lats - 1)])
    south = lax.ppermute(head, "lat", [(i + 1, i) for i in range(lats - 1)])
    return west, east, north, south


def local(field, filter_values, block_lat, block_lon, mixing, cotangent):
    rows, cols, channels = field.shape
    basis_count, _, blocks, taps = filter_values.shape
    first = (lax.axis_index("lat") * rows).astype(jnp.int32).reshape(1)
    field_halo = halo(field)
    cot_halo = halo(cotangent)

    psi_lines = filter_values.transpose(2, 0, 3, 1).reshape(blocks, basis_count * taps, -1)
    lat_lines = block_lat.T
    lon_lines = block_lon.T
    bank = jnp.concatenate(
        [psi_lines, lon_lines[:, None].astype(BF16), lat_lines[:, None].astype(BF16)], axis=1
    )
    wide = cols + 2 * WL
    fwd_taps, adj_taps = pl.pallas_call(
        taps_kernel,
        out_shape=(
            jax.ShapeDtypeStruct((rows, basis_count * cols, blocks * wide), BF16),
            jax.ShapeDtypeStruct((rows, basis_count * cols, SPAN * wide), BF16),
        ),
        in_specs=[SMEM, VMEM],
        out_specs=(VMEM, VMEM),
        compiler_params=PARAMS,
        name="taps",
    )(first, bank)

    lat_count = lax.axis_size("lat")
    share = channels // lat_count
    terms, filtered = pl.pallas_call(
        filter_kernel,
        out_shape=(
            jax.ShapeDtypeStruct((lat_count, basis_count, share, channels), BF16),
            jax.ShapeDtypeStruct((basis_count, rows, cols, channels), BF16),
        ),
        in_specs=[SMEM] * 2 + [VMEM] * 7,
        out_specs=(VMEM, VMEM),
        scratch_shapes=[pltpu.VMEM((rows + 2 * HL, wide, channels), BF16)],
        compiler_params=PARAMS,
        name="filtering",
    )(first, lat_lines, fwd_taps, field, *field_halo, cotangent)

    output = pl.pallas_call(
        output_kernel,
        out_shape=jax.ShapeDtypeStruct((rows, cols, channels), BF16),
        in_specs=[VMEM] * 2,
        out_specs=VMEM,
        compiler_params=PARAMS,
        name="mixed",
    )(filtered, mixing)

    field_grad = pl.pallas_call(
        adjoint_kernel,
        out_shape=jax.ShapeDtypeStruct((rows, cols, channels), BF16),
        in_specs=[VMEM] * 7,
        out_specs=VMEM,
        scratch_shapes=[
            pltpu.VMEM((rows + 2 * HL, wide, channels), BF16),
            pltpu.VMEM((basis_count, rows, cols, channels), BF16),
        ],
        compiler_params=PARAMS,
        name="adjoint",
    )(adj_taps, cotangent, *cot_halo, mixing)

    normalizer = 1.0 / math.sqrt(rows * lat_count * cols * lax.axis_size("lon"))
    summed = reduced(terms)
    return (output, field_grad, summed * normalizer)


def reduced(terms):
    summed = lax.psum_scatter(terms.astype(F32), "lat", scatter_dimension=0, tiled=True)
    return lax.psum(summed[0], "lon")


def solution(mesh):
    return jax.shard_map(
        local,
        mesh=mesh,
        in_specs=(P("lat", "lon", None), P(), P(), P(), P(), P("lat", "lon", None)),
        out_specs=(P("lat", "lon", None), P("lat", "lon", None), P(None, "lat", None)),
        check_vma=False,
    )
```

time: 430 us -> 274 us (0.64)
  matrix products: 110 us -> 0 us
  loops' own time: 83.7 us -> 0 us
  waiting for transfers between devices: 154 us -> 221 us
  local copies, waits for them, and re-layouts: 30.4 us -> 3.75 us
  Pallas kernels: 0 us -> 14.8 us
  other arithmetic: 14.1 us -> 5.61 us
  starting transfers between devices: 20.1 us -> 13.3 us
    dot_general x99 -> x0, matrix products: 110 us -> none  [the longest x16 37.5 us: adjoint_one_cycle(): jnp.einsum('kljq,kjc->lqc', taps, slab, precision=lax.Precision.HIGHEST)]
    another operation x2 -> x0, loops' own time: 83.7 us -> none  [the longest x1 52.2 us: forward_filter(): return lax.map(forward_one_cycle, jnp.arange(band_rows, dtype=jnp.int32))]
    reduce_scatter x1, waiting for transfers between devices: 0.02 us -> 79.9 us  [reduced(): lax.psum_scatter(terms.astype(F32), 'lat', scatter_dimension=0, tiled=True)]
    dynamic_slice x34 -> x0, local copies, waits for them, and re-layouts: 20.2 us -> none  [the longest x32 18.6 us: forward_filter(): return lax.map(forward_one_cycle, jnp.arange(band_rows, dtype=jnp.int32))]
    pallas_call x0 -> x4, Pallas kernels: none -> 14.8 us  [the longest x1 5.61 us: local(): pl.pallas_call(taps_kernel, out_shape=(jax.ShapeDtypeStruct((rows, basis_...]
    ppermute x8, waiting for transfers between devices: 24.6 us -> 15.4 us  [the longest x2 8.32 us: halo(): east = lax.ppermute(cells[:, :WL], 'lon', ring(-1, lons))]
    ppermute x8, starting transfers between devices: 20 us -> 13.2 us  [the longest x2 6.29 us: halo(): east = lax.ppermute(cells[:, :WL], 'lon', ring(-1, lons))]
    add x129 -> x0, other arithmetic: 6.54 us -> none  [the longest x64 2.65 us: tap_matrix(): lon_row[:, None] + jnp.arange(block_width, dtype=jnp.int32)[None, :]]
  transfers between devices with their start and end apart: 10 -> 10, of which waited for: 5 -> 7; matrix products, arithmetic and copies ran while one was open for 20% -> 1% of each run, Pallas kernels for 0% -> 4%
where the time goes in v1:
time: 274 us; the launch traced here: 273 us
  waiting for transfers between devices  221 us (81%)
  Pallas kernels  14.8 us (5%)
  between operations  14.3 us (5%)
  starting transfers between devices  13.3 us (5%)
  other arithmetic  5.61 us (2%)
  local copies, waits for them, and re-layouts  3.75 us (1%)
    psum x1, waiting for transfers between devices, reduced(): return lax.psum(summed[0], 'lon')  125 us
    reduce_scatter x1, waiting for transfers between devices, reduced(): lax.psum_scatter(terms.astype(F32), 'lat', scatter_dimension=0, tiled=True)  79.9 us
    ppermute x2, waiting for transfers between devices, halo(): east = lax.ppermute(cells[:, :WL], 'lon', ring(-1, lons))  8.32 us
    ppermute x2, waiting for transfers between devices, halo(): west = lax.ppermute(cells[:, cols - WL:], 'lon', ring(1, lons))  6.72 us
    ppermute x2, starting transfers between devices, halo(): east = lax.ppermute(cells[:, :WL], 'lon', ring(-1, lons))  6.29 us
    pallas_call x1, Pallas kernels, local(): pl.pallas_call(taps_kernel, out_shape=(jax.ShapeDtypeStruct((rows, basis_...  5.61 us
  transfers between devices with their start and end apart: 10, of which 7 were waited for; matrix products, arithmetic and copies ran while one was open for 1% of the time, Pallas kernels for 4%

profile of v1, /device:TPU:2, one launch (start us, length us, event | category | flops | bytes accessed | tf_op | source)
XLA Modules:
  0.0 272.6 jit_solution(12020574437278766747)
XLA Ops:
  7.2 0.0 copy-start.2
  7.2 0.0 copy-start.6
  7.2 0.0 copy-start.7
  7.2 0.0 copy-start.1
  7.2 0.0 reduce-scatter.2.cloned.1.call-start
  7.3 1.1 fusion.3
  8.4 5.9 %collective-permute-start.1 = (bf16[16,16,512]{2,1,0:T(8,128)(2,1)S(1)}, bf16[16,16,512]{2,1,0:T(8,128)(2,1)S(1)}, u32[]{:S(2)}, u32[]{:S(2)}) collective-permute-start(bf16[16,16,512]{2,1,0:T(8,128)(2,1)S(1)} %get-tuple-element.17), channel_id=1, source_target_pairs={{0,15},{1,0},{2,1},{3,2},{4,3},{5,4},{6,5},{7,6},{8,7},{9,8},{10,9... | collective-permute-start | bytes 786440 | tf_op jit(solution)/shard_map/ppermute | solution.py:166
  14.3 0.0 collective-permute-start
  14.3 0.9 fusion.2
  15.2 0.7 convert_bitcast_fusion.1
  15.9 4.0 %collective-permute-done.1.east = bf16[16,16,512]{2,1,0:T(8,128)(2,1)S(1)} collective-permute-done((bf16[16,16,512]{2,1,0:T(8,128)(2,1)S(1)}, bf16[16,16,512]{2,1,0:T(8,128)(2,1)S(1)}, u32[]{:S(2)}, u32[]{:S(2)}) %collective-permute-start.1) | collective-permute-done | bytes 262176 | tf_op jit(solution)/shard_map/ppermute | solution.py:166
  19.9 4.3 %collective-permute-done.west = bf16[16,16,512]{2,1,0:T(8,128)(2,1)S(1)} collective-permute-done((bf16[16,16,512]{2,1,0:T(8,128)(2,1)S(1)}, bf16[16,16,512]{2,1,0:T(8,128)(2,1)S(1)}, u32[]{:S(2)}, u32[]{:S(2)}) %collective-permute-start) | collective-permute-done | bytes 262176 | tf_op jit(solution)/shard_map/ppermute | solution.py:165
  24.2 1.3 collective-permute-start.2
  25.5 0.7 pad_maximum_fusion.1
  26.2 1.3 collective-permute-start.3
  27.5 0.0 copy-done.6
  27.5 0.0 copy-done.7
  27.6 5.6 %taps.1 = (bf16[16,128,256]{2,1,0:T(8,128)(2,1)S(1)}, bf16[16,128,320]{2,1,0:T(8,128)(2,1)S(1)}) custom-call(s32[1]{0:T(128)} %bitcast.first, bf16[4,18,256]{2,1,0:T(8,128)(2,1)S(1)} %pad_maximum_fusion.4.bank), custom_call_target="tpu_custom_call" | custom-call | tf_op jit(solution)/shard_map/taps/pallas_call | solution.py:188
  33.2 0.0 copy-start.4
  33.2 0.0 collective-permute-done.2.north
  33.2 0.0 collective-permute-done.3.south
  33.2 0.0 copy-done.2
  33.3 0.0 copy-done.1
  33.3 3.3 %filtering.1 = (bf16[16,4,32,512]{3,2,1,0:T(8,128)(2,1)S(1)}, bf16[4,16,32,512]{3,2,1,0:T(8,128)(2,1)}) custom-call(s32[1]{0:T(128)} %bitcast.first, s32[4,256]{1,0:T(4,128)S(1)} %bitcast.11, bf16[16,128,256]{2,1,0:T(8,128)(2,1)S(1)} %get-tuple-element.7.taps, bf16[16,32,512]{2,1,0:T(8,128)(2,1)S(1)} %copy-done.2, ...), custom_call_target="tpu_custom_call" | custom-call | tf_op jit(solution)/shard_map/filtering/pallas_call | solution.py:202
  36.6 2.5 convert_element_type.23
  39.1 0.0 copy-done.4
  39.1 0.0 reduce-scatter.2.cloned.1.call-update
  39.1 0.0 copy-start
  39.1 0.0 all-reduce.2.cloned.1.call-start
  39.2 0.4 collective-permute-start.5
  39.6 1.7 collective-permute-start.4
  41.3 4.3 %collective-permute-done.5.east = bf16[16,16,512]{2,1,0:T(8,128)(2,1)S(1)} collective-permute-done((bf16[16,16,512]{2,1,0:T(8,128)(2,1)S(1)}, bf16[16,16,512]{2,1,0:T(8,128)(2,1)S(1)}, u32[]{:S(2)}, u32[]{:S(2)}) %collective-permute-start.5) | collective-permute-done | bytes 262176 | tf_op jit(solution)/shard_map/ppermute | solution.py:166
  45.7 2.4 collective-permute-done.4.west
  48.1 79.9 %reduce-scatter.2.cloned.1.call-done = f32[1,4,32,512]{3,2,1,0:T(8,128)} async-done(((f32[16,4,32,512]{3,2,1,0:T(8,128)}), f32[1,4,32,512]{3,2,1,0:T(8,128)}) %reduce-scatter.2.cloned.1.call-update) | async-done | bytes 262160 | tf_op jit(solution)/shard_map/reduce_scatter | solution.py:243
  128.0 0.0 all-reduce.2.cloned.1.call-update
  128.1 1.3 collective-permute-start.6
  129.4 1.3 collective-permute-start.7
  130.7 0.0 copy-done
  130.7 0.0 copy-start.3
  130.7 1.6 copy-done.3
  132.3 0.0 copy-start.5
  132.3 2.0 mixed.1
  134.3 0.0 collective-permute-done.6.north
  134.3 0.3 collective-permute-done.7.south
  134.7 0.0 copy-done.5
  134.7 3.9 %adjoint.1 = bf16[16,32,512]{2,1,0:T(8,128)(2,1)} custom-call(bf16[16,128,320]{2,1,0:T(8,128)(2,1)S(1)} %copy-done.5, bf16[16,32,512]{2,1,0:T(8,128)(2,1)S(1)} %copy-done.1, bf16[16,16,512]{2,1,0:T(8,128)(2,1)S(1)} %collective-permute-done.4.west, bf16[16,16,512]{2,1,0:T(8,128)(2,1)S(1)} %collective-permute-done.5.east, ...), custom_call_target="tpu_custom_call" | custom-call | tf_op jit(solution)/shard_map/adjoint/pallas_call | solution.py:224
  138.6 125.5 %all-reduce.2.cloned.1.call-done = f32[4,32,512]{2,1,0:T(8,128)} async-done(((f32[4,32,512]{2,1,0:T(8,128)}), f32[4,32,512]{2,1,0:T(8,128)}) %all-reduce.2.cloned.1.call-update) | async-done | bytes 262160 | tf_op jit(solution)/shard_map/psum | solution.py:244
  264.1 1.7 broadcast_multiply_fusion
  (15 shorter events, 0.2 us)
Async XLA Ops:
  7.2 26.1 %copy-start.2 = (bf16[16,32,512]{2,1,0:T(8,128)(2,1)S(1)}, bf16[16,32,512]{2,1,0:T(8,128)(2,1)}, u32[]{:S(2)}) copy-start(bf16[16,32,512]{2,1,0:T(8,128)(2,1)} %center.2) | copy-start | bytes 1572868
  7.2 20.3 %copy-start.6 = (s32[256,4]{0,1:T(4,128)S(1)}, s32[256,4]{0,1:T(4,128)}, u32[]{:S(2)}) copy-start(s32[256,4]{0,1:T(4,128)} %param.8) | copy-start | bytes 12292
  7.2 20.3 %copy-start.7 = (bf16[4,256,4,4]{1,3,2,0:T(4,128)(2,1)S(1)}, bf16[4,256,4,4]{1,3,2,0:T(4,128)(2,1)}, u32[]{:S(2)}) copy-start(bf16[4,256,4,4]{1,3,2,0:T(4,128)(2,1)} %param.7) | copy-start | bytes 98308
  7.2 26.1 %copy-start.1 = (bf16[16,32,512]{2,1,0:T(8,128)(2,1)S(1)}, bf16[16,32,512]{2,1,0:T(8,128)(2,1)}, u32[]{:S(2)}) copy-start(bf16[16,32,512]{2,1,0:T(8,128)(2,1)} %center.3) | copy-start | bytes 1572868
  7.2 120.8 %reduce-scatter.2.cloned.1.call-start = ((), (), s32[]{:S(2)}) async-start(), calls=%async_computation.1 | async-start | bytes 4456448 | tf_op jit(solution)/shard_map/reduce_scatter | solution.py:243
  8.4 11.5 %collective-permute-start.1 = (bf16[16,16,512]{2,1,0:T(8,128)(2,1)S(1)}, bf16[16,16,512]{2,1,0:T(8,128)(2,1)S(1)}, u32[]{:S(2)}, u32[]{:S(2)}) collective-permute-start(bf16[16,16,512]{2,1,0:T(8,128)(2,1)S(1)} %get-tuple-element.17), channel_id=1, source_target_pairs={{0,15},{1,0},{2,1},{3,2},{4,3},{5,4},{6,5},{7,6},{8,7},{9,8},{10,9... | collective-permute-start | bytes 786440 | tf_op jit(solution)/shard_map/ppermute | solution.py:166
  14.3 9.9 %collective-permute-start = (bf16[16,16,512]{2,1,0:T(8,128)(2,1)S(1)}, bf16[16,16,512]{2,1,0:T(8,128)(2,1)S(1)}, u32[]{:S(2)}, u32[]{:S(2)}) collective-permute-start(bf16[16,16,512]{2,1,0:T(8,128)(2,1)S(1)} %get-tuple-element.18), channel_id=1, source_target_pairs={{0,1},{1,2},{2,3},{3,4},{4,5},{5,6},{6,7},{7,8},{8,9},{9,10},{10,1... | collective-permute-start | bytes 786440 | tf_op jit(solution)/shard_map/ppermute | solution.py:165
  24.2 9.0 %collective-permute-start.2 = (bf16[2,64,512]{2,1,0:T(8,128)(2,1)S(1)}, bf16[2,64,512]{2,1,0:T(8,128)(2,1)S(1)}, u32[]{:S(2)}, u32[]{:S(2)}) collective-permute-start(bf16[2,64,512]{2,1,0:T(8,128)(2,1)S(1)} %pad_maximum_fusion), channel_id=1, source_target_pairs={{0,16},{16,32},{32,48},{48,64},{64,80},{80,96},{96,112},{112,128},... | collective-permute-start | bytes 393224 | tf_op jit(solution)/shard_map/ppermute | solution.py:169
  26.2 7.1 %collective-permute-start.3 = (bf16[2,64,512]{2,1,0:T(8,128)(2,1)}, bf16[2,64,512]{2,1,0:T(8,128)(2,1)S(1)}, u32[]{:S(2)}, u32[]{:S(2)}) collective-permute-start(bf16[2,64,512]{2,1,0:T(8,128)(2,1)} %pad_maximum_fusion.1), channel_id=1, source_target_pairs={{16,0},{32,16},{48,32},{64,48},{80,64},{96,80},{112,96},{128,112},... | collective-permute-start | bytes 393224 | tf_op jit(solution)/shard_map/ppermute | solution.py:170
  33.2 5.9 %copy-start.4 = (bf16[16,128,320]{2,1,0:T(8,128)(2,1)}, bf16[16,128,320]{2,1,0:T(8,128)(2,1)S(1)}, u32[]{:S(2)}) copy-start(bf16[16,128,320]{2,1,0:T(8,128)(2,1)S(1)} %get-tuple-element.9.taps) | copy-start | bytes 3932164
  39.1 91.6 %copy-start = (bf16[4,512,512]{2,1,0:T(8,128)(2,1)S(1)}, bf16[4,512,512]{2,1,0:T(8,128)(2,1)}, u32[]{:S(2)}) copy-start(bf16[4,512,512]{2,1,0:T(8,128)(2,1)} %mixing.3) | copy-start | bytes 6291460
  39.1 224.9 %all-reduce.2.cloned.1.call-start = ((), (), s32[]{:S(2)}) async-start(), calls=%async_computation.2 | async-start | bytes 524288 | tf_op jit(solution)/shard_map/psum | solution.py:244
  39.2 6.5 %collective-permute-start.5 = (bf16[16,16,512]{2,1,0:T(8,128)(2,1)S(1)}, bf16[16,16,512]{2,1,0:T(8,128)(2,1)S(1)}, u32[]{:S(2)}, u32[]{:S(2)}) collective-permute-start(bf16[16,16,512]{2,1,0:T(8,128)(2,1)S(1)} %get-tuple-element.13), channel_id=1, source_target_pairs={{0,15},{1,0},{2,1},{3,2},{4,3},{5,4},{6,5},{7,6},{8,7},{9,8},{10,9... | collective-permute-start | bytes 786440 | tf_op jit(solution)/shard_map/ppermute | solution.py:166
  39.6 8.5 %collective-permute-start.4 = (bf16[16,16,512]{2,1,0:T(8,128)(2,1)S(1)}, bf16[16,16,512]{2,1,0:T(8,128)(2,1)S(1)}, u32[]{:S(2)}, u32[]{:S(2)}) collective-permute-start(bf16[16,16,512]{2,1,0:T(8,128)(2,1)S(1)} %get-tuple-element.14), channel_id=1, source_target_pairs={{0,1},{1,2},{2,3},{3,4},{4,5},{5,6},{6,7},{7,8},{8,9},{9,10},{10,1... | collective-permute-start | bytes 786440 | tf_op jit(solution)/shard_map/ppermute | solution.py:165
  128.1 6.3 %collective-permute-start.6 = (bf16[2,64,512]{2,1,0:T(8,128)(2,1)S(1)}, bf16[2,64,512]{2,1,0:T(8,128)(2,1)S(1)}, u32[]{:S(2)}, u32[]{:S(2)}) collective-permute-start(bf16[2,64,512]{2,1,0:T(8,128)(2,1)S(1)} %pad_maximum_fusion.2), channel_id=1, source_target_pairs={{0,16},{16,32},{32,48},{48,64},{64,80},{80,96},{96,112},{112,128},... | collective-permute-start | bytes 393224 | tf_op jit(solution)/shard_map/ppermute | solution.py:169
  129.4 5.3 %collective-permute-start.7 = (bf16[2,64,512]{2,1,0:T(8,128)(2,1)S(1)}, bf16[2,64,512]{2,1,0:T(8,128)(2,1)S(1)}, u32[]{:S(2)}, u32[]{:S(2)}) collective-permute-start(bf16[2,64,512]{2,1,0:T(8,128)(2,1)S(1)} %pad_maximum_fusion.3), channel_id=1, source_target_pairs={{16,0},{32,16},{48,32},{64,48},{80,64},{96,80},{112,96},{128,112},... | collective-permute-start | bytes 393224 | tf_op jit(solution)/shard_map/ppermute | solution.py:170
  130.7 1.6 copy-start.3
  132.3 2.4 copy-start.5
Sparse Core Ops, SparseCore 0:
  39.2 88.7 reduce-scatter.1
  130.8 133.1 all-reduce.1

commit v2 on v1

--- a/solution.py
+++ b/solution.py
@@ -1,3 +1,4 @@
+import functools
 import math
 
 import jax
@@ -84,23 +85,29 @@
     lax.fori_loop(0, rows, one_row, 0, unroll=2)
 
 
-def assemble(extended, center, west, east, north, south):
+def assemble(extended, center, west, east, north, south, rims_w, rims_e):
     rows, cols, _ = center.shape
     extended[HL : HL + rows, 0:WL] = west[...]
     extended[HL : HL + rows, WL : WL + cols] = center[...]
     extended[HL : HL + rows, WL + cols :] = east[...]
-    extended[0:HL] = north[...]
-    extended[HL + rows :] = south[...]
-
-
-def filter_kernel(first, lat, taps, center, west, east, north, south, cot, weight_out, filt_out, extended):
+    extended[0:HL, WL : WL + cols] = north[...]
+    extended[HL + rows :, WL : WL + cols] = south[...]
+    extended[0:HL, 0:WL] = rims_w[0:HL]
+    extended[HL + rows :, 0:WL] = rims_w[HL:]
+    extended[0:HL, WL + cols :] = rims_e[0:HL]
+    extended[HL + rows :, WL + cols :] = rims_e[HL:]
+
+
+def filter_kernel(
+    place, lat, taps, center, west, east, north, south, rims_w, rims_e, cot, keep, send, filt_out, extended
+):
     rows, cols, channels = center.shape
     basis_count = filt_out.shape[0]
     blocks = lat.shape[0]
-    assemble(extended, center, west, east, north, south)
+    assemble(extended, center, west, east, north, south, rims_w, rims_e)
 
     def one_row(row, carry):
-        slabs = [extended[row + HL + lat[block, first[0] + row]] for block in range(blocks)]
+        slabs = [extended[row + HL + lat[block, place[0] + row]] for block in range(blocks)]
         slab = jnp.concatenate(slabs, axis=0)
         filtered = jnp.dot(taps[row], slab, preferred_element_type=F32).astype(BF16)
         filt_out[:, row] = filtered.reshape(basis_count, cols, channels)
@@ -108,15 +115,17 @@
 
     lax.fori_loop(0, rows, one_row, 0, unroll=4)
     cot_flat = cot[...].reshape(rows * cols, channels)
-    shares = weight_out.shape[0]
+    pairs = keep.shape[0]
+    share = channels // (2 * pairs)
+    core = place[3]
     for basis in range(basis_count):
         filtered = filt_out[basis].reshape(rows * cols, channels)
         terms = lax.dot_general(
             filtered, cot_flat, (((0,), (0,)), ((), ())), preferred_element_type=F32
-        )
-        weight_out[:, basis] = terms.reshape(shares, channels // shares, channels).astype(
-            weight_out.dtype
-        )
+        ).reshape(pairs, 2, share, channels)
+        lines = slice(basis * share, (basis + 1) * share)
+        keep[:, lines] = jnp.where(core == 0, terms[:, 0], terms[:, 1])
+        send[:, lines] = jnp.where(core == 0, terms[:, 1], terms[:, 0]).astype(BF16)
 
 
 def output_kernel(filt, mixing, out):
@@ -130,10 +139,12 @@
     out[...] = total.reshape(rows, cols, channels).astype(BF16)
 
 
-def adjoint_kernel(taps, center, west, east, north, south, mixing, out, extended, spread):
+def adjoint_kernel(
+    taps, center, west, east, north, south, rims_w, rims_e, mixing, out, extended, spread
+):
     rows, cols, channels = center.shape
     basis_count = mixing.shape[0]
-    assemble(extended, center, west, east, north, south)
+    assemble(extended, center, west, east, north, south, rims_w, rims_e)
 
     def one_row(row, carry):
         slab = extended[pl.ds(row, SPAN)].reshape(SPAN * (cols + 2 * WL), channels)
@@ -154,29 +165,207 @@
     out[...] = total.reshape(rows, cols, channels).astype(BF16)
 
 
-def ring(step, count):
-    return [(i, (i + step) % count) for i in range(count)]
+def first_sum_kernel(place, keep, recv, *outs):
+    fours = outs[:4]
+    eights = outs[4:]
+    half = keep.shape[2] // 2
+    y, x = place[1], place[2]
+    depth = eights[0].shape[1]
+    for step in range(4):
+        row = 2 * lax.rem(y + step, 4)
+        total = keep[pl.ds(row, 2), :, :half] + recv[pl.ds(row, 2), :, :half].astype(F32)
+        fours[step][...] = total.astype(fours[step].dtype)
+        target = lax.rem(x + step, 4)
+        lines = pl.ds(pl.multiple_of(lax.rem(target, 2) * depth, depth), depth)
+        for other in range(4):
+            pair = 2 * other + target // 2
+            total = keep[pair, lines, half:] + recv[pair, lines, half:].astype(F32)
+            eights[step][other] = total.astype(eights[step].dtype)
+
+
+def added(refs):
+    total = refs[0][...]
+    for ref in refs[1:]:
+        total = total + ref[...].astype(F32)
+    return total
+
+
+def second_sum_kernel(place, *refs):
+    by_y, by_x = refs[:4], refs[4:8]
+    over_x, over_y = refs[8:12], refs[12:16]
+    one, two = refs[16:]
+    one[...] = added(by_y)
+    two[...] = added(by_x)
+    y, x = place[1], place[2]
+    depth = over_x[0].shape[0]
+    for step in range(4):
+        target = lax.rem(x + step, 4)
+        lines = pl.ds(pl.multiple_of(lax.rem(target, 2) * depth, depth), depth)
+        over_x[step][...] = one[target // 2, lines, :].astype(over_x[step].dtype)
+        over_y[step][...] = two[lax.rem(y + step, 4)].astype(over_y[step].dtype)
+
+
+def third_sum_kernel(place, *refs):
+    over_x, over_y = refs[:4], refs[4:8]
+    keep, send, whole = refs[8:]
+    half = over_x[0].shape[1]
+    whole[:, :half] = added(over_x)
+    whole[:, half:] = added(over_y)
+    depth = keep.shape[0]
+    odd = lax.rem(place[4], 2)
+    keep[...] = whole[pl.ds(pl.multiple_of(odd * depth, depth), depth), :]
+    send[...] = whole[pl.ds(pl.multiple_of((1 - odd) * depth, depth), depth), :]
+
+
+def fourth_sum_kernel(keep, recv, out):
+    out[...] = (keep[...] + recv[...]).astype(BF16)
+
+
+def fifth_sum_kernel(normalizer, one, two, three, four, out):
+    near = one[...].astype(F32) + two[...].astype(F32)
+    far = three[...].astype(F32) + four[...].astype(F32)
+    out[...] = (near + far) * normalizer
+
+
+def placing_kernel(place, own, by_z, by_x, by_both, out):
+    odd = lax.rem(place[4], 2)
+    low = lax.rem(place[2], 2)
+    out[2 * low + odd] = own[...]
+    out[2 * low + 1 - odd] = by_z[...]
+    out[2 * (1 - low) + odd] = by_x[...]
+    out[2 * (1 - low) + 1 - odd] = by_both[...]
+
+
+LAT = ("y", "xh", "core")
+LON = ("xl", "z")
+CROSS = ("xh", "xl")
+
+
+def shift(cells, axis, count, step):
+    return lax.ppermute(cells, axis, [(i, (i + step) % count) for i in range(count)])
+
+
+def swap(cells, axis, count, mask):
+    return lax.ppermute(cells, axis, [(i, i ^ mask) for i in range(count)])
 
 
 def halo(cells):
     rows, cols, _ = cells.shape
-    lons = lax.axis_size("lon")
-    lats = lax.axis_size("lat")
-    west = lax.ppermute(cells[:, cols - WL :], "lon", ring(1, lons))
-    east = lax.ppermute(cells[:, :WL], "lon", ring(-1, lons))
-    tail = jnp.concatenate([a[rows - HL :] for a in (west, cells, east)], axis=1)
-    head = jnp.concatenate([a[:HL] for a in (west, cells, east)], axis=1)
-    north = lax.ppermute(tail, "lat", [(i, i + 1) for i in range(lats - 1)])
-    south = lax.ppermute(head, "lat", [(i + 1, i) for i in range(lats - 1)])
-    return west, east, north, south
+    lons = lax.axis_size(LON)
+    lats = lax.axis_size(LAT)
+    west = shift(cells[:, cols - WL :], LON, lons, 1)
+    east = shift(cells[:, :WL], LON, lons, -1)
+    north = lax.ppermute(cells[rows - HL :], LAT, [(i, i + 1) for i in range(lats - 1)])
+    south = lax.ppermute(cells[:HL], LAT, [(i + 1, i) for i in range(lats - 1)])
+    both = jnp.concatenate([north, south], axis=0)
+    rims_w = shift(both[:, cols - WL :], LON, lons, 1)
+    rims_e = shift(both[:, :WL], LON, lons, -1)
+    return west, east, north, south, rims_w, rims_e
+
+
+def call(kernel, outs, args, specs, name, scratch=(), flops=0, moved=0):
+    return pl.pallas_call(
+        kernel,
+        out_shape=outs,
+        in_specs=specs,
+        out_specs=jax.tree.map(lambda _: VMEM, outs),
+        scratch_shapes=list(scratch),
+        compiler_params=PARAMS,
+        cost_estimate=pl.CostEstimate(flops=flops, bytes_accessed=moved, transcendentals=0),
+        name=name,
+    )(*args)
+
+
+def shaped(shape, dtype):
+    return jax.ShapeDtypeStruct(shape, dtype)
+
+
+def reduced(place, keep, send, normalizer):
+    pairs, lines, channels = keep.shape
+    half = channels // 2
+    deep = lines // 2
+    kinds = [F32, BF16, BF16, BF16]
+    recv = swap(send, "core", 2, 1)
+    parts = call(
+        first_sum_kernel,
+        tuple(shaped((2, lines, half), kind) for kind in kinds)
+        + tuple(shaped((4, deep, half), kind) for kind in kinds),
+        (place, keep, recv),
+        [SMEM, VMEM, VMEM],
+        "first_sum",
+        flops=keep.size * 4,
+        moved=keep.size * 8,
+    )
+    by_y = [parts[0]] + [shift(parts[s], "y", 4, s) for s in (1, 2, 3)]
+    by_x = [parts[4]] + [shift(parts[4 + s], CROSS, 4, s) for s in (1, 2, 3)]
+    parts = call(
+        second_sum_kernel,
+        tuple(shaped((deep, half), kind) for kind in kinds + kinds),
+        (place, *by_y, *by_x),
+        [SMEM] + [VMEM] * 8,
+        "second_sum",
+        [pltpu.VMEM((2, lines, half), F32), pltpu.VMEM((4, deep, half), F32)],
+        flops=keep.size,
+        moved=keep.size * 2,
+    )
+    over_x = [parts[0]] + [shift(parts[s], CROSS, 4, s) for s in (1, 2, 3)]
+    over_y = [parts[4]] + [shift(parts[4 + s], "y", 4, s) for s in (1, 2, 3)]
+    own, other = call(
+        third_sum_kernel,
+        (shaped((deep // 2, channels), F32),) * 2,
+        (place, *over_x, *over_y),
+        [SMEM] + [VMEM] * 8,
+        "third_sum",
+        [pltpu.VMEM((deep, channels), F32)],
+        flops=keep.size // 4,
+        moved=keep.size // 2,
+    )
+    recv = swap(other, "z", 8, 1)
+    mine = call(
+        fourth_sum_kernel,
+        shaped(own.shape, BF16),
+        (own, recv),
+        [VMEM] * 2,
+        "fourth_sum",
+        flops=own.size,
+        moved=own.size * 8,
+    )
+    result = call(
+        functools.partial(fifth_sum_kernel, normalizer),
+        shaped(own.shape, F32),
+        (mine, *(swap(mine, "z", 8, mask) for mask in (2, 4, 6))),
+        [VMEM] * 4,
+        "fifth_sum",
+        flops=own.size * 4,
+        moved=own.size * 12,
+    )
+    by_z = swap(result, "z", 8, 1)
+    by_x = swap(result, "xl", 2, 1)
+    by_both = swap(result, LON, 16, 9)
+    return call(
+        placing_kernel,
+        shaped((4,) + result.shape, F32),
+        (place, result, by_z, by_x, by_both),
+        [SMEM] + [VMEM] * 4,
+        "placing",
+        moved=own.size * 32,
+    )
 
 
 def local(field, filter_values, block_lat, block_lon, mixing, cotangent):
     rows, cols, channels = field.shape
     basis_count, _, blocks, taps = filter_values.shape
-    first = (lax.axis_index("lat") * rows).astype(jnp.int32).reshape(1)
     field_halo = halo(field)
     cot_halo = halo(cotangent)
+    place = jnp.stack(
+        [
+            lax.axis_index(LAT) * rows,
+            lax.axis_index("y"),
+            lax.axis_index(CROSS),
+            lax.axis_index("core"),
+            lax.axis_index("z"),
+        ]
+    ).astype(jnp.int32)
 
     psi_lines = filter_values.transpose(2, 0, 3, 1).reshape(blocks, basis_count * taps, -1)
     lat_lines = block_lat.T
@@ -185,70 +374,68 @@
         [psi_lines, lon_lines[:, None].astype(BF16), lat_lines[:, None].astype(BF16)], axis=1
     )
     wide = cols + 2 * WL
-    fwd_taps, adj_taps = pl.pallas_call(
+    fwd_taps, adj_taps = call(
         taps_kernel,
-        out_shape=(
-            jax.ShapeDtypeStruct((rows, basis_count * cols, blocks * wide), BF16),
-            jax.ShapeDtypeStruct((rows, basis_count * cols, SPAN * wide), BF16),
+        (
+            shaped((rows, basis_count * cols, blocks * wide), BF16),
+            shaped((rows, basis_count * cols, SPAN * wide), BF16),
         ),
-        in_specs=[SMEM, VMEM],
-        out_specs=(VMEM, VMEM),
-        compiler_params=PARAMS,
-        name="taps",
-    )(first, bank)
-
-    lat_count = lax.axis_size("lat")
+        (place, bank),
+        [SMEM, VMEM],
+        "taps",
+        flops=4_000_000_000,
+        moved=2_000_000,
+    )
+
+    lat_count = lax.axis_size(LAT)
     share = channels // lat_count
-    terms, filtered = pl.pallas_call(
+    lines = basis_count * share
+    keep, send, filtered = call(
         filter_kernel,
-        out_shape=(
-            jax.ShapeDtypeStruct((lat_count, basis_count, share, channels), BF16),
-            jax.ShapeDtypeStruct((basis_count, rows, cols, channels), BF16),
+        (
+            shaped((lat_count // 2, lines, channels), F32),
+            shaped((lat_count // 2, lines, channels), BF16),
+            shaped((basis_count, rows, cols, channels), BF16),
         ),
-        in_specs=[SMEM] * 2 + [VMEM] * 7,
-        out_specs=(VMEM, VMEM),
-        scratch_shapes=[pltpu.VMEM((rows + 2 * HL, wide, channels), BF16)],
-        compiler_params=PARAMS,
-        name="filtering",
-    )(first, lat_lines, fwd_taps, field, *field_halo, cotangent)
-
-    output = pl.pallas_call(
+        (place, lat_lines, fwd_taps, field, *field_halo, cotangent),
+        [SMEM] * 2 + [VMEM] * 9,
+        "filtering",
+        [pltpu.VMEM((rows + 2 * HL, wide, channels), BF16)],
+        flops=2_000_000_000,
+        moved=8_000_000,
+    )
+    output = call(
         output_kernel,
-        out_shape=jax.ShapeDtypeStruct((rows, cols, channels), BF16),
-        in_specs=[VMEM] * 2,
-        out_specs=VMEM,
-        compiler_params=PARAMS,
-        name="mixed",
-    )(filtered, mixing)
-
-    field_grad = pl.pallas_call(
+        shaped((rows, cols, channels), BF16),
+        (filtered, mixing),
+        [VMEM] * 2,
+        "mixed",
+        flops=1_500_000_000,
+        moved=4_500_000,
+    )
+    field_grad = call(
         adjoint_kernel,
-        out_shape=jax.ShapeDtypeStruct((rows, cols, channels), BF16),
-        in_specs=[VMEM] * 7,
-        out_specs=VMEM,
-        scratch_shapes=[
+        shaped((rows, cols, channels), BF16),
+        (adj_taps, cotangent, *cot_halo, mixing),
+        [VMEM] * 9,
+        "adjoint",
+        [
             pltpu.VMEM((rows + 2 * HL, wide, channels), BF16),
             pltpu.VMEM((basis_count, rows, cols, channels), BF16),
         ],
-        compiler_params=PARAMS,
-        name="adjoint",
-    )(adj_taps, cotangent, *cot_halo, mixing)
-
-    normalizer = 1.0 / math.sqrt(rows * lat_count * cols * lax.axis_size("lon"))
-    summed = reduced(terms)
-    return (output, field_grad, summed * normalizer)
-
-
-def reduced(terms):
-    summed = lax.psum_scatter(terms.astype(F32), "lat", scatter_dimension=0, tiled=True)
-    return lax.psum(summed[0], "lon")
+        flops=3_000_000_000,
+        moved=6_000_000,
+    )
+    normalizer = 1.0 / math.sqrt(rows * lat_count * cols * lax.axis_size(LON))
+    return (output, field_grad, reduced(place, keep, send, normalizer))
 
 
 def solution(mesh):
+    grid = Mesh(mesh.devices.reshape(4, 2, 2, 2, 8), ("y", "xh", "core", "xl", "z"))
     return jax.shard_map(
         local,
-        mesh=mesh,
-        in_specs=(P("lat", "lon", None), P(), P(), P(), P(), P("lat", "lon", None)),
-        out_specs=(P("lat", "lon", None), P("lat", "lon", None), P(None, "lat", None)),
+        mesh=grid,
+        in_specs=(P(LAT, LON, None), P(), P(), P(), P(), P(LAT, LON, None)),
+        out_specs=(P(LAT, LON, None), P(LAT, LON, None), P(None, LAT, None)),
         check_vma=False,
     )

time: 274 us -> 95.4 us (0.35)
  waiting for transfers between devices: 221 us -> 13.8 us
  starting transfers between devices: 13.3 us -> 57.2 us
  between operations: 14.3 us -> 0.91 us
  other arithmetic: 5.61 us -> 1.39 us
  Pallas kernels: 14.8 us -> 18.8 us
    psum x1 -> x0, waiting for transfers between devices: 125 us -> none  [reduced(): return lax.psum(summed[0], 'lon')]
    reduce_scatter x1 -> x0, waiting for transfers between devices: 79.9 us -> none  [reduced(): lax.psum_scatter(terms.astype(F32), 'lat', scatter_dimension=0, tiled=True)]
    ppermute x8 -> x32, starting transfers between devices: 13.2 us -> 57.2 us  [the longest x20 38.8 us: shift(): lax.ppermute(cells, axis, [(i, (i + step) % count) for i in range(count)])]
    pallas_call x4 -> x10, Pallas kernels: 14.8 us -> 18.8 us  [call(): pl.pallas_call(kernel, out_shape=outs, in_specs=specs, out_specs=jax.tree...]
    ppermute x8 -> x32, waiting for transfers between devices: 15.4 us -> 13.8 us  [the longest x20 7.95 us: shift(): lax.ppermute(cells, axis, [(i, (i + step) % count) for i in range(count)])]
  transfers between devices with their start and end apart: 10 -> 32, of which waited for: 7 -> 9; matrix products, arithmetic and copies ran while one was open for 1% -> 4% of each run, Pallas kernels for 4% -> 14%
where the time goes in v2:
time: 95.4 us; the launch traced here: 95.1 us
  starting transfers between devices  57.2 us (60%)
  Pallas kernels  18.8 us (20%)
  waiting for transfers between devices  13.8 us (14%)
  local copies, waits for them, and re-layouts  2.96 us (3%)
  other arithmetic  1.39 us (1%)
    ppermute x20, starting transfers between devices, shift(): lax.ppermute(cells, axis, [(i, (i + step) % count) for i in range(count)])  38.8 us
    pallas_call x10, Pallas kernels, call(): pl.pallas_call(kernel, out_shape=outs, in_specs=specs, out_specs=jax.tree...  18.8 us
    ppermute x8, starting transfers between devices, swap(): return lax.ppermute(cells, axis, [(i, i ^ mask) for i in range(count)])  11.3 us
    ppermute x20, waiting for transfers between devices, shift(): lax.ppermute(cells, axis, [(i, (i + step) % count) for i in range(count)])  7.95 us
    ppermute x8, waiting for transfers between devices, swap(): return lax.ppermute(cells, axis, [(i, i ^ mask) for i in range(count)])  5.88 us
    ppermute x2, starting transfers between devices, halo(): lax.ppermute(cells[rows - HL:], LAT, [(i, i + 1) for i in range(lats - 1)])  4.52 us
    ppermute x2, starting transfers between devices, halo(): south = lax.ppermute(cells[:HL], LAT, [(i + 1, i) for i in range(lats - 1)])  2.58 us
  transfers between devices with their start and end apart: 32, of which 9 were waited for; matrix products, arithmetic and copies ran while one was open for 4% of the time, Pallas kernels for 14%

profile of v2, /device:TPU:2, one launch (start us, length us, event | category | flops | bytes accessed | tf_op | source)
XLA Modules:
  0.0 95.1 jit_solution(13081288911547449076)
XLA Ops:
  0.6 0.9 fusion.2
  1.5 1.3 %collective-permute-start.3 = (bf16[2,32,512]{2,1,0:T(8,128)(2,1)S(1)}, bf16[2,32,512]{2,1,0:T(8,128)(2,1)S(1)}, u32[]{:S(2)}, u32[]{:S(2)}) collective-permute-start(bf16[2,32,512]{2,1,0:T(8,128)(2,1)S(1)} %get-tuple-element.53), channel_id=1, source_target_pairs={{16,0},{32,16},{48,32},{64,48},{80,64},{96,80},{112,96},{128,112},... | collective-permute-start | bytes 196616 | tf_op jit(solution)/shard_map/ppermute | solution.py:259
  2.8 3.0 %collective-permute-start.2 = (bf16[2,32,512]{2,1,0:T(8,128)(2,1)S(1)}, bf16[2,32,512]{2,1,0:T(8,128)(2,1)S(1)}, u32[]{:S(2)}, u32[]{:S(2)}) collective-permute-start(bf16[2,32,512]{2,1,0:T(8,128)(2,1)S(1)} %get-tuple-element.54), channel_id=1, source_target_pairs={{0,16},{16,32},{32,48},{48,64},{64,80},{80,96},{96,112},{112,128},... | collective-permute-start | bytes 196616 | tf_op jit(solution)/shard_map/ppermute | solution.py:258
  5.9 1.1 %fusion.3 = (bf16[16,16,512]{2,1,0:T(8,128)(2,1)S(1)}, bf16[16,16,512]{2,1,0:T(8,128)(2,1)S(1)}) fusion(bf16[16,32,512]{2,1,0:T(8,128)(2,1)} %center.2), kind=kLoop, calls=%fused_computation.10 | loop fusion | bytes 1048576 | tf_op jit(solution)/shard_map/slice | solution.py:257
  6.9 5.9 %collective-permute-start.1 = (bf16[16,16,512]{2,1,0:T(8,128)(2,1)S(1)}, bf16[16,16,512]{2,1,0:T(8,128)(2,1)S(1)}, u32[]{:S(2)}, u32[]{:S(2)}) collective-permute-start(bf16[16,16,512]{2,1,0:T(8,128)(2,1)S(1)} %get-tuple-element.55), channel_id=1, source_target_pairs={{0,15},{1,0},{2,1},{3,2},{4,3},{5,4},{6,5},{7,6},{8,7},{9,8},{10,9... | collective-permute-start | bytes 786440 | tf_op jit(solution)/shard_map/ppermute | solution.py:245
  12.8 0.7 convert_bitcast_fusion.1
  13.5 0.7 convert_bitcast_fusion
  14.2 0.8 copy.11
  15.0 0.1 stack.23.first.place
  15.1 0.0 collective-permute-done.2.north
  15.2 4.2 %collective-permute-start.5 = (bf16[4,16,512]{2,1,0:T(8,128)(2,1)S(1)}, bf16[4,16,512]{2,1,0:T(8,128)(2,1)S(1)}, u32[]{:S(2)}, u32[]{:S(2)}) collective-permute-start(bf16[4,16,512]{2,1,0:T(8,128)(2,1)S(1)} %get-tuple-element.59), channel_id=1, source_target_pairs={{0,15},{1,0},{2,1},{3,2},{4,3},{5,4},{6,5},{7,6},{8,7},{9,8},{10,9... | collective-permute-start | bytes 196616 | tf_op jit(solution)/shard_map/ppermute | solution.py:245
  19.4 6.1 %taps.1 = (bf16[16,128,256]{2,1,0:T(8,128)(2,1)S(1)}, bf16[16,128,320]{2,1,0:T(8,128)(2,1)S(1)}) custom-call(s32[5]{0:T(128)S(1)} %stack.23.first.place, bf16[4,18,256]{2,1,0:T(8,128)(2,1)S(1)} %pad_maximum_fusion.bank), custom_call_target="tpu_custom_call" | custom-call | flops 4000000000 | bytes 2000000 | tf_op jit(solution)/shard_map/taps/pallas_call | solution.py:267
  25.6 0.2 collective-permute-done.4.rims_w
  25.8 0.0 collective-permute-done.1.east
  25.8 0.0 collective-permute-done.west
  25.8 3.3 %filtering.1 = (f32[8,128,512]{2,1,0:T(8,128)S(1)}, bf16[8,128,512]{2,1,0:T(8,128)(2,1)S(1)}, bf16[4,16,32,512]{3,2,1,0:T(8,128)(2,1)}) custom-call(s32[5]{0:T(128)S(1)} %stack.23.first.place, s32[4,256]{1,0:T(4,128)S(1)} %bitcast.14, bf16[16,128,256]{2,1,0:T(8,128)(2,1)S(1)} %get-tuple-element.26.taps, bf16[16,32,512]{2,1,0:T(8,128)(2,1)S(1)} %copy-done, ...), custom_call_target="tpu_custom_call" | custom-call | flops 2000000000 | bytes 8000000 | tf_op jit(solution)/shard_map/filtering/pallas_call | solution.py:267
  29.1 1.7 %collective-permute-start.12 = (bf16[8,128,512]{2,1,0:T(8,128)(2,1)S(1)}, bf16[8,128,512]{2,1,0:T(8,128)(2,1)S(1)}, u32[]{:S(2)}, u32[]{:S(2)}) collective-permute-start(bf16[8,128,512]{2,1,0:T(8,128)(2,1)S(1)} %get-tuple-element.30), channel_id=1, source_target_pairs={{0,16},{16,0},{1,17},{17,1},{2,18},{18,2},{3,19},{19,3},{4,20},{20... | collective-permute-start | bytes 3145736 | tf_op jit(solution)/shard_map/ppermute | solution.py:249
  30.8 2.3 %collective-permute-done.12.recv = bf16[8,128,512]{2,1,0:T(8,128)(2,1)S(1)} collective-permute-done((bf16[8,128,512]{2,1,0:T(8,128)(2,1)S(1)}, bf16[8,128,512]{2,1,0:T(8,128)(2,1)S(1)}, u32[]{:S(2)}, u32[]{:S(2)}) %collective-permute-start.12) | collective-permute-done | bytes 1048608 | tf_op jit(solution)/shard_map/ppermute | solution.py:249
  33.1 0.8 first_sum.1
  33.9 0.0 copy-start.3
  33.9 2.3 %collective-permute-start.13 = (bf16[2,128,256]{2,1,0:T(8,128)(2,1)S(1)}, bf16[2,128,256]{2,1,0:T(8,128)(2,1)S(1)}, u32[]{:S(2)}, u32[]{:S(2)}) collective-permute-start(bf16[2,128,256]{2,1,0:T(8,128)(2,1)S(1)} %get-tuple-element.32), channel_id=1, source_target_pairs={{0,64},{64,128},{128,192},{192,0},{1,65},{65,129},{129,193},{193,1... | collective-permute-start | bytes 393224 | tf_op jit(solution)/shard_map/ppermute | solution.py:245
  36.1 3.2 %collective-permute-start.14 = (bf16[2,128,256]{2,1,0:T(8,128)(2,1)S(1)}, bf16[2,128,256]{2,1,0:T(8,128)(2,1)S(1)}, u32[]{:S(2)}, u32[]{:S(2)}) collective-permute-start(bf16[2,128,256]{2,1,0:T(8,128)(2,1)S(1)} %get-tuple-element.33), channel_id=1, source_target_pairs={{0,128},{64,192},{128,0},{192,64},{1,129},{65,193},{129,1},{193,65... | collective-permute-start | bytes 393224 | tf_op jit(solution)/shard_map/ppermute | solution.py:245
  39.3 1.5 %collective-permute-start.8 = (bf16[2,32,512]{2,1,0:T(8,128)(2,1)S(1)}, bf16[2,32,512]{2,1,0:T(8,128)(2,1)S(1)}, u32[]{:S(2)}, u32[]{:S(2)}) collective-permute-start(bf16[2,32,512]{2,1,0:T(8,128)(2,1)S(1)} %get-tuple-element.50), channel_id=1, source_target_pairs={{0,16},{16,32},{32,48},{48,64},{64,80},{80,96},{96,112},{112,128},... | collective-permute-start | bytes 196616 | tf_op jit(solution)/shard_map/ppermute | solution.py:258
  40.8 1.6 %collective-permute-start.15 = (bf16[2,128,256]{2,1,0:T(8,128)(2,1)S(1)}, bf16[2,128,256]{2,1,0:T(8,128)(2,1)S(1)}, u32[]{:S(2)}, u32[]{:S(2)}) collective-permute-start(bf16[2,128,256]{2,1,0:T(8,128)(2,1)S(1)} %get-tuple-element.34), channel_id=1, source_target_pairs={{0,192},{64,0},{128,64},{192,128},{1,193},{65,1},{129,65},{193,129... | collective-permute-start | bytes 393224 | tf_op jit(solution)/shard_map/ppermute | solution.py:245
  42.4 2.4 %collective-permute-start.16 = (bf16[4,64,256]{2,1,0:T(8,128)(2,1)S(1)}, bf16[4,64,256]{2,1,0:T(8,128)(2,1)S(1)}, u32[]{:S(2)}, u32[]{:S(2)}) collective-permute-start(bf16[4,64,256]{2,1,0:T(8,128)(2,1)S(1)} %get-tuple-element.36), channel_id=1, source_target_pairs={{0,8},{8,32},{32,40},{40,0},{1,9},{9,33},{33,41},{41,1},{2,10},{10... | collective-permute-start | bytes 393224 | tf_op jit(solution)/shard_map/ppermute | solution.py:245
  44.8 0.0 collective-permute-done.13.refs_1_
  44.8 0.8 collective-permute-start.17
  45.6 0.1 collective-permute-done.14.refs_2_
  45.7 2.1 %collective-permute-start.18 = (bf16[4,64,256]{2,1,0:T(8,128)(2,1)S(1)}, bf16[4,64,256]{2,1,0:T(8,128)(2,1)S(1)}, u32[]{:S(2)}, u32[]{:S(2)}) collective-permute-start(bf16[4,64,256]{2,1,0:T(8,128)(2,1)S(1)} %get-tuple-element.38), channel_id=1, source_target_pairs={{0,40},{8,0},{32,8},{40,32},{1,41},{9,1},{33,9},{41,33},{2,42},{10... | collective-permute-start | bytes 393224 | tf_op jit(solution)/shard_map/ppermute | solution.py:245
  47.8 0.0 collective-permute-done.15.refs_3_
  47.8 1.3 %collective-permute-start.9 = (bf16[2,32,512]{2,1,0:T(8,128)(2,1)S(1)}, bf16[2,32,512]{2,1,0:T(8,128)(2,1)S(1)}, u32[]{:S(2)}, u32[]{:S(2)}) collective-permute-start(bf16[2,32,512]{2,1,0:T(8,128)(2,1)S(1)} %get-tuple-element.49), channel_id=1, source_target_pairs={{16,0},{32,16},{48,32},{64,48},{80,64},{96,80},{112,96},{128,112},... | collective-permute-start | bytes 196616 | tf_op jit(solution)/shard_map/ppermute | solution.py:259
  49.1 3.6 %collective-permute-done.17.refs_6_ = bf16[4,64,256]{2,1,0:T(8,128)(2,1)S(1)} collective-permute-done((bf16[4,64,256]{2,1,0:T(8,128)(2,1)S(1)}, bf16[4,64,256]{2,1,0:T(8,128)(2,1)S(1)}, u32[]{:S(2)}, u32[]{:S(2)}) %collective-permute-start.17) | collective-permute-done | bytes 131104 | tf_op jit(solution)/shard_map/ppermute | solution.py:245
  52.7 1.9 %collective-permute-done.18.refs_7_ = bf16[4,64,256]{2,1,0:T(8,128)(2,1)S(1)} collective-permute-done((bf16[4,64,256]{2,1,0:T(8,128)(2,1)S(1)}, bf16[4,64,256]{2,1,0:T(8,128)(2,1)S(1)}, u32[]{:S(2)}, u32[]{:S(2)}) %collective-permute-start.18) | collective-permute-done | bytes 131104 | tf_op jit(solution)/shard_map/ppermute | solution.py:245
  54.6 0.7 second_sum.1
  55.3 1.0 %collective-permute-start.19 = (bf16[64,256]{1,0:T(8,128)(2,1)S(1)}, bf16[64,256]{1,0:T(8,128)(2,1)S(1)}, u32[]{:S(2)}, u32[]{:S(2)}) collective-permute-start(bf16[64,256]{1,0:T(8,128)(2,1)S(1)} %get-tuple-element.40), channel_id=1, source_target_pairs={{0,8},{8,32},{32,40},{40,0},{1,9},{9,33},{33,41},{41,1},{2,10},{10... | collective-permute-start | bytes 98312 | tf_op jit(solution)/shard_map/ppermute | solution.py:245
  56.4 0.0 collective-permute-done.8.north
  56.4 1.3 %collective-permute-start.20 = (bf16[64,256]{1,0:T(8,128)(2,1)S(1)}, bf16[64,256]{1,0:T(8,128)(2,1)S(1)}, u32[]{:S(2)}, u32[]{:S(2)}) collective-permute-start(bf16[64,256]{1,0:T(8,128)(2,1)S(1)} %get-tuple-element.41), channel_id=1, source_target_pairs={{0,32},{8,40},{32,0},{40,8},{1,33},{9,41},{33,1},{41,9},{2,34},{10... | collective-permute-start | bytes 98312 | tf_op jit(solution)/shard_map/ppermute | solution.py:245
  57.7 2.6 %collective-permute-start.21 = (bf16[64,256]{1,0:T(8,128)(2,1)S(1)}, bf16[64,256]{1,0:T(8,128)(2,1)S(1)}, u32[]{:S(2)}, u32[]{:S(2)}) collective-permute-start(bf16[64,256]{1,0:T(8,128)(2,1)S(1)} %get-tuple-element.42), channel_id=1, source_target_pairs={{0,40},{8,0},{32,8},{40,32},{1,41},{9,1},{33,9},{41,33},{2,42},{10... | collective-permute-start | bytes 98312 | tf_op jit(solution)/shard_map/ppermute | solution.py:245
  60.3 2.1 %collective-permute-start.23 = (bf16[64,256]{1,0:T(8,128)(2,1)S(1)}, bf16[64,256]{1,0:T(8,128)(2,1)S(1)}, u32[]{:S(2)}, u32[]{:S(2)}) collective-permute-start(bf16[64,256]{1,0:T(8,128)(2,1)S(1)} %get-tuple-element.45), channel_id=1, source_target_pairs={{0,128},{64,192},{128,0},{192,64},{1,129},{65,193},{129,1},{193,65... | collective-permute-start | bytes 98312 | tf_op jit(solution)/shard_map/ppermute | solution.py:245
  62.4 0.0 collective-permute-done.19.refs_1_
  62.4 2.4 %collective-permute-start.24 = (bf16[64,256]{1,0:T(8,128)(2,1)S(1)}, bf16[64,256]{1,0:T(8,128)(2,1)S(1)}, u32[]{:S(2)}, u32[]{:S(2)}) collective-permute-start(bf16[64,256]{1,0:T(8,128)(2,1)S(1)} %get-tuple-element.46), channel_id=1, source_target_pairs={{0,192},{64,0},{128,64},{192,128},{1,193},{65,1},{129,65},{193,129... | collective-permute-start | bytes 98312 | tf_op jit(solution)/shard_map/ppermute | solution.py:245
  64.8 0.0 collective-permute-done.20.refs_2_
  64.8 2.8 %collective-permute-start.7 = (bf16[16,16,512]{2,1,0:T(8,128)(2,1)S(1)}, bf16[16,16,512]{2,1,0:T(8,128)(2,1)S(1)}, u32[]{:S(2)}, u32[]{:S(2)}) collective-permute-start(bf16[16,16,512]{2,1,0:T(8,128)(2,1)S(1)} %get-tuple-element.51), channel_id=1, source_target_pairs={{0,15},{1,0},{2,1},{3,2},{4,3},{5,4},{6,5},{7,6},{8,7},{9,8},{10,9... | collective-permute-start | bytes 786440 | tf_op jit(solution)/shard_map/ppermute | solution.py:245
  67.6 0.0 collective-permute-done.21.refs_3_
  67.6 0.0 collective-permute-done.23.refs_6_
  67.7 0.6 third_sum.1
  68.2 0.1 collective-permute-start.25
  68.4 4.2 %collective-permute-start.11 = (bf16[4,16,512]{2,1,0:T(8,128)(2,1)S(1)}, bf16[4,16,512]{2,1,0:T(8,128)(2,1)S(1)}, u32[]{:S(2)}, u32[]{:S(2)}) collective-permute-start(bf16[4,16,512]{2,1,0:T(8,128)(2,1)S(1)} %get-tuple-element.57), channel_id=1, source_target_pairs={{0,15},{1,0},{2,1},{3,2},{4,3},{5,4},{6,5},{7,6},{8,7},{9,8},{10,9... | collective-permute-start | bytes 196616 | tf_op jit(solution)/shard_map/ppermute | solution.py:245
  72.6 1.4 %collective-permute-done.25.recv = f32[32,512]{1,0:T(8,128)S(1)} collective-permute-done((f32[32,512]{1,0:T(8,128)S(1)}, f32[32,512]{1,0:T(8,128)S(1)}, u32[]{:S(2)}, u32[]{:S(2)}) %collective-permute-start.25) | collective-permute-done | bytes 65568 | tf_op jit(solution)/shard_map/ppermute | solution.py:249
  73.9 2.9 %collective-permute-start.28 = (bf16[32,512]{1,0:T(8,128)(2,1)S(1)}, bf16[32,512]{1,0:T(8,128)(2,1)S(1)}, u32[]{:S(2)}, u32[]{:S(2)}) collective-permute-start(bf16[32,512]{1,0:T(8,128)(2,1)S(1)} %fourth_sum.1.one), channel_id=1, source_target_pairs={{0,6},{1,7},{2,4},{3,5},{4,2},{5,3},{6,0},{7,1},{8,14},{9,15},{10,... | collective-permute-start | bytes 98312 | tf_op jit(solution)/shard_map/ppermute | solution.py:249
  76.8 0.0 collective-permute-done.11.rims_e
  76.8 0.0 collective-permute-start.27
  76.8 2.1 %collective-permute-done.10.rims_w = bf16[4,16,512]{2,1,0:T(8,128)(2,1)S(1)} collective-permute-done((bf16[4,16,512]{2,1,0:T(8,128)(2,1)S(1)}, bf16[4,16,512]{2,1,0:T(8,128)(2,1)S(1)}, u32[]{:S(2)}, u32[]{:S(2)}) %collective-permute-start.10) | collective-permute-done | bytes 65568 | tf_op jit(solution)/shard_map/ppermute | solution.py:245
  78.9 2.3 %collective-permute-start.26 = (bf16[32,512]{1,0:T(8,128)(2,1)S(1)}, bf16[32,512]{1,0:T(8,128)(2,1)S(1)}, u32[]{:S(2)}, u32[]{:S(2)}) collective-permute-start(bf16[32,512]{1,0:T(8,128)(2,1)S(1)} %fourth_sum.1.one), channel_id=1, source_target_pairs={{0,2},{1,3},{2,0},{3,1},{4,6},{5,7},{6,4},{7,5},{8,10},{9,11},{10,... | collective-permute-start | bytes 98312 | tf_op jit(solution)/shard_map/ppermute | solution.py:249
  81.2 3.9 %adjoint.1 = bf16[16,32,512]{2,1,0:T(8,128)(2,1)} custom-call(bf16[16,128,320]{2,1,0:T(8,128)(2,1)S(1)} %get-tuple-element.28.taps, bf16[16,32,512]{2,1,0:T(8,128)(2,1)S(1)} %copy-done.1, bf16[16,16,512]{2,1,0:T(8,128)(2,1)S(1)} %collective-permute-done.6.west, bf16[16,16,512]{2,1,0:T(8,128)(2,1)S(1)} %collective-permute-done.7.east, ...), custom_call_target="tpu_custom_call" | custom-call | flops 3000000000 | bytes 6000000 | tf_op jit(solution)/shard_map/adjoint/pallas_call | solution.py:267
  85.1 0.0 collective-permute-done.28.four
  85.1 0.0 collective-permute-done.27.three
  85.1 0.0 collective-permute-done.26.two
  85.2 3.5 %collective-permute-start.31 = (f32[32,512]{1,0:T(8,128)S(1)}, f32[32,512]{1,0:T(8,128)S(1)}, u32[]{:S(2)}, u32[]{:S(2)}) collective-permute-start(f32[32,512]{1,0:T(8,128)S(1)} %fifth_sum.1.own), channel_id=1, source_target_pairs={{0,9},{1,8},{2,11},{3,10},{4,13},{5,12},{6,15},{7,14},{8,1},{9,0},... | collective-permute-start | bytes 196616 | tf_op jit(solution)/shard_map/ppermute | solution.py:249
  88.6 0.9 collective-permute-start.30
  89.5 2.0 %mixed.1 = bf16[16,32,512]{2,1,0:T(8,128)(2,1)} custom-call(bf16[4,16,32,512]{3,2,1,0:T(8,128)(2,1)S(1)} %copy-done.4, bf16[4,512,512]{2,1,0:T(8,128)(2,1)S(1)} %copy-done.3), custom_call_target="tpu_custom_call" | custom-call | flops 1500000000 | bytes 4500000 | tf_op jit(solution)/shard_map/mixed/pallas_call | solution.py:267
  91.6 1.3 %collective-permute-done.30.by_x = f32[32,512]{1,0:T(8,128)S(1)} collective-permute-done((f32[32,512]{1,0:T(8,128)S(1)}, f32[32,512]{1,0:T(8,128)S(1)}, u32[]{:S(2)}, u32[]{:S(2)}) %collective-permute-start.30) | collective-permute-done | bytes 65568 | tf_op jit(solution)/shard_map/ppermute | solution.py:249
  92.9 0.9 collective-permute-done.29.by_z
  93.8 1.3 %placing.1 = f32[4,32,512]{2,1,0:T(8,128)} custom-call(s32[5]{0:T(128)S(1)} %stack.23.first.place, f32[32,512]{1,0:T(8,128)S(1)} %fifth_sum.1.own, f32[32,512]{1,0:T(8,128)S(1)} %collective-permute-done.29.by_z, f32[32,512]{1,0:T(8,128)S(1)} %collective-permute-done.30.by_x, f32[32,512]{1,0:T(8,128)S(1)} %collective-permute-done.31.by_both), custom_call_target="tpu_custom_call" | custom-call | bytes 524288 | tf_op jit(solution)/shard_map/placing/pallas_call | solution.py:267
  (38 shorter events, 0.2 us)
Async XLA Ops:
  1.5 13.7 %collective-permute-start.3 = (bf16[2,32,512]{2,1,0:T(8,128)(2,1)S(1)}, bf16[2,32,512]{2,1,0:T(8,128)(2,1)S(1)}, u32[]{:S(2)}, u32[]{:S(2)}) collective-permute-start(bf16[2,32,512]{2,1,0:T(8,128)(2,1)S(1)} %get-tuple-element.53), channel_id=1, source_target_pairs={{16,0},{32,16},{48,32},{64,48},{80,64},{96,80},{112,96},{128,112},... | collective-permute-start | bytes 196616 | tf_op jit(solution)/shard_map/ppermute | solution.py:259
  2.8 12.3 %collective-permute-start.2 = (bf16[2,32,512]{2,1,0:T(8,128)(2,1)S(1)}, bf16[2,32,512]{2,1,0:T(8,128)(2,1)S(1)}, u32[]{:S(2)}, u32[]{:S(2)}) collective-permute-start(bf16[2,32,512]{2,1,0:T(8,128)(2,1)S(1)} %get-tuple-element.54), channel_id=1, source_target_pairs={{0,16},{16,32},{32,48},{48,64},{64,80},{80,96},{96,112},{112,128},... | collective-permute-start | bytes 196616 | tf_op jit(solution)/shard_map/ppermute | solution.py:258
  6.9 18.9 %collective-permute-start.1 = (bf16[16,16,512]{2,1,0:T(8,128)(2,1)S(1)}, bf16[16,16,512]{2,1,0:T(8,128)(2,1)S(1)}, u32[]{:S(2)}, u32[]{:S(2)}) collective-permute-start(bf16[16,16,512]{2,1,0:T(8,128)(2,1)S(1)} %get-tuple-element.55), channel_id=1, source_target_pairs={{0,15},{1,0},{2,1},{3,2},{4,3},{5,4},{6,5},{7,6},{8,7},{9,8},{10,9... | collective-permute-start | bytes 786440 | tf_op jit(solution)/shard_map/ppermute | solution.py:245
  12.8 13.0 %collective-permute-start = (bf16[16,16,512]{2,1,0:T(8,128)(2,1)S(1)}, bf16[16,16,512]{2,1,0:T(8,128)(2,1)S(1)}, u32[]{:S(2)}, u32[]{:S(2)}) collective-permute-start(bf16[16,16,512]{2,1,0:T(8,128)(2,1)S(1)} %get-tuple-element.56), channel_id=1, source_target_pairs={{0,1},{1,2},{2,3},{3,4},{4,5},{5,6},{6,7},{7,8},{8,9},{9,10},{10,1... | collective-permute-start | bytes 786440 | tf_op jit(solution)/shard_map/ppermute | solution.py:245
  15.2 10.4 %collective-permute-start.5 = (bf16[4,16,512]{2,1,0:T(8,128)(2,1)S(1)}, bf16[4,16,512]{2,1,0:T(8,128)(2,1)S(1)}, u32[]{:S(2)}, u32[]{:S(2)}) collective-permute-start(bf16[4,16,512]{2,1,0:T(8,128)(2,1)S(1)} %get-tuple-element.59), channel_id=1, source_target_pairs={{0,15},{1,0},{2,1},{3,2},{4,3},{5,4},{6,5},{7,6},{8,7},{9,8},{10,9... | collective-permute-start | bytes 196616 | tf_op jit(solution)/shard_map/ppermute | solution.py:245
  19.4 6.4 %copy-start = (bf16[16,32,512]{2,1,0:T(8,128)(2,1)S(1)}, bf16[16,32,512]{2,1,0:T(8,128)(2,1)}, u32[]{:S(2)}) copy-start(bf16[16,32,512]{2,1,0:T(8,128)(2,1)} %center.2) | copy-start | bytes 1572868
  19.4 6.4 %copy-start.1 = (bf16[16,32,512]{2,1,0:T(8,128)(2,1)S(1)}, bf16[16,32,512]{2,1,0:T(8,128)(2,1)}, u32[]{:S(2)}) copy-start(bf16[16,32,512]{2,1,0:T(8,128)(2,1)} %center.3) | copy-start | bytes 1572868
  19.4 6.4 %copy-start.2 = (s32[256,4]{0,1:T(4,128)S(1)}, s32[256,4]{0,1:T(4,128)}, u32[]{:S(2)}) copy-start(s32[256,4]{0,1:T(4,128)} %param.8) | copy-start | bytes 12292
  19.4 6.4 %collective-permute-start.4 = (bf16[4,16,512]{2,1,0:T(8,128)(2,1)S(1)}, bf16[4,16,512]{2,1,0:T(8,128)(2,1)S(1)}, u32[]{:S(2)}, u32[]{:S(2)}) collective-permute-start(bf16[4,16,512]{2,1,0:T(8,128)(2,1)S(1)} %get-tuple-element.60), channel_id=1, source_target_pairs={{0,1},{1,2},{2,3},{3,4},{4,5},{5,6},{6,7},{7,8},{8,9},{9,10},{10,1... | collective-permute-start | bytes 196616 | tf_op jit(solution)/shard_map/ppermute | solution.py:245
  29.1 4.0 %collective-permute-start.12 = (bf16[8,128,512]{2,1,0:T(8,128)(2,1)S(1)}, bf16[8,128,512]{2,1,0:T(8,128)(2,1)S(1)}, u32[]{:S(2)}, u32[]{:S(2)}) collective-permute-start(bf16[8,128,512]{2,1,0:T(8,128)(2,1)S(1)} %get-tuple-element.30), channel_id=1, source_target_pairs={{0,16},{16,0},{1,17},{17,1},{2,18},{18,2},{3,19},{19,3},{4,20},{20... | collective-permute-start | bytes 3145736 | tf_op jit(solution)/shard_map/ppermute | solution.py:249
  33.9 47.3 %copy-start.3 = (bf16[4,512,512]{2,1,0:T(8,128)(2,1)S(1)}, bf16[4,512,512]{2,1,0:T(8,128)(2,1)}, u32[]{:S(2)}) copy-start(bf16[4,512,512]{2,1,0:T(8,128)(2,1)} %mixing.3) | copy-start | bytes 6291460
  33.9 10.9 %collective-permute-start.13 = (bf16[2,128,256]{2,1,0:T(8,128)(2,1)S(1)}, bf16[2,128,256]{2,1,0:T(8,128)(2,1)S(1)}, u32[]{:S(2)}, u32[]{:S(2)}) collective-permute-start(bf16[2,128,256]{2,1,0:T(8,128)(2,1)S(1)} %get-tuple-element.32), channel_id=1, source_target_pairs={{0,64},{64,128},{128,192},{192,0},{1,65},{65,129},{129,193},{193,1... | collective-permute-start | bytes 393224 | tf_op jit(solution)/shard_map/ppermute | solution.py:245
  36.1 9.5 %collective-permute-start.14 = (bf16[2,128,256]{2,1,0:T(8,128)(2,1)S(1)}, bf16[2,128,256]{2,1,0:T(8,128)(2,1)S(1)}, u32[]{:S(2)}, u32[]{:S(2)}) collective-permute-start(bf16[2,128,256]{2,1,0:T(8,128)(2,1)S(1)} %get-tuple-element.33), channel_id=1, source_target_pairs={{0,128},{64,192},{128,0},{192,64},{1,129},{65,193},{129,1},{193,65... | collective-permute-start | bytes 393224 | tf_op jit(solution)/shard_map/ppermute | solution.py:245
  39.3 17.0 %collective-permute-start.8 = (bf16[2,32,512]{2,1,0:T(8,128)(2,1)S(1)}, bf16[2,32,512]{2,1,0:T(8,128)(2,1)S(1)}, u32[]{:S(2)}, u32[]{:S(2)}) collective-permute-start(bf16[2,32,512]{2,1,0:T(8,128)(2,1)S(1)} %get-tuple-element.50), channel_id=1, source_target_pairs={{0,16},{16,32},{32,48},{48,64},{64,80},{80,96},{96,112},{112,128},... | collective-permute-start | bytes 196616 | tf_op jit(solution)/shard_map/ppermute | solution.py:258
  40.8 6.9 %collective-permute-start.15 = (bf16[2,128,256]{2,1,0:T(8,128)(2,1)S(1)}, bf16[2,128,256]{2,1,0:T(8,128)(2,1)S(1)}, u32[]{:S(2)}, u32[]{:S(2)}) collective-permute-start(bf16[2,128,256]{2,1,0:T(8,128)(2,1)S(1)} %get-tuple-element.34), channel_id=1, source_target_pairs={{0,192},{64,0},{128,64},{192,128},{1,193},{65,1},{129,65},{193,129... | collective-permute-start | bytes 393224 | tf_op jit(solution)/shard_map/ppermute | solution.py:245
  42.4 6.7 %collective-permute-start.16 = (bf16[4,64,256]{2,1,0:T(8,128)(2,1)S(1)}, bf16[4,64,256]{2,1,0:T(8,128)(2,1)S(1)}, u32[]{:S(2)}, u32[]{:S(2)}) collective-permute-start(bf16[4,64,256]{2,1,0:T(8,128)(2,1)S(1)} %get-tuple-element.36), channel_id=1, source_target_pairs={{0,8},{8,32},{32,40},{40,0},{1,9},{9,33},{33,41},{41,1},{2,10},{10... | collective-permute-start | bytes 393224 | tf_op jit(solution)/shard_map/ppermute | solution.py:245
  44.8 7.9 %collective-permute-start.17 = (bf16[4,64,256]{2,1,0:T(8,128)(2,1)S(1)}, bf16[4,64,256]{2,1,0:T(8,128)(2,1)S(1)}, u32[]{:S(2)}, u32[]{:S(2)}) collective-permute-start(bf16[4,64,256]{2,1,0:T(8,128)(2,1)S(1)} %get-tuple-element.37), channel_id=1, source_target_pairs={{0,32},{8,40},{32,0},{40,8},{1,33},{9,41},{33,1},{41,9},{2,34},{10... | collective-permute-start | bytes 393224 | tf_op jit(solution)/shard_map/ppermute | solution.py:245
  45.7 9.0 %collective-permute-start.18 = (bf16[4,64,256]{2,1,0:T(8,128)(2,1)S(1)}, bf16[4,64,256]{2,1,0:T(8,128)(2,1)S(1)}, u32[]{:S(2)}, u32[]{:S(2)}) collective-permute-start(bf16[4,64,256]{2,1,0:T(8,128)(2,1)S(1)} %get-tuple-element.38), channel_id=1, source_target_pairs={{0,40},{8,0},{32,8},{40,32},{1,41},{9,1},{33,9},{41,33},{2,42},{10... | collective-permute-start | bytes 393224 | tf_op jit(solution)/shard_map/ppermute | solution.py:245
  47.8 12.5 %collective-permute-start.9 = (bf16[2,32,512]{2,1,0:T(8,128)(2,1)S(1)}, bf16[2,32,512]{2,1,0:T(8,128)(2,1)S(1)}, u32[]{:S(2)}, u32[]{:S(2)}) collective-permute-start(bf16[2,32,512]{2,1,0:T(8,128)(2,1)S(1)} %get-tuple-element.49), channel_id=1, source_target_pairs={{16,0},{32,16},{48,32},{64,48},{80,64},{96,80},{112,96},{128,112},... | collective-permute-start | bytes 196616 | tf_op jit(solution)/shard_map/ppermute | solution.py:259
  55.3 7.1 %collective-permute-start.19 = (bf16[64,256]{1,0:T(8,128)(2,1)S(1)}, bf16[64,256]{1,0:T(8,128)(2,1)S(1)}, u32[]{:S(2)}, u32[]{:S(2)}) collective-permute-start(bf16[64,256]{1,0:T(8,128)(2,1)S(1)} %get-tuple-element.40), channel_id=1, source_target_pairs={{0,8},{8,32},{32,40},{40,0},{1,9},{9,33},{33,41},{41,1},{2,10},{10... | collective-permute-start | bytes 98312 | tf_op jit(solution)/shard_map/ppermute | solution.py:245
  56.4 8.4 %collective-permute-start.20 = (bf16[64,256]{1,0:T(8,128)(2,1)S(1)}, bf16[64,256]{1,0:T(8,128)(2,1)S(1)}, u32[]{:S(2)}, u32[]{:S(2)}) collective-permute-start(bf16[64,256]{1,0:T(8,128)(2,1)S(1)} %get-tuple-element.41), channel_id=1, source_target_pairs={{0,32},{8,40},{32,0},{40,8},{1,33},{9,41},{33,1},{41,9},{2,34},{10... | collective-permute-start | bytes 98312 | tf_op jit(solution)/shard_map/ppermute | solution.py:245
  57.7 9.9 %collective-permute-start.21 = (bf16[64,256]{1,0:T(8,128)(2,1)S(1)}, bf16[64,256]{1,0:T(8,128)(2,1)S(1)}, u32[]{:S(2)}, u32[]{:S(2)}) collective-permute-start(bf16[64,256]{1,0:T(8,128)(2,1)S(1)} %get-tuple-element.42), channel_id=1, source_target_pairs={{0,40},{8,0},{32,8},{40,32},{1,41},{9,1},{33,9},{41,33},{2,42},{10... | collective-permute-start | bytes 98312 | tf_op jit(solution)/shard_map/ppermute | solution.py:245
  60.3 7.3 %collective-permute-start.22 = (bf16[64,256]{1,0:T(8,128)(2,1)S(1)}, bf16[64,256]{1,0:T(8,128)(2,1)S(1)}, u32[]{:S(2)}, u32[]{:S(2)}) collective-permute-start(bf16[64,256]{1,0:T(8,128)(2,1)S(1)} %get-tuple-element.44), channel_id=1, source_target_pairs={{0,64},{64,128},{128,192},{192,0},{1,65},{65,129},{129,193},{193,1... | collective-permute-start | bytes 98312 | tf_op jit(solution)/shard_map/ppermute | solution.py:245
  60.3 7.3 %collective-permute-start.23 = (bf16[64,256]{1,0:T(8,128)(2,1)S(1)}, bf16[64,256]{1,0:T(8,128)(2,1)S(1)}, u32[]{:S(2)}, u32[]{:S(2)}) collective-permute-start(bf16[64,256]{1,0:T(8,128)(2,1)S(1)} %get-tuple-element.45), channel_id=1, source_target_pairs={{0,128},{64,192},{128,0},{192,64},{1,129},{65,193},{129,1},{193,65... | collective-permute-start | bytes 98312 | tf_op jit(solution)/shard_map/ppermute | solution.py:245
  62.4 5.3 %collective-permute-start.24 = (bf16[64,256]{1,0:T(8,128)(2,1)S(1)}, bf16[64,256]{1,0:T(8,128)(2,1)S(1)}, u32[]{:S(2)}, u32[]{:S(2)}) collective-permute-start(bf16[64,256]{1,0:T(8,128)(2,1)S(1)} %get-tuple-element.46), channel_id=1, source_target_pairs={{0,192},{64,0},{128,64},{192,128},{1,193},{65,1},{129,65},{193,129... | collective-permute-start | bytes 98312 | tf_op jit(solution)/shard_map/ppermute | solution.py:245
  64.8 16.4 %collective-permute-start.7 = (bf16[16,16,512]{2,1,0:T(8,128)(2,1)S(1)}, bf16[16,16,512]{2,1,0:T(8,128)(2,1)S(1)}, u32[]{:S(2)}, u32[]{:S(2)}) collective-permute-start(bf16[16,16,512]{2,1,0:T(8,128)(2,1)S(1)} %get-tuple-element.51), channel_id=1, source_target_pairs={{0,15},{1,0},{2,1},{3,2},{4,3},{5,4},{6,5},{7,6},{8,7},{9,8},{10,9... | collective-permute-start | bytes 786440 | tf_op jit(solution)/shard_map/ppermute | solution.py:245
  67.6 13.6 %collective-permute-start.6 = (bf16[16,16,512]{2,1,0:T(8,128)(2,1)S(1)}, bf16[16,16,512]{2,1,0:T(8,128)(2,1)S(1)}, u32[]{:S(2)}, u32[]{:S(2)}) collective-permute-start(bf16[16,16,512]{2,1,0:T(8,128)(2,1)S(1)} %get-tuple-element.52), channel_id=1, source_target_pairs={{0,1},{1,2},{2,3},{3,4},{4,5},{5,6},{6,7},{7,8},{8,9},{9,10},{10,1... | collective-permute-start | bytes 786440 | tf_op jit(solution)/shard_map/ppermute | solution.py:245
  68.2 5.7 %collective-permute-start.25 = (f32[32,512]{1,0:T(8,128)S(1)}, f32[32,512]{1,0:T(8,128)S(1)}, u32[]{:S(2)}, u32[]{:S(2)}) collective-permute-start(f32[32,512]{1,0:T(8,128)S(1)} %get-tuple-element.48), channel_id=1, source_target_pairs={{0,1},{1,0},{2,3},{3,2},{4,5},{5,4},{6,7},{7,6},{8,9},{9,8},{10,11... | collective-permute-start | bytes 196616 | tf_op jit(solution)/shard_map/ppermute | solution.py:249
  68.4 8.5 %collective-permute-start.11 = (bf16[4,16,512]{2,1,0:T(8,128)(2,1)S(1)}, bf16[4,16,512]{2,1,0:T(8,128)(2,1)S(1)}, u32[]{:S(2)}, u32[]{:S(2)}) collective-permute-start(bf16[4,16,512]{2,1,0:T(8,128)(2,1)S(1)} %get-tuple-element.57), channel_id=1, source_target_pairs={{0,15},{1,0},{2,1},{3,2},{4,3},{5,4},{6,5},{7,6},{8,7},{9,8},{10,9... | collective-permute-start | bytes 196616 | tf_op jit(solution)/shard_map/ppermute | solution.py:245
  72.6 6.4 %collective-permute-start.10 = (bf16[4,16,512]{2,1,0:T(8,128)(2,1)S(1)}, bf16[4,16,512]{2,1,0:T(8,128)(2,1)S(1)}, u32[]{:S(2)}, u32[]{:S(2)}) collective-permute-start(bf16[4,16,512]{2,1,0:T(8,128)(2,1)S(1)} %get-tuple-element.58), channel_id=1, source_target_pairs={{0,1},{1,2},{2,3},{3,4},{4,5},{5,6},{6,7},{7,8},{8,9},{9,10},{10,1... | collective-permute-start | bytes 196616 | tf_op jit(solution)/shard_map/ppermute | solution.py:245
  73.9 11.2 %collective-permute-start.28 = (bf16[32,512]{1,0:T(8,128)(2,1)S(1)}, bf16[32,512]{1,0:T(8,128)(2,1)S(1)}, u32[]{:S(2)}, u32[]{:S(2)}) collective-permute-start(bf16[32,512]{1,0:T(8,128)(2,1)S(1)} %fourth_sum.1.one), channel_id=1, source_target_pairs={{0,6},{1,7},{2,4},{3,5},{4,2},{5,3},{6,0},{7,1},{8,14},{9,15},{10,... | collective-permute-start | bytes 98312 | tf_op jit(solution)/shard_map/ppermute | solution.py:249
  76.8 8.3 %collective-permute-start.27 = (bf16[32,512]{1,0:T(8,128)(2,1)S(1)}, bf16[32,512]{1,0:T(8,128)(2,1)S(1)}, u32[]{:S(2)}, u32[]{:S(2)}) collective-permute-start(bf16[32,512]{1,0:T(8,128)(2,1)S(1)} %fourth_sum.1.one), channel_id=1, source_target_pairs={{0,4},{1,5},{2,6},{3,7},{4,0},{5,1},{6,2},{7,3},{8,12},{9,13},{10,... | collective-permute-start | bytes 98312 | tf_op jit(solution)/shard_map/ppermute | solution.py:249
  78.9 6.2 %collective-permute-start.26 = (bf16[32,512]{1,0:T(8,128)(2,1)S(1)}, bf16[32,512]{1,0:T(8,128)(2,1)S(1)}, u32[]{:S(2)}, u32[]{:S(2)}) collective-permute-start(bf16[32,512]{1,0:T(8,128)(2,1)S(1)} %fourth_sum.1.one), channel_id=1, source_target_pairs={{0,2},{1,3},{2,0},{3,1},{4,6},{5,7},{6,4},{7,5},{8,10},{9,11},{10,... | collective-permute-start | bytes 98312 | tf_op jit(solution)/shard_map/ppermute | solution.py:249
  81.2 8.3 %copy-start.4 = (bf16[4,16,32,512]{3,2,1,0:T(8,128)(2,1)S(1)}, bf16[4,16,32,512]{3,2,1,0:T(8,128)(2,1)}, u32[]{:S(2)}) copy-start(bf16[4,16,32,512]{3,2,1,0:T(8,128)(2,1)} %get-tuple-element.27.filt) | copy-start | bytes 6291460
  85.2 6.4 %collective-permute-start.31 = (f32[32,512]{1,0:T(8,128)S(1)}, f32[32,512]{1,0:T(8,128)S(1)}, u32[]{:S(2)}, u32[]{:S(2)}) collective-permute-start(f32[32,512]{1,0:T(8,128)S(1)} %fifth_sum.1.own), channel_id=1, source_target_pairs={{0,9},{1,8},{2,11},{3,10},{4,13},{5,12},{6,15},{7,14},{8,1},{9,0},... | collective-permute-start | bytes 196616 | tf_op jit(solution)/shard_map/ppermute | solution.py:249
  88.6 4.3 %collective-permute-start.30 = (f32[32,512]{1,0:T(8,128)S(1)}, f32[32,512]{1,0:T(8,128)S(1)}, u32[]{:S(2)}, u32[]{:S(2)}) collective-permute-start(f32[32,512]{1,0:T(8,128)S(1)} %fifth_sum.1.own), channel_id=1, source_target_pairs={{0,8},{8,0},{1,9},{9,1},{2,10},{10,2},{3,11},{11,3},{4,12},{12,4},... | collective-permute-start | bytes 196616 | tf_op jit(solution)/shard_map/ppermute | solution.py:249
  89.5 4.3 %collective-permute-start.29 = (f32[32,512]{1,0:T(8,128)S(1)}, f32[32,512]{1,0:T(8,128)S(1)}, u32[]{:S(2)}, u32[]{:S(2)}) collective-permute-start(f32[32,512]{1,0:T(8,128)S(1)} %fifth_sum.1.own), channel_id=1, source_target_pairs={{0,1},{1,0},{2,3},{3,2},{4,5},{5,4},{6,7},{7,6},{8,9},{9,8},{10,11... | collective-permute-start | bytes 196616 | tf_op jit(solution)/shard_map/ppermute | solution.py:249

commit v3 on v1

v3 whole, which is shorter than its diff:
```python
import functools
import math

import jax
import jax.numpy as jnp
from jax import lax
from jax.experimental import pallas as pl
from jax.experimental.pallas import tpu as pltpu
from jax.sharding import Mesh
from jax.sharding import PartitionSpec as P

HL = 2
WL = 16
SPAN = 2 * HL + 1
F32 = jnp.float32
BF16 = jnp.bfloat16
VMEM = pl.BlockSpec(memory_space=pltpu.VMEM)
SMEM = pl.BlockSpec(memory_space=pltpu.SMEM)
PARAMS = pltpu.CompilerParams(vmem_limit_bytes=24 * 1024 * 1024)


def iota(shape, axis):
    return lax.broadcasted_iota(jnp.int32, shape, axis)


def placed_lines(weights, distance, count):
    kinds = iota((weights.shape[0], 1), 0) % count
    return jnp.where(distance == kinds, weights, 0.0)


def store_bands(out, row, lines, basis_count, count, taps):
    cols = out.shape[1] // basis_count
    width = out.shape[2]
    for basis in range(basis_count):
        first = basis * count
        line = lines[first : first + 1]
        for tap in range(1, taps):
            line = line + lines[first + tap : first + tap + 1]
        for lane in range(0, width, 128):
            tile = jnp.broadcast_to(line[:, lane : lane + 128], (cols, 128))
            tile = pltpu.roll(tile, 0, 1, stride=1, stride_axis=0).astype(BF16)
            room = min(128, width - lane)
            out[row, basis * cols : (basis + 1) * cols, lane : lane + room] = tile[:, :room]


def gathered(near_all, place, psi, lat, lon, rows):
    basis_count, blocks, taps, cycles = psi.shape
    lines = basis_count * (taps + 2)
    cycle = iota((cycles, 128), 0) - place[0] + HL
    hot = ((iota((cycles, 128), 1) == cycle) & (cycle < rows + 2 * HL)).astype(BF16)
    for block in range(blocks):
        turns = [lon[block : block + 1].astype(F32), lat[block : block + 1].astype(F32)]
        here = []
        for basis in range(basis_count):
            here += [psi[basis, block].astype(F32)] + turns
        here = jnp.concatenate(here, axis=0).astype(BF16)
        near_all[block * lines : (block + 1) * lines] = jnp.dot(
            here, hot, preferred_element_type=F32
        ).astype(BF16)


def forward_taps_kernel(place, psi, lat, lon, forward, near_all, spread):
    rows = forward.shape[0]
    basis_count, blocks, taps, cycles = psi.shape
    count = taps + 2
    wide = forward.shape[2] // blocks
    lines = basis_count * count
    gathered(near_all, place, psi, lat, lon, rows)
    near = near_all[...]
    slot = iota((128, 128), 0) - HL
    base = iota((1, wide), 1) - WL

    def one_row(row, carry):
        weights_all = jnp.dot(near, (slot == row).astype(BF16), preferred_element_type=F32)
        totals = []
        for block in range(blocks):
            weights = weights_all[block * lines : (block + 1) * lines, :wide]
            distance = base - weights[taps : taps + 1].astype(jnp.int32)
            totals.append(placed_lines(weights, distance, count))
        store_bands(forward, row, jnp.concatenate(totals, axis=1), basis_count, count, taps)
        return carry

    lax.fori_loop(0, rows, one_row, 0, unroll=4)


def adjoint_taps_kernel(place, after, psi, lat, lon, adjoint, near_all, adj_wide):
    rows = adjoint.shape[0]
    basis_count, blocks, taps, cycles = psi.shape
    count = taps + 2
    wide = adjoint.shape[2] // SPAN
    lines = basis_count * count
    gathered(near_all, place, psi, lat, lon, rows)
    near = near_all[...]
    lanes = adj_wide.shape[1]
    slot = iota((128, lanes), 0) - iota((128, lanes), 1) // wide
    inside = iota((128, lanes), 1) // wide < SPAN
    turn = iota((1, lanes), 1)
    wanted = HL - turn // wide
    base = WL - turn % wide

    def one_row(row, carry):
        adj_wide[...] = jnp.dot(
            near, ((slot == row) & inside).astype(BF16), preferred_element_type=F32
        )
        total = None
        for block in range(blocks):
            weights = adj_wide[block * lines : (block + 1) * lines, :]
            shift = weights[taps : taps + 1].astype(jnp.int32)
            match = weights[taps + 1 : taps + 2].astype(jnp.int32) == wanted
            value = placed_lines(weights, base - jnp.where(match, shift, 4 * wide), count)
            total = value if total is None else total + value
        store_bands(adjoint, row, total, basis_count, count, taps)
        return carry

    lax.fori_loop(0, rows, one_row, 0, unroll=2)


def rims_kernel(place, after, inner, outer, to_east, to_west):
    cols = inner.shape[2]
    odd = place[3] == 1
    north = jnp.where(odd, inner[...], outer[...])
    south = jnp.where(odd, outer[...], inner[...])
    to_east[0] = north[:, :, cols - WL :]
    to_east[1] = south[:, :, cols - WL :]
    to_west[0] = north[:, :, :WL]
    to_west[1] = south[:, :, :WL]


def assemble(which, place, extended, center, west, east, inner, outer, rims_w, rims_e):
    rows, cols, _ = center.shape
    extended[HL : HL + rows, 0:WL] = west[...]
    extended[HL : HL + rows, WL : WL + cols] = center[...]
    extended[HL : HL + rows, WL + cols :] = east[...]
    odd = place[3] == 1
    above = place[0] > 0
    below = place[0] + rows < place[5]
    none = jnp.zeros((), BF16)
    north = jnp.where(odd, inner[which], outer[which])
    south = jnp.where(odd, outer[which], inner[which])
    for side, (inside, rim, lines) in enumerate(
        ((above, north, slice(0, HL)), (below, south, slice(HL + rows, None)))
    ):
        extended[lines, 0:WL] = jnp.where(inside, rims_w[side, which], none)
        extended[lines, WL : WL + cols] = jnp.where(inside, rim, none)
        extended[lines, WL + cols :] = jnp.where(inside, rims_e[side, which], none)


def filter_kernel(
    place, lat, taps, center, west, east, inner, outer, rims_w, rims_e, cot, keep, send, filt_out, extended
):
    rows, cols, channels = center.shape
    basis_count = filt_out.shape[0]
    blocks = lat.shape[0]
    assemble(0, place, extended, center, west, east, inner, outer, rims_w, rims_e)

    def one_row(row, carry):
        slabs = [extended[row + HL + lat[block, place[0] + row]] for block in range(blocks)]
        slab = jnp.concatenate(slabs, axis=0)
        filtered = jnp.dot(taps[row], slab, preferred_element_type=F32).astype(BF16)
        filt_out[:, row] = filtered.reshape(basis_count, cols, channels)
        return carry

    lax.fori_loop(0, rows, one_row, 0, unroll=4)
    cot_flat = cot[...].reshape(rows * cols, channels)
    pairs = keep.shape[0] // 2
    share = channels // (2 * pairs)
    per = keep.shape[1] // share
    core = place[3]
    for basis in range(basis_count):
        filtered = filt_out[basis].reshape(rows * cols, channels)
        terms = lax.dot_general(
            filtered, cot_flat, (((0,), (0,)), ((), ())), preferred_element_type=F32
        ).reshape(pairs, 2, share, channels)
        lines = slice(basis % per * share, (basis % per + 1) * share)
        mine = jnp.where(core == 0, terms[:, 0], terms[:, 1])
        other = jnp.where(core == 0, terms[:, 1], terms[:, 0]).astype(BF16)
        for pair in range(pairs):
            keep[2 * pair + basis // per, lines] = mine[pair]
            send[2 * pair + basis // per, lines] = other[pair]


def output_kernel(filt, mixing, out, token):
    token[...] = jnp.zeros_like(token)
    basis_count, rows, cols, channels = filt.shape
    total = None
    for basis in range(basis_count):
        part = jnp.dot(
            filt[basis].reshape(rows * cols, channels), mixing[basis], preferred_element_type=F32
        )
        total = part if total is None else total + part
    out[...] = total.reshape(rows, cols, channels).astype(BF16)


def adjoint_kernel(
    place, after, taps, center, west, east, inner, outer, rims_w, rims_e, mixing, out, token, extended, spread
):
    token[...] = jnp.zeros_like(token)
    rows, cols, channels = center.shape
    basis_count = mixing.shape[0]
    assemble(1, place, extended, center, west, east, inner, outer, rims_w, rims_e)

    def one_row(row, carry):
        slab = extended[pl.ds(row, SPAN)].reshape(SPAN * (cols + 2 * WL), channels)
        pulled = jnp.dot(taps[row], slab, preferred_element_type=F32).astype(BF16)
        spread[:, row] = pulled.reshape(basis_count, cols, channels)
        return carry

    lax.fori_loop(0, rows, one_row, 0, unroll=4)
    total = None
    for basis in range(basis_count):
        part = lax.dot_general(
            spread[basis].reshape(rows * cols, channels),
            mixing[basis],
            (((1,), (1,)), ((), ())),
            preferred_element_type=F32,
        )
        total = part if total is None else total + part
    out[...] = total.reshape(rows, cols, channels).astype(BF16)


def pair_sum_kernel(after, keep, recv, out):
    out[...] = (keep[...] + recv[...].astype(F32)).astype(BF16)


def chip_sum_kernel(after, parts, out):
    total = parts[0].astype(F32)
    for chip in range(1, parts.shape[0]):
        total = total + parts[chip].astype(F32)
    out[...] = total.astype(BF16)


def four_sum_kernel(one, two, three, four, out):
    near = one[...].astype(F32) + two[...].astype(F32)
    far = three[...].astype(F32) + four[...].astype(F32)
    out[...] = (near + far).astype(BF16)


def last_sum_kernel(normalizer, place, own, by_z, by_x, by_both, out):
    low = lax.rem(place[2], 2)
    shape = (2,) + out.shape[1:]
    mine = own[...].astype(F32) + by_z[...].astype(F32)
    other = by_x[...].astype(F32) + by_both[...].astype(F32)
    out[pl.ds(2 * low, 2)] = (mine * normalizer).reshape(shape)
    out[pl.ds(2 * (1 - low), 2)] = (other * normalizer).reshape(shape)


LAT = ("y", "xh", "core")
LON = ("xl", "z")
CROSS = ("xh", "xl")


def shift(cells, axis, count, step):
    return lax.ppermute(cells, axis, [(i, (i + step) % count) for i in range(count)])


def swap(cells, axis, count, mask):
    return lax.ppermute(cells, axis, [(i, i ^ mask) for i in range(count)])


def call(kernel, outs, args, specs, name, scratch=(), flops=0, moved=0):
    return pl.pallas_call(
        kernel,
        out_shape=outs,
        in_specs=specs,
        out_specs=jax.tree.map(lambda _: VMEM, outs),
        scratch_shapes=list(scratch),
        compiler_params=PARAMS,
        cost_estimate=pl.CostEstimate(flops=flops, bytes_accessed=moved, transcendentals=0),
        name=name,
    )(*args)


def shaped(shape, dtype):
    return jax.ShapeDtypeStruct(shape, dtype)


def local(field, filter_values, block_lat, block_lon, mixing, cotangent):
    rows, cols, channels = field.shape
    basis_count, _, blocks, taps = filter_values.shape
    lats = lax.axis_size(LAT)
    lons = lax.axis_size(LON)
    place = jnp.stack(
        [
            lax.axis_index(LAT) * rows,
            lax.axis_index("y"),
            lax.axis_index(CROSS),
            lax.axis_index("core"),
            lax.axis_index("z"),
            jnp.int32(rows * lats),
        ]
    ).astype(jnp.int32)
    both = (field, cotangent)
    odd = lax.axis_index("core") == 1
    top = jnp.stack([cells[:HL] for cells in both])
    bottom = jnp.stack([cells[rows - HL :] for cells in both])
    inner = jnp.where(odd, top, bottom)
    outer = jnp.where(odd, bottom, top)
    west = shift(field[:, cols - WL :], LON, lons, 1)
    east = shift(field[:, :WL], LON, lons, -1)
    psi = filter_values.transpose(0, 2, 3, 1)
    lat = block_lat.T
    lon = block_lon.T
    wide = cols + 2 * WL
    lines = basis_count * blocks * (taps + 2)
    fwd_taps = call(
        forward_taps_kernel,
        shaped((rows, basis_count * cols, blocks * wide), BF16),
        (place, psi, lat, lon),
        [SMEM] + [VMEM] * 3,
        "forward_taps",
        [pltpu.VMEM((lines, 128), BF16), pltpu.VMEM((lines, 128), F32)],
        flops=1_000_000_000,
        moved=1_000_000,
    )
    inner = swap(inner, LAT, lats, 1)
    pairs = [(0, 0), (lats - 1, lats - 1)]
    for low in range(1, lats - 1, 2):
        pairs += [(low, low + 1), (low + 1, low)]
    outer = lax.ppermute(outer, LAT, pairs)
    rim = shaped((2, 2, HL, WL, channels), BF16)
    rim_to_east, rim_to_west = call(
        rims_kernel,
        (rim, rim),
        (place, fwd_taps, inner, outer),
        [SMEM] + [VMEM] * 3,
        "rims",
        moved=1_000_000,
    )
    rims_w = shift(rim_to_east, LON, lons, 1)
    rims_e = shift(rim_to_west, LON, lons, -1)
    share = basis_count * channels // lats
    keep, send, filtered = call(
        filter_kernel,
        (
            shaped((lats, share // 2, channels), F32),
            shaped((lats, share // 2, channels), BF16),
            shaped((basis_count, rows, cols, channels), BF16),
        ),
        (place, lat, fwd_taps, field, west, east, inner, outer, rims_w, rims_e, cotangent),
        [SMEM] * 2 + [VMEM] * 9,
        "filtering",
        [pltpu.VMEM((rows + 2 * HL, wide, channels), BF16)],
        flops=2_000_000_000,
        moved=8_000_000,
    )
    recv = swap(send, "core", 2, 1)
    cot_west = shift(cotangent[:, cols - WL :], LON, lons, 1)
    cot_east = shift(cotangent[:, :WL], LON, lons, -1)
    token = shaped((8, 128), F32)
    output, token_one = call(
        output_kernel,
        (shaped((rows, cols, channels), BF16), token),
        (filtered, mixing),
        [VMEM] * 2,
        "mixed",
        flops=1_500_000_000,
        moved=4_500_000,
    )
    summed = call(
        pair_sum_kernel,
        shaped(keep.shape, BF16),
        (token_one, keep, recv),
        [VMEM] * 3,
        "pair_sum",
        flops=keep.size,
        moved=keep.size * 8,
    )
    parts = lax.all_to_all(summed, ("y", "xh", "xl"), 0, 0)

    adj_taps = call(
        adjoint_taps_kernel,
        shaped((rows, basis_count * cols, SPAN * wide), BF16),
        (place, summed, psi, lat, lon),
        [SMEM] + [VMEM] * 4,
        "adjoint_taps",
        [
            pltpu.VMEM((lines, 128), BF16),
            pltpu.VMEM((lines, -(-SPAN * wide // 128) * 128), F32),
        ],
        flops=2_000_000_000,
        moved=2_000_000,
    )
    field_grad, token_two = call(
        adjoint_kernel,
        (shaped((rows, cols, channels), BF16), token),
        (
            place,
            summed,
            adj_taps,
            cotangent,
            cot_west,
            cot_east,
            inner,
            outer,
            rims_w,
            rims_e,
            mixing,
        ),
        [SMEM, VMEM] + [VMEM] * 9,
        "adjoint",
        [
            pltpu.VMEM((rows + 2 * HL, wide, channels), BF16),
            pltpu.VMEM((basis_count, rows, cols, channels), BF16),
        ],
        flops=3_000_000_000,
        moved=6_000_000,
    )

    _, deep, _ = parts.shape
    part = call(
        chip_sum_kernel,
        shaped((deep, channels), BF16),
        (token_two, parts),
        [VMEM] * 2,
        "chip_sum",
        flops=parts.size,
        moved=parts.size * 2,
    )
    part = call(
        four_sum_kernel,
        shaped((deep, channels), BF16),
        (part, *(swap(part, "z", 8, mask) for mask in (2, 4, 6))),
        [VMEM] * 4,
        "four_sum",
        flops=part.size * 4,
        moved=part.size * 10,
    )
    normalizer = 1.0 / math.sqrt(rows * lats * cols * lons)
    mixing_grad = call(
        functools.partial(last_sum_kernel, normalizer),
        shaped((basis_count, channels // lats, channels), F32),
        (place, part, swap(part, "z", 8, 1), swap(part, "xl", 2, 1), swap(part, LON, 16, 9)),
        [SMEM] + [VMEM] * 4,
        "last_sum",
        flops=part.size * 4,
        moved=part.size * 16,
    )
    return (output, field_grad, mixing_grad)


def solution(mesh):
    grid = Mesh(mesh.devices.reshape(4, 2, 2, 2, 8), ("y", "xh", "core", "xl", "z"))
    return jax.shard_map(
        local,
        mesh=grid,
        in_specs=(P(LAT, LON, None), P(), P(), P(), P(), P(LAT, LON, None)),
        out_specs=(P(LAT, LON, None), P(LAT, LON, None), P(None, LAT, None)),
        check_vma=False,
    )
```

time: 274 us -> 79.9 us (0.29)
  waiting for transfers between devices: 221 us -> 18.2 us
  starting transfers between devices: 13.3 us -> 37.5 us
  between operations: 14.3 us -> 0.85 us
  other arithmetic: 5.61 us -> 0.03 us
  Pallas kernels: 14.8 us -> 19.9 us
    psum x1 -> x0, waiting for transfers between devices: 125 us -> none  [reduced(): return lax.psum(summed[0], 'lon')]
    reduce_scatter x1 -> x0, waiting for transfers between devices: 79.9 us -> none  [reduced(): lax.psum_scatter(terms.astype(F32), 'lat', scatter_dimension=0, tiled=True)]
    ppermute x8 -> x15, starting transfers between devices: 13.2 us -> 28.3 us  [the longest x6 14.4 us: shift(): lax.ppermute(cells, axis, [(i, (i + step) % count) for i in range(count)])]
    all_to_all x0 -> x1, starting transfers between devices: none -> 9.19 us  [local(): parts = lax.all_to_all(summed, ('y', 'xh', 'xl'), 0, 0)]
    all_to_all x0 -> x1, waiting for transfers between devices: none -> 6.43 us  [local(): parts = lax.all_to_all(summed, ('y', 'xh', 'xl'), 0, 0)]
    pallas_call x4 -> x10, Pallas kernels: 14.8 us -> 19.9 us  [call(): pl.pallas_call(kernel, out_shape=outs, in_specs=specs, out_specs=jax.tree...]
    ppermute x8 -> x15, waiting for transfers between devices: 15.4 us -> 11.8 us  [the longest x8 7.02 us: swap(): return lax.ppermute(cells, axis, [(i, i ^ mask) for i in range(count)])]
    convert_element_type x3 -> x0, other arithmetic: 3.22 us -> none  [the longest x1 2.52 us: reduced(): terms.astype(F32)]
  transfers between devices with their start and end apart: 10 -> 16, of which waited for: 7 -> 9; matrix products, arithmetic and copies ran while one was open for 1% -> 1% of each run, Pallas kernels for 4% -> 18%
where the time goes in v3:
time: 79.9 us; the launch traced here: 79.5 us
  starting transfers between devices  37.5 us (47%)
  Pallas kernels  19.9 us (25%)
  waiting for transfers between devices  18.2 us (23%)
  local copies, waits for them, and re-layouts  3 us (4%)
  between operations  0.85 us (1%)
    pallas_call x10, Pallas kernels, call(): pl.pallas_call(kernel, out_shape=outs, in_specs=specs, out_specs=jax.tree...  19.9 us
    ppermute x6, starting transfers between devices, shift(): lax.ppermute(cells, axis, [(i, (i + step) % count) for i in range(count)])  14.4 us
    ppermute x8, starting transfers between devices, swap(): return lax.ppermute(cells, axis, [(i, i ^ mask) for i in range(count)])  13.3 us
    all_to_all x1, starting transfers between devices, local(): parts = lax.all_to_all(summed, ('y', 'xh', 'xl'), 0, 0)  9.19 us
    ppermute x8, waiting for transfers between devices, swap(): return lax.ppermute(cells, axis, [(i, i ^ mask) for i in range(count)])  7.02 us
    all_to_all x1, waiting for transfers between devices, local(): parts = lax.all_to_all(summed, ('y', 'xh', 'xl'), 0, 0)  6.43 us
    ppermute x6, waiting for transfers between devices, shift(): lax.ppermute(cells, axis, [(i, (i + step) % count) for i in range(count)])  4.74 us
    another operation x2, local copies, waits for them, and re-layouts, local(): top = jnp.stack([cells[:HL] for cells in both])  1.78 us
  transfers between devices with their start and end apart: 16, of which 9 were waited for; matrix products, arithmetic and copies ran while one was open for 1% of the time, Pallas kernels for 18%

profile of v3, /device:TPU:2, one launch (start us, length us, event | category | flops | bytes accessed | tf_op | source)
XLA Modules:
  0.0 79.5 jit_solution(9191491288621647354)
XLA Ops:
  0.6 0.0 copy-start.5
  0.6 0.0 copy-start.4
  0.7 0.0 copy-start.6
  0.7 0.9 %slice_bitcast_fusion.3 = (bf16[1,2,32,512]{3,2,1,0:T(8,128)(2,1)S(1)}, bf16[1,2,32,512]{3,2,1,0:T(8,128)(2,1)S(1)}) fusion(bf16[16,32,512]{2,1,0:T(8,128)(2,1)} %center.2), kind=kLoop, calls=%fused_computation.7 | loop fusion | bytes 262144 | tf_op jit(solution)/shard_map/stack | solution.py:294
  1.6 0.9 %slice_bitcast_fusion.2 = (bf16[1,2,32,512]{3,2,1,0:T(8,128)(2,1)S(1)}, bf16[1,2,32,512]{3,2,1,0:T(8,128)(2,1)S(1)}) fusion(bf16[16,32,512]{2,1,0:T(8,128)(2,1)} %center.3), kind=kLoop, calls=%fused_computation.6 | loop fusion | bytes 262144 | tf_op jit(solution)/shard_map/stack | solution.py:294
  2.5 0.1 collective-permute-start.2
  2.6 0.7 collective-permute-start.3
  3.3 1.1 %fusion.1 = (bf16[16,16,512]{2,1,0:T(8,128)(2,1)S(1)}, bf16[16,16,512]{2,1,0:T(8,128)(2,1)S(1)}) fusion(bf16[16,32,512]{2,1,0:T(8,128)(2,1)} %center.2), kind=kLoop, calls=%fused_computation.9 | loop fusion | bytes 1048576 | tf_op jit(solution)/shard_map/slice | solution.py:299
  4.3 2.0 %collective-permute-start = (bf16[16,16,512]{2,1,0:T(8,128)(2,1)S(1)}, bf16[16,16,512]{2,1,0:T(8,128)(2,1)S(1)}, u32[]{:S(2)}, u32[]{:S(2)}) collective-permute-start(bf16[16,16,512]{2,1,0:T(8,128)(2,1)S(1)} %get-tuple-element.28), channel_id=1, source_target_pairs={{0,1},{1,2},{2,3},{3,4},{4,5},{5,6},{6,7},{7,8},{8,9},{9,10},{10,1... | collective-permute-start | bytes 786440 | tf_op jit(solution)/shard_map/ppermute | solution.py:253
  6.3 4.0 %collective-permute-start.1 = (bf16[16,16,512]{2,1,0:T(8,128)(2,1)S(1)}, bf16[16,16,512]{2,1,0:T(8,128)(2,1)S(1)}, u32[]{:S(2)}, u32[]{:S(2)}) collective-permute-start(bf16[16,16,512]{2,1,0:T(8,128)(2,1)S(1)} %get-tuple-element.27), channel_id=1, source_target_pairs={{0,15},{1,0},{2,1},{3,2},{4,3},{5,4},{6,5},{7,6},{8,7},{9,8},{10,9... | collective-permute-start | bytes 786440 | tf_op jit(solution)/shard_map/ppermute | solution.py:253
  10.3 0.1 stack.41.place
  10.4 0.0 copy-done.5
  10.4 0.0 copy-done.4
  10.4 0.0 copy-done.6
  10.4 0.0 copy-start
  10.4 0.0 copy-start.1
  10.5 2.2 %forward_taps.1.after.taps = bf16[16,128,256]{2,1,0:T(8,128)(2,1)S(1)} custom-call(s32[6]{0:T(128)S(1)} %stack.41.place, bf16[4,4,4,256]{3,2,1,0:T(4,128)(2,1)S(1)} %bitcast.16, s32[4,256]{1,0:T(4,128)S(1)} %bitcast.18, s32[4,256]{1,0:T(4,128)S(1)} %bitcast.21), custom_call_target="tpu_custom_call" | custom-call | flops 1000000000 | bytes 1000000 | tf_op jit(solution)/shard_map/forward_taps/pallas_call | solution.py:261
  12.7 0.0 collective-permute-done.2.inner
  12.7 0.0 collective-permute-done.3.outer
  12.7 0.6 rims.1
  13.3 0.1 collective-permute-start.4
  13.4 0.0 copy-start.2
  13.4 4.1 %collective-permute-start.5 = (bf16[2,2,2,16,512]{4,3,2,1,0:T(8,128)(2,1)S(1)}, bf16[2,2,2,16,512]{4,3,2,1,0:T(8,128)(2,1)S(1)}, u32[]{:S(2)}, u32[]{:S(2)}) collective-permute-start(bf16[2,2,2,16,512]{4,3,2,1,0:T(8,128)(2,1)S(1)} %get-tuple-element.13), channel_id=1, source_target_pairs={{0,15},{1,0},{2,1},{3,2},{4,3},{5,4},{6,5},{7,6},{8,7},{9,8},{10,9... | collective-permute-start | bytes 393224 | tf_op jit(solution)/shard_map/ppermute | solution.py:253
  17.5 2.9 %collective-permute-done.4.rims_w = bf16[2,2,2,16,512]{4,3,2,1,0:T(8,128)(2,1)S(1)} collective-permute-done((bf16[2,2,2,16,512]{4,3,2,1,0:T(8,128)(2,1)S(1)}, bf16[2,2,2,16,512]{4,3,2,1,0:T(8,128)(2,1)S(1)}, u32[]{:S(2)}, u32[]{:S(2)}) %collective-permute-start.4) | collective-permute-done | bytes 131104 | tf_op jit(solution)/shard_map/ppermute | solution.py:253
  20.4 0.0 collective-permute-done.5.rims_e
  20.4 0.0 collective-permute-done.west
  20.4 0.0 collective-permute-done.1.east
  20.4 0.0 copy-done
  20.4 0.0 copy-done.1
  20.5 3.2 %filtering.1 = (f32[16,64,512]{2,1,0:T(8,128)S(1)}, bf16[16,64,512]{2,1,0:T(8,128)(2,1)S(1)}, bf16[4,16,32,512]{3,2,1,0:T(8,128)(2,1)S(1)}) custom-call(s32[6]{0:T(128)S(1)} %stack.41.place, s32[4,256]{1,0:T(4,128)S(1)} %bitcast.19, bf16[16,128,256]{2,1,0:T(8,128)(2,1)S(1)} %forward_taps.1.after.taps, bf16[16,32,512]{2,1,0:T(8,128)(2,1)S(1)} %copy-done, ...), custom_call_target="tpu_custom_call" | custom-call | flops 2000000000 | bytes 8000000 | tf_op jit(solution)/shard_map/filtering/pallas_call | solution.py:261
  23.7 3.0 %collective-permute-start.6 = (bf16[16,64,512]{2,1,0:T(8,128)(2,1)S(1)}, bf16[16,64,512]{2,1,0:T(8,128)(2,1)S(1)}, u32[]{:S(2)}, u32[]{:S(2)}) collective-permute-start(bf16[16,64,512]{2,1,0:T(8,128)(2,1)S(1)} %get-tuple-element.18), channel_id=1, source_target_pairs={{0,16},{16,0},{1,17},{17,1},{2,18},{18,2},{3,19},{19,3},{4,20},{20... | collective-permute-start | bytes 3145736 | tf_op jit(solution)/shard_map/ppermute | solution.py:257
  26.7 0.0 copy-done.2
  26.7 2.0 %mixed.1 = (bf16[16,32,512]{2,1,0:T(8,128)(2,1)}, f32[8,128]{1,0:T(8,128)S(1)}) custom-call(bf16[4,16,32,512]{3,2,1,0:T(8,128)(2,1)S(1)} %get-tuple-element.14.filt, bf16[4,512,512]{2,1,0:T(8,128)(2,1)S(1)} %copy-done.2), custom_call_target="tpu_custom_call" | custom-call | flops 1500000000 | bytes 4500000 | tf_op jit(solution)/shard_map/mixed/pallas_call | solution.py:261
  28.8 0.2 collective-permute-done.6.recv
  29.0 1.2 %pair_sum.1.after = bf16[16,64,512]{2,1,0:T(8,128)(2,1)} custom-call(f32[8,128]{1,0:T(8,128)S(1)} %get-tuple-element.16.after, f32[16,64,512]{2,1,0:T(8,128)S(1)} %get-tuple-element.17.keep, bf16[16,64,512]{2,1,0:T(8,128)(2,1)S(1)} %collective-permute-done.6.recv), custom_call_target="tpu_custom_call" | custom-call | flops 524288 | bytes 4194304 | tf_op jit(solution)/shard_map/pair_sum/pallas_call | solution.py:261
  30.2 9.2 %all-to-all-start = ((bf16[16,64,512]{2,1,0:T(8,128)(2,1)}), bf16[16,64,512]{2,1,0:T(8,128)(2,1)S(1)}, u32[]{:S(2)}, u32[]{:S(2)}) async-start(bf16[16,64,512]{2,1,0:T(8,128)(2,1)} %pair_sum.1.after), calls=%async_computation | async-start | bytes 2097152 | tf_op jit(solution)/shard_map/all_to_all | solution.py:368
  39.5 0.1 collective-permute-start.7
  39.5 0.0 copy-start.3
  39.6 4.1 %collective-permute-start.8 = (bf16[16,16,512]{2,1,0:T(8,128)(2,1)S(1)}, bf16[16,16,512]{2,1,0:T(8,128)(2,1)S(1)}, u32[]{:S(2)}, u32[]{:S(2)}) collective-permute-start(bf16[16,16,512]{2,1,0:T(8,128)(2,1)S(1)} %get-tuple-element.21), channel_id=1, source_target_pairs={{0,15},{1,0},{2,1},{3,2},{4,3},{5,4},{6,5},{7,6},{8,7},{9,8},{10,9... | collective-permute-start | bytes 786440 | tf_op jit(solution)/shard_map/ppermute | solution.py:253
  43.7 4.1 %adjoint_taps.1.taps = bf16[16,128,320]{2,1,0:T(8,128)(2,1)S(1)} custom-call(s32[6]{0:T(128)S(1)} %stack.41.place, bf16[16,64,512]{2,1,0:T(8,128)(2,1)} %pair_sum.1.after, bf16[4,4,4,256]{3,2,1,0:T(4,128)(2,1)S(1)} %bitcast.17, s32[4,256]{1,0:T(4,128)S(1)} %bitcast.20, s32[4,256]{1,0:T(4,128)S(1)} %bitcast.22), custom_call_target="tpu_custom_call" | custom-call | flops 2000000000 | bytes 2000000 | tf_op jit(solution)/shard_map/adjoint_taps/pallas_call | solution.py:261
  47.7 1.8 %collective-permute-done.7.west = bf16[16,16,512]{2,1,0:T(8,128)(2,1)S(1)} collective-permute-done((bf16[16,16,512]{2,1,0:T(8,128)(2,1)S(1)}, bf16[16,16,512]{2,1,0:T(8,128)(2,1)S(1)}, u32[]{:S(2)}, u32[]{:S(2)}) %collective-permute-start.7) | collective-permute-done | bytes 262176 | tf_op jit(solution)/shard_map/ppermute | solution.py:253
  49.5 0.0 collective-permute-done.8.east
  49.5 0.0 copy-done.3
  49.5 5.2 %adjoint.1 = (bf16[16,32,512]{2,1,0:T(8,128)(2,1)}, f32[8,128]{1,0:T(8,128)S(1)}) custom-call(s32[6]{0:T(128)S(1)} %stack.41.place, bf16[16,64,512]{2,1,0:T(8,128)(2,1)} %pair_sum.1.after, bf16[16,128,320]{2,1,0:T(8,128)(2,1)S(1)} %adjoint_taps.1.taps, bf16[16,32,512]{2,1,0:T(8,128)(2,1)S(1)} %copy-done.1, ...), custom_call_target="tpu_custom_call" | custom-call | flops 3000000000 | bytes 6000000 | tf_op jit(solution)/shard_map/adjoint/pallas_call | solution.py:261
  54.7 6.4 %all-to-all-done.parts = bf16[16,64,512]{2,1,0:T(8,128)(2,1)S(1)} async-done(((bf16[16,64,512]{2,1,0:T(8,128)(2,1)}), bf16[16,64,512]{2,1,0:T(8,128)(2,1)S(1)}, u32[]{:S(2)}, u32[]{:S(2)}) %all-to-all-start) | async-done | bytes 1048608 | tf_op jit(solution)/shard_map/all_to_all | solution.py:368
  61.1 0.1 chip_sum.1.one
  61.3 0.1 collective-permute-start.10
  61.4 0.1 collective-permute-start.11
  61.5 6.4 %collective-permute-start.9 = (bf16[64,512]{1,0:T(8,128)(2,1)S(1)}, bf16[64,512]{1,0:T(8,128)(2,1)S(1)}, u32[]{:S(2)}, u32[]{:S(2)}) collective-permute-start(bf16[64,512]{1,0:T(8,128)(2,1)S(1)} %chip_sum.1.one), channel_id=1, source_target_pairs={{0,2},{1,3},{2,0},{3,1},{4,6},{5,7},{6,4},{7,5},{8,10},{9,11},{10,... | collective-permute-start | bytes 196616 | tf_op jit(solution)/shard_map/ppermute | solution.py:257
  67.9 2.5 %collective-permute-done.10.three = bf16[64,512]{1,0:T(8,128)(2,1)S(1)} collective-permute-done((bf16[64,512]{1,0:T(8,128)(2,1)S(1)}, bf16[64,512]{1,0:T(8,128)(2,1)S(1)}, u32[]{:S(2)}, u32[]{:S(2)}) %collective-permute-start.10) | collective-permute-done | bytes 65568 | tf_op jit(solution)/shard_map/ppermute | solution.py:257
  70.3 0.0 collective-permute-done.11.four
  70.3 1.0 %collective-permute-done.9.two = bf16[64,512]{1,0:T(8,128)(2,1)S(1)} collective-permute-done((bf16[64,512]{1,0:T(8,128)(2,1)S(1)}, bf16[64,512]{1,0:T(8,128)(2,1)S(1)}, u32[]{:S(2)}, u32[]{:S(2)}) %collective-permute-start.9) | collective-permute-done | bytes 65568 | tf_op jit(solution)/shard_map/ppermute | solution.py:257
  71.4 0.3 collective-permute-start.12
  71.6 1.5 %collective-permute-start.13 = (bf16[64,512]{1,0:T(8,128)(2,1)S(1)}, bf16[64,512]{1,0:T(8,128)(2,1)S(1)}, u32[]{:S(2)}, u32[]{:S(2)}) collective-permute-start(bf16[64,512]{1,0:T(8,128)(2,1)S(1)} %four_sum.1.own), channel_id=1, source_target_pairs={{0,8},{8,0},{1,9},{9,1},{2,10},{10,2},{3,11},{11,3},{4,12},{12,4},... | collective-permute-start | bytes 196616 | tf_op jit(solution)/shard_map/ppermute | solution.py:257
  73.1 1.9 %collective-permute-start.14 = (bf16[64,512]{1,0:T(8,128)(2,1)S(1)}, bf16[64,512]{1,0:T(8,128)(2,1)S(1)}, u32[]{:S(2)}, u32[]{:S(2)}) collective-permute-start(bf16[64,512]{1,0:T(8,128)(2,1)S(1)} %four_sum.1.own), channel_id=1, source_target_pairs={{0,9},{1,8},{2,11},{3,10},{4,13},{5,12},{6,15},{7,14},{8,1},{9,0},... | collective-permute-start | bytes 196616 | tf_op jit(solution)/shard_map/ppermute | solution.py:257
  74.9 0.8 collective-permute-done.12.by_z
  75.7 0.2 collective-permute-done.13.by_x
  75.9 2.4 %collective-permute-done.14.by_both = bf16[64,512]{1,0:T(8,128)(2,1)S(1)} collective-permute-done((bf16[64,512]{1,0:T(8,128)(2,1)S(1)}, bf16[64,512]{1,0:T(8,128)(2,1)S(1)}, u32[]{:S(2)}, u32[]{:S(2)}) %collective-permute-start.14) | collective-permute-done | bytes 65568 | tf_op jit(solution)/shard_map/ppermute | solution.py:257
  78.2 1.3 %last_sum.1 = f32[4,32,512]{2,1,0:T(8,128)} custom-call(s32[6]{0:T(128)S(1)} %stack.41.place, bf16[64,512]{1,0:T(8,128)(2,1)S(1)} %four_sum.1.own, bf16[64,512]{1,0:T(8,128)(2,1)S(1)} %collective-permute-done.12.by_z, bf16[64,512]{1,0:T(8,128)(2,1)S(1)} %collective-permute-done.13.by_x, bf16[64,512]{1,0:T(8,128)(2,1)S(1)} %collective-permute-done.14.by_both), custom_call_target="tpu_custom_call" | custom-call | flops 131072 | bytes 524288 | tf_op jit(solution)/shard_map/last_sum/pallas_call | solution.py:261
  (3 shorter events, 0.1 us)
Async XLA Ops:
  0.6 9.8 %copy-start.5 = (s32[256,4]{0,1:T(4,128)S(1)}, s32[256,4]{0,1:T(4,128)}, u32[]{:S(2)}) copy-start(s32[256,4]{0,1:T(4,128)} %param.8) | copy-start | bytes 12292
  0.6 9.8 %copy-start.4 = (bf16[4,256,4,4]{1,3,2,0:T(4,128)(2,1)S(1)}, bf16[4,256,4,4]{1,3,2,0:T(4,128)(2,1)}, u32[]{:S(2)}) copy-start(bf16[4,256,4,4]{1,3,2,0:T(4,128)(2,1)} %param.7) | copy-start | bytes 98308
  0.7 9.8 %copy-start.6 = (s32[256,4]{0,1:T(4,128)S(1)}, s32[256,4]{0,1:T(4,128)}, u32[]{:S(2)}) copy-start(s32[256,4]{0,1:T(4,128)} %param.9) | copy-start | bytes 12292
  2.5 10.2 %collective-permute-start.2 = (bf16[2,2,32,512]{3,2,1,0:T(8,128)(2,1)S(1)}, bf16[2,2,32,512]{3,2,1,0:T(8,128)(2,1)S(1)}, u32[]{:S(2)}, u32[]{:S(2)}) collective-permute-start(bf16[2,2,32,512]{3,2,1,0:T(8,128)(2,1)S(1)} %get-tuple-element.30), channel_id=1, source_target_pairs={{0,16},{16,0},{32,48},{48,32},{64,80},{80,64},{96,112},{112,96},{1... | collective-permute-start | bytes 393224 | tf_op jit(solution)/shard_map/ppermute | solution.py:257
  2.6 10.1 %collective-permute-start.3 = (bf16[2,2,32,512]{3,2,1,0:T(8,128)(2,1)S(1)}, bf16[2,2,32,512]{3,2,1,0:T(8,128)(2,1)S(1)}, u32[]{:S(2)}, u32[]{:S(2)}) collective-permute-start(bf16[2,2,32,512]{3,2,1,0:T(8,128)(2,1)S(1)} %get-tuple-element.29), channel_id=1, source_target_pairs={{0,0},{240,240},{16,32},{32,16},{48,64},{64,48},{80,96},{96,80},{1... | collective-permute-start | bytes 393224 | tf_op jit(solution)/shard_map/ppermute | solution.py:319
  4.3 16.1 %collective-permute-start = (bf16[16,16,512]{2,1,0:T(8,128)(2,1)S(1)}, bf16[16,16,512]{2,1,0:T(8,128)(2,1)S(1)}, u32[]{:S(2)}, u32[]{:S(2)}) collective-permute-start(bf16[16,16,512]{2,1,0:T(8,128)(2,1)S(1)} %get-tuple-element.28), channel_id=1, source_target_pairs={{0,1},{1,2},{2,3},{3,4},{4,5},{5,6},{6,7},{7,8},{8,9},{9,10},{10,1... | collective-permute-start | bytes 786440 | tf_op jit(solution)/shard_map/ppermute | solution.py:253
  6.3 14.1 %collective-permute-start.1 = (bf16[16,16,512]{2,1,0:T(8,128)(2,1)S(1)}, bf16[16,16,512]{2,1,0:T(8,128)(2,1)S(1)}, u32[]{:S(2)}, u32[]{:S(2)}) collective-permute-start(bf16[16,16,512]{2,1,0:T(8,128)(2,1)S(1)} %get-tuple-element.27), channel_id=1, source_target_pairs={{0,15},{1,0},{2,1},{3,2},{4,3},{5,4},{6,5},{7,6},{8,7},{9,8},{10,9... | collective-permute-start | bytes 786440 | tf_op jit(solution)/shard_map/ppermute | solution.py:253
  10.4 10.0 %copy-start = (bf16[16,32,512]{2,1,0:T(8,128)(2,1)S(1)}, bf16[16,32,512]{2,1,0:T(8,128)(2,1)}, u32[]{:S(2)}) copy-start(bf16[16,32,512]{2,1,0:T(8,128)(2,1)} %center.2) | copy-start | bytes 1572868
  10.4 10.0 %copy-start.1 = (bf16[16,32,512]{2,1,0:T(8,128)(2,1)S(1)}, bf16[16,32,512]{2,1,0:T(8,128)(2,1)}, u32[]{:S(2)}) copy-start(bf16[16,32,512]{2,1,0:T(8,128)(2,1)} %center.3) | copy-start | bytes 1572868
  13.3 7.2 %collective-permute-start.4 = (bf16[2,2,2,16,512]{4,3,2,1,0:T(8,128)(2,1)S(1)}, bf16[2,2,2,16,512]{4,3,2,1,0:T(8,128)(2,1)S(1)}, u32[]{:S(2)}, u32[]{:S(2)}) collective-permute-start(bf16[2,2,2,16,512]{4,3,2,1,0:T(8,128)(2,1)S(1)} %get-tuple-element.12), channel_id=1, source_target_pairs={{0,1},{1,2},{2,3},{3,4},{4,5},{5,6},{6,7},{7,8},{8,9},{9,10},{10,1... | collective-permute-start | bytes 393224 | tf_op jit(solution)/shard_map/ppermute | solution.py:253
  13.4 13.4 %copy-start.2 = (bf16[4,512,512]{2,1,0:T(8,128)(2,1)S(1)}, bf16[4,512,512]{2,1,0:T(8,128)(2,1)}, u32[]{:S(2)}) copy-start(bf16[4,512,512]{2,1,0:T(8,128)(2,1)} %mixing.3) | copy-start | bytes 6291460
  13.4 7.1 %collective-permute-start.5 = (bf16[2,2,2,16,512]{4,3,2,1,0:T(8,128)(2,1)S(1)}, bf16[2,2,2,16,512]{4,3,2,1,0:T(8,128)(2,1)S(1)}, u32[]{:S(2)}, u32[]{:S(2)}) collective-permute-start(bf16[2,2,2,16,512]{4,3,2,1,0:T(8,128)(2,1)S(1)} %get-tuple-element.13), channel_id=1, source_target_pairs={{0,15},{1,0},{2,1},{3,2},{4,3},{5,4},{6,5},{7,6},{8,7},{9,8},{10,9... | collective-permute-start | bytes 393224 | tf_op jit(solution)/shard_map/ppermute | solution.py:253
  23.7 5.3 %collective-permute-start.6 = (bf16[16,64,512]{2,1,0:T(8,128)(2,1)S(1)}, bf16[16,64,512]{2,1,0:T(8,128)(2,1)S(1)}, u32[]{:S(2)}, u32[]{:S(2)}) collective-permute-start(bf16[16,64,512]{2,1,0:T(8,128)(2,1)S(1)} %get-tuple-element.18), channel_id=1, source_target_pairs={{0,16},{16,0},{1,17},{17,1},{2,18},{18,2},{3,19},{19,3},{4,20},{20... | collective-permute-start | bytes 3145736 | tf_op jit(solution)/shard_map/ppermute | solution.py:257
  30.2 30.9 %all-to-all-start = ((bf16[16,64,512]{2,1,0:T(8,128)(2,1)}), bf16[16,64,512]{2,1,0:T(8,128)(2,1)S(1)}, u32[]{:S(2)}, u32[]{:S(2)}) async-start(bf16[16,64,512]{2,1,0:T(8,128)(2,1)} %pair_sum.1.after), calls=%async_computation | async-start | bytes 2097152 | tf_op jit(solution)/shard_map/all_to_all | solution.py:368
  39.5 10.1 %collective-permute-start.7 = (bf16[16,16,512]{2,1,0:T(8,128)(2,1)S(1)}, bf16[16,16,512]{2,1,0:T(8,128)(2,1)S(1)}, u32[]{:S(2)}, u32[]{:S(2)}) collective-permute-start(bf16[16,16,512]{2,1,0:T(8,128)(2,1)S(1)} %get-tuple-element.22), channel_id=1, source_target_pairs={{0,1},{1,2},{2,3},{3,4},{4,5},{5,6},{6,7},{7,8},{8,9},{9,10},{10,1... | collective-permute-start | bytes 786440 | tf_op jit(solution)/shard_map/ppermute | solution.py:253
  39.5 10.0 %copy-start.3 = (bf16[4,512,512]{2,1,0:T(8,128)(2,1)S(1)}, bf16[4,512,512]{2,1,0:T(8,128)(2,1)}, u32[]{:S(2)}) copy-start(bf16[4,512,512]{2,1,0:T(8,128)(2,1)} %mixing.3) | copy-start | bytes 6291460
  39.6 10.0 %collective-permute-start.8 = (bf16[16,16,512]{2,1,0:T(8,128)(2,1)S(1)}, bf16[16,16,512]{2,1,0:T(8,128)(2,1)S(1)}, u32[]{:S(2)}, u32[]{:S(2)}) collective-permute-start(bf16[16,16,512]{2,1,0:T(8,128)(2,1)S(1)} %get-tuple-element.21), channel_id=1, source_target_pairs={{0,15},{1,0},{2,1},{3,2},{4,3},{5,4},{6,5},{7,6},{8,7},{9,8},{10,9... | collective-permute-start | bytes 786440 | tf_op jit(solution)/shard_map/ppermute | solution.py:253
  61.3 9.1 %collective-permute-start.10 = (bf16[64,512]{1,0:T(8,128)(2,1)S(1)}, bf16[64,512]{1,0:T(8,128)(2,1)S(1)}, u32[]{:S(2)}, u32[]{:S(2)}) collective-permute-start(bf16[64,512]{1,0:T(8,128)(2,1)S(1)} %chip_sum.1.one), channel_id=1, source_target_pairs={{0,4},{1,5},{2,6},{3,7},{4,0},{5,1},{6,2},{7,3},{8,12},{9,13},{10,... | collective-permute-start | bytes 196616 | tf_op jit(solution)/shard_map/ppermute | solution.py:257
  61.4 9.0 %collective-permute-start.11 = (bf16[64,512]{1,0:T(8,128)(2,1)S(1)}, bf16[64,512]{1,0:T(8,128)(2,1)S(1)}, u32[]{:S(2)}, u32[]{:S(2)}) collective-permute-start(bf16[64,512]{1,0:T(8,128)(2,1)S(1)} %chip_sum.1.one), channel_id=1, source_target_pairs={{0,6},{1,7},{2,4},{3,5},{4,2},{5,3},{6,0},{7,1},{8,14},{9,15},{10,... | collective-permute-start | bytes 196616 | tf_op jit(solution)/shard_map/ppermute | solution.py:257
  61.5 9.9 %collective-permute-start.9 = (bf16[64,512]{1,0:T(8,128)(2,1)S(1)}, bf16[64,512]{1,0:T(8,128)(2,1)S(1)}, u32[]{:S(2)}, u32[]{:S(2)}) collective-permute-start(bf16[64,512]{1,0:T(8,128)(2,1)S(1)} %chip_sum.1.one), channel_id=1, source_target_pairs={{0,2},{1,3},{2,0},{3,1},{4,6},{5,7},{6,4},{7,5},{8,10},{9,11},{10,... | collective-permute-start | bytes 196616 | tf_op jit(solution)/shard_map/ppermute | solution.py:257
  71.4 4.4 %collective-permute-start.12 = (bf16[64,512]{1,0:T(8,128)(2,1)S(1)}, bf16[64,512]{1,0:T(8,128)(2,1)S(1)}, u32[]{:S(2)}, u32[]{:S(2)}) collective-permute-start(bf16[64,512]{1,0:T(8,128)(2,1)S(1)} %four_sum.1.own), channel_id=1, source_target_pairs={{0,1},{1,0},{2,3},{3,2},{4,5},{5,4},{6,7},{7,6},{8,9},{9,8},{10,11... | collective-permute-start | bytes 196616 | tf_op jit(solution)/shard_map/ppermute | solution.py:257
  71.6 4.3 %collective-permute-start.13 = (bf16[64,512]{1,0:T(8,128)(2,1)S(1)}, bf16[64,512]{1,0:T(8,128)(2,1)S(1)}, u32[]{:S(2)}, u32[]{:S(2)}) collective-permute-start(bf16[64,512]{1,0:T(8,128)(2,1)S(1)} %four_sum.1.own), channel_id=1, source_target_pairs={{0,8},{8,0},{1,9},{9,1},{2,10},{10,2},{3,11},{11,3},{4,12},{12,4},... | collective-permute-start | bytes 196616 | tf_op jit(solution)/shard_map/ppermute | solution.py:257
  73.1 5.2 %collective-permute-start.14 = (bf16[64,512]{1,0:T(8,128)(2,1)S(1)}, bf16[64,512]{1,0:T(8,128)(2,1)S(1)}, u32[]{:S(2)}, u32[]{:S(2)}) collective-permute-start(bf16[64,512]{1,0:T(8,128)(2,1)S(1)} %four_sum.1.own), channel_id=1, source_target_pairs={{0,9},{1,8},{2,11},{3,10},{4,13},{5,12},{6,15},{7,14},{8,1},{9,0},... | collective-permute-start | bytes 196616 | tf_op jit(solution)/shard_map/ppermute | solution.py:257

commit v4 on v3

--- a/solution.py
+++ b/solution.py
@@ -10,6 +10,8 @@
 from jax.sharding import PartitionSpec as P
 
 HL = 2
+MIXED_COST = 60_000_000_000
+FILTER_COST = 20_000_000_000
 WL = 16
 SPAN = 2 * HL + 1
 F32 = jnp.float32
@@ -115,7 +117,9 @@
     lax.fori_loop(0, rows, one_row, 0, unroll=2)
 
 
-def rims_kernel(place, after, inner, outer, to_east, to_west):
+def rims_kernel(place, after, inner, outer, cot, to_east, to_west, cot_to_east, cot_to_west):
+    cot_to_east[...] = cot[:, cot.shape[1] - WL :]
+    cot_to_west[...] = cot[:, :WL]
     cols = inner.shape[2]
     odd = place[3] == 1
     north = jnp.where(odd, inner[...], outer[...])
@@ -179,7 +183,7 @@
             send[2 * pair + basis // per, lines] = other[pair]
 
 
-def output_kernel(filt, mixing, out, token):
+def output_kernel(ready_w, ready_e, filt, mixing, out, token):
     token[...] = jnp.zeros_like(token)
     basis_count, rows, cols, channels = filt.shape
     total = None
@@ -318,11 +322,12 @@
         pairs += [(low, low + 1), (low + 1, low)]
     outer = lax.ppermute(outer, LAT, pairs)
     rim = shaped((2, 2, HL, WL, channels), BF16)
-    rim_to_east, rim_to_west = call(
+    side = shaped((rows, WL, channels), BF16)
+    rim_to_east, rim_to_west, cot_to_east, cot_to_west = call(
         rims_kernel,
-        (rim, rim),
-        (place, fwd_taps, inner, outer),
-        [SMEM] + [VMEM] * 3,
+        (rim, rim, side, side),
+        (place, fwd_taps, inner, outer, cotangent),
+        [SMEM] + [VMEM] * 4,
         "rims",
         moved=1_000_000,
     )
@@ -340,20 +345,20 @@
         [SMEM] * 2 + [VMEM] * 9,
         "filtering",
         [pltpu.VMEM((rows + 2 * HL, wide, channels), BF16)],
-        flops=2_000_000_000,
+        flops=FILTER_COST,
         moved=8_000_000,
     )
     recv = swap(send, "core", 2, 1)
-    cot_west = shift(cotangent[:, cols - WL :], LON, lons, 1)
-    cot_east = shift(cotangent[:, :WL], LON, lons, -1)
+    cot_west = shift(cot_to_east, LON, lons, 1)
+    cot_east = shift(cot_to_west, LON, lons, -1)
     token = shaped((8, 128), F32)
     output, token_one = call(
         output_kernel,
         (shaped((rows, cols, channels), BF16), token),
-        (filtered, mixing),
-        [VMEM] * 2,
+        (cot_west, cot_east, filtered, mixing),
+        [VMEM] * 4,
         "mixed",
-        flops=1_500_000_000,
+        flops=MIXED_COST,
         moved=4_500_000,
     )
     summed = call(

time: 79.9 us -> 78 us (0.976); the launches traced: 79.5 us -> 76.8 us
  waiting for transfers between devices: 18.2 us -> 15.3 us
    all_to_all x1, starting transfers between devices: 9.19 us -> 7.24 us  [local(): parts = lax.all_to_all(summed, ('y', 'xh', 'xl'), 0, 0)]
    ppermute x8, waiting for transfers between devices: 7.02 us -> 5.24 us  [swap(): return lax.ppermute(cells, axis, [(i, i ^ mask) for i in range(count)])]
    ppermute x8, starting transfers between devices: 13.3 us -> 14.4 us  [swap(): return lax.ppermute(cells, axis, [(i, i ^ mask) for i in range(count)])]
    ppermute x6, waiting for transfers between devices: 4.74 us -> 3.72 us  [shift(): lax.ppermute(cells, axis, [(i, (i + step) % count) for i in range(count)])]
    ppermute x6, starting transfers between devices: 14.4 us -> 15.2 us  [shift(): lax.ppermute(cells, axis, [(i, (i + step) % count) for i in range(count)])]
  transfers between devices with their start and end apart: 16 -> 16, of which waited for: 9 -> 8; matrix products, arithmetic and copies ran while one was open for 1% -> 1% of each run, Pallas kernels for 18% -> 23%
where the time goes in v4:
time: 78 us; the launch traced here: 76.8 us
  starting transfers between devices  37.5 us (48%)
  Pallas kernels  20.1 us (26%)
  waiting for transfers between devices  15.3 us (20%)
  local copies, waits for them, and re-layouts  2.96 us (4%)
  between operations  0.83 us (1%)
    pallas_call x10, Pallas kernels, call(): pl.pallas_call(kernel, out_shape=outs, in_specs=specs, out_specs=jax.tree...  20.1 us
    ppermute x6, starting transfers between devices, shift(): lax.ppermute(cells, axis, [(i, (i + step) % count) for i in range(count)])  15.2 us
    ppermute x8, starting transfers between devices, swap(): return lax.ppermute(cells, axis, [(i, i ^ mask) for i in range(count)])  14.4 us
    all_to_all x1, starting transfers between devices, local(): parts = lax.all_to_all(summed, ('y', 'xh', 'xl'), 0, 0)  7.24 us
    all_to_all x1, waiting for transfers between devices, local(): parts = lax.all_to_all(summed, ('y', 'xh', 'xl'), 0, 0)  6.33 us
    ppermute x8, waiting for transfers between devices, swap(): return lax.ppermute(cells, axis, [(i, i ^ mask) for i in range(count)])  5.24 us
    ppermute x6, waiting for transfers between devices, shift(): lax.ppermute(cells, axis, [(i, (i + step) % count) for i in range(count)])  3.72 us
    another operation x2, local copies, waits for them, and re-layouts, local(): top = jnp.stack([cells[:HL] for cells in both])  1.78 us
  transfers between devices with their start and end apart: 16, of which 8 were waited for; matrix products, arithmetic and copies ran while one was open for 1% of the time, Pallas kernels for 23%

profile of v4, /device:TPU:2, one launch (start us, length us, event | category | flops | bytes accessed | tf_op | source)
XLA Modules:
  0.0 76.8 jit_solution(15666706797448302962)
XLA Ops:
  0.6 0.0 copy-start.6
  0.6 0.0 copy-start.5
  0.7 0.0 copy-start.4
  0.7 0.9 %slice_bitcast_fusion.3 = (bf16[1,2,32,512]{3,2,1,0:T(8,128)(2,1)S(1)}, bf16[1,2,32,512]{3,2,1,0:T(8,128)(2,1)S(1)}) fusion(bf16[16,32,512]{2,1,0:T(8,128)(2,1)} %center.2), kind=kLoop, calls=%fused_computation.7 | loop fusion | bytes 262144 | tf_op jit(solution)/shard_map/stack | solution.py:298
  1.6 0.9 %slice_bitcast_fusion.2 = (bf16[1,2,32,512]{3,2,1,0:T(8,128)(2,1)S(1)}, bf16[1,2,32,512]{3,2,1,0:T(8,128)(2,1)S(1)}) fusion(bf16[16,32,512]{2,1,0:T(8,128)(2,1)} %center.3), kind=kLoop, calls=%fused_computation.6 | loop fusion | bytes 262144 | tf_op jit(solution)/shard_map/stack | solution.py:298
  2.5 0.7 collective-permute-start.1
  3.2 3.6 %collective-permute-start = (bf16[2,2,32,512]{3,2,1,0:T(8,128)(2,1)S(1)}, bf16[2,2,32,512]{3,2,1,0:T(8,128)(2,1)S(1)}, u32[]{:S(2)}, u32[]{:S(2)}) collective-permute-start(bf16[2,2,32,512]{3,2,1,0:T(8,128)(2,1)S(1)} %get-tuple-element.32), channel_id=1, source_target_pairs={{0,16},{16,0},{32,48},{48,32},{64,80},{80,64},{96,112},{112,96},{1... | collective-permute-start | bytes 393224 | tf_op jit(solution)/shard_map/ppermute | solution.py:261
  6.7 1.1 %fusion = (bf16[16,16,512]{2,1,0:T(8,128)(2,1)S(1)}, bf16[16,16,512]{2,1,0:T(8,128)(2,1)S(1)}) fusion(bf16[16,32,512]{2,1,0:T(8,128)(2,1)} %center.2), kind=kLoop, calls=%fused_computation.8 | loop fusion | bytes 1048576 | tf_op jit(solution)/shard_map/slice | solution.py:303
  7.8 0.0 copy-start.1
  7.8 6.8 %collective-permute-start.5 = (bf16[16,16,512]{2,1,0:T(8,128)(2,1)S(1)}, bf16[16,16,512]{2,1,0:T(8,128)(2,1)S(1)}, u32[]{:S(2)}, u32[]{:S(2)}) collective-permute-start(bf16[16,16,512]{2,1,0:T(8,128)(2,1)S(1)} %get-tuple-element.25), channel_id=1, source_target_pairs={{0,15},{1,0},{2,1},{3,2},{4,3},{5,4},{6,5},{7,6},{8,7},{9,8},{10,9... | collective-permute-start | bytes 786440 | tf_op jit(solution)/shard_map/ppermute | solution.py:257
  14.6 0.0 collective-permute-start.4
  14.6 0.1 stack.41.place
  14.7 0.0 copy-done.6
  14.7 0.0 copy-done.5
  14.7 0.0 copy-done.4
  14.7 0.0 copy-start
  14.7 2.2 %forward_taps.1.after.taps = bf16[16,128,256]{2,1,0:T(8,128)(2,1)S(1)} custom-call(s32[6]{0:T(128)S(1)} %stack.41.place, bf16[4,4,4,256]{3,2,1,0:T(4,128)(2,1)S(1)} %bitcast.16, s32[4,256]{1,0:T(4,128)S(1)} %bitcast.18, s32[4,256]{1,0:T(4,128)S(1)} %bitcast.21), custom_call_target="tpu_custom_call" | custom-call | flops 1000000000 | bytes 1000000 | tf_op jit(solution)/shard_map/forward_taps/pallas_call | solution.py:265
  16.9 0.0 collective-permute-done.1.outer
  17.0 0.0 collective-permute-done.inner
  17.0 0.0 copy-done.1
  17.0 0.6 rims.1
  17.6 0.1 collective-permute-start.6
  17.7 4.2 %collective-permute-start.7 = (bf16[2,2,2,16,512]{4,3,2,1,0:T(8,128)(2,1)S(1)}, bf16[2,2,2,16,512]{4,3,2,1,0:T(8,128)(2,1)S(1)}, u32[]{:S(2)}, u32[]{:S(2)}) collective-permute-start(bf16[2,2,2,16,512]{4,3,2,1,0:T(8,128)(2,1)S(1)} %get-tuple-element.17), channel_id=1, source_target_pairs={{0,15},{1,0},{2,1},{3,2},{4,3},{5,4},{6,5},{7,6},{8,7},{9,8},{10,9... | collective-permute-start | bytes 393224 | tf_op jit(solution)/shard_map/ppermute | solution.py:257
  21.9 0.0 collective-permute-start.2
  21.9 0.0 collective-permute-done.5.east
  21.9 0.0 copy-start.2
  21.9 4.1 %collective-permute-start.3 = (bf16[16,16,512]{2,1,0:T(8,128)(2,1)S(1)}, bf16[16,16,512]{2,1,0:T(8,128)(2,1)S(1)}, u32[]{:S(2)}, u32[]{:S(2)}) collective-permute-start(bf16[16,16,512]{2,1,0:T(8,128)(2,1)S(1)} %get-tuple-element.15), channel_id=1, source_target_pairs={{0,15},{1,0},{2,1},{3,2},{4,3},{5,4},{6,5},{7,6},{8,7},{9,8},{10,9... | collective-permute-start | bytes 786440 | tf_op jit(solution)/shard_map/ppermute | solution.py:257
  26.0 0.0 collective-permute-done.4.west
  26.0 2.7 %collective-permute-done.6.rims_w = bf16[2,2,2,16,512]{4,3,2,1,0:T(8,128)(2,1)S(1)} collective-permute-done((bf16[2,2,2,16,512]{4,3,2,1,0:T(8,128)(2,1)S(1)}, bf16[2,2,2,16,512]{4,3,2,1,0:T(8,128)(2,1)S(1)}, u32[]{:S(2)}, u32[]{:S(2)}) %collective-permute-start.6) | collective-permute-done | bytes 131104 | tf_op jit(solution)/shard_map/ppermute | solution.py:257
  28.7 0.0 collective-permute-done.7.rims_e
  28.7 0.0 copy-done
  28.7 3.2 %filtering.1 = (f32[16,64,512]{2,1,0:T(8,128)S(1)}, bf16[16,64,512]{2,1,0:T(8,128)(2,1)S(1)}, bf16[4,16,32,512]{3,2,1,0:T(8,128)(2,1)S(1)}) custom-call(s32[6]{0:T(128)S(1)} %stack.41.place, s32[4,256]{1,0:T(4,128)S(1)} %bitcast.19, bf16[16,128,256]{2,1,0:T(8,128)(2,1)S(1)} %forward_taps.1.after.taps, bf16[16,32,512]{2,1,0:T(8,128)(2,1)S(1)} %copy-done, ...), custom_call_target="tpu_custom_call" | custom-call | flops 20000000000 | bytes 8000000 | tf_op jit(solution)/shard_map/filtering/pallas_call | solution.py:265
  32.0 0.1 collective-permute-start.8
  32.1 1.0 %collective-permute-done.2.ready_w.west = bf16[16,16,512]{2,1,0:T(8,128)(2,1)S(1)} collective-permute-done((bf16[16,16,512]{2,1,0:T(8,128)(2,1)S(1)}, bf16[16,16,512]{2,1,0:T(8,128)(2,1)S(1)}, u32[]{:S(2)}, u32[]{:S(2)}) %collective-permute-start.2) | collective-permute-done | bytes 262176 | tf_op jit(solution)/shard_map/ppermute | solution.py:257
  33.1 0.0 collective-permute-done.3.ready_e.east
  33.1 0.0 copy-done.2
  33.1 2.1 %mixed.1 = (bf16[16,32,512]{2,1,0:T(8,128)(2,1)}, f32[8,128]{1,0:T(8,128)S(1)}) custom-call(bf16[16,16,512]{2,1,0:T(8,128)(2,1)S(1)} %collective-permute-done.2.ready_w.west, bf16[16,16,512]{2,1,0:T(8,128)(2,1)S(1)} %collective-permute-done.3.ready_e.east, bf16[4,16,32,512]{3,2,1,0:T(8,128)(2,1)S(1)} %get-tuple-element.18.filt, ...), custom_call_target="tpu_custom_call" | custom-call | flops 60000002048 | bytes 4500000 | tf_op jit(solution)/shard_map/mixed/pallas_call | solution.py:265
  35.2 0.0 collective-permute-done.8.recv
  35.2 1.2 %pair_sum.1.after = bf16[16,64,512]{2,1,0:T(8,128)(2,1)} custom-call(f32[8,128]{1,0:T(8,128)S(1)} %get-tuple-element.20.after, f32[16,64,512]{2,1,0:T(8,128)S(1)} %get-tuple-element.21.keep, bf16[16,64,512]{2,1,0:T(8,128)(2,1)S(1)} %collective-permute-done.8.recv), custom_call_target="tpu_custom_call" | custom-call | flops 524288 | bytes 4194304 | tf_op jit(solution)/shard_map/pair_sum/pallas_call | solution.py:265
  36.4 7.2 %all-to-all-start = ((bf16[16,64,512]{2,1,0:T(8,128)(2,1)}), bf16[16,64,512]{2,1,0:T(8,128)(2,1)S(1)}, u32[]{:S(2)}, u32[]{:S(2)}) async-start(bf16[16,64,512]{2,1,0:T(8,128)(2,1)} %pair_sum.1.after), calls=%async_computation | async-start | bytes 2097152 | tf_op jit(solution)/shard_map/all_to_all | solution.py:373
  43.6 0.0 copy-start.3
  43.6 4.2 %adjoint_taps.1.taps = bf16[16,128,320]{2,1,0:T(8,128)(2,1)S(1)} custom-call(s32[6]{0:T(128)S(1)} %stack.41.place, bf16[16,64,512]{2,1,0:T(8,128)(2,1)} %pair_sum.1.after, bf16[4,4,4,256]{3,2,1,0:T(4,128)(2,1)S(1)} %bitcast.17, s32[4,256]{1,0:T(4,128)S(1)} %bitcast.20, s32[4,256]{1,0:T(4,128)S(1)} %bitcast.22), custom_call_target="tpu_custom_call" | custom-call | flops 2000000000 | bytes 2000000 | tf_op jit(solution)/shard_map/adjoint_taps/pallas_call | solution.py:265
  47.8 0.0 copy-done.3
  47.8 5.2 %adjoint.1 = (bf16[16,32,512]{2,1,0:T(8,128)(2,1)}, f32[8,128]{1,0:T(8,128)S(1)}) custom-call(s32[6]{0:T(128)S(1)} %stack.41.place, bf16[16,64,512]{2,1,0:T(8,128)(2,1)} %pair_sum.1.after, bf16[16,128,320]{2,1,0:T(8,128)(2,1)S(1)} %adjoint_taps.1.taps, bf16[16,32,512]{2,1,0:T(8,128)(2,1)S(1)} %copy-done.1, ...), custom_call_target="tpu_custom_call" | custom-call | flops 3000000000 | bytes 6000000 | tf_op jit(solution)/shard_map/adjoint/pallas_call | solution.py:265
  53.0 6.3 %all-to-all-done.parts = bf16[16,64,512]{2,1,0:T(8,128)(2,1)S(1)} async-done(((bf16[16,64,512]{2,1,0:T(8,128)(2,1)}), bf16[16,64,512]{2,1,0:T(8,128)(2,1)S(1)}, u32[]{:S(2)}, u32[]{:S(2)}) %all-to-all-start) | async-done | bytes 1048608 | tf_op jit(solution)/shard_map/all_to_all | solution.py:373
  59.3 0.1 chip_sum.1.one
  59.5 0.1 collective-permute-start.11
  59.6 0.5 collective-permute-start.10
  60.1 6.0 %collective-permute-start.9 = (bf16[64,512]{1,0:T(8,128)(2,1)S(1)}, bf16[64,512]{1,0:T(8,128)(2,1)S(1)}, u32[]{:S(2)}, u32[]{:S(2)}) collective-permute-start(bf16[64,512]{1,0:T(8,128)(2,1)S(1)} %chip_sum.1.one), channel_id=1, source_target_pairs={{0,2},{1,3},{2,0},{3,1},{4,6},{5,7},{6,4},{7,5},{8,10},{9,11},{10,... | collective-permute-start | bytes 196616 | tf_op jit(solution)/shard_map/ppermute | solution.py:261
  66.1 0.0 collective-permute-done.11.four
  66.1 1.9 %collective-permute-done.10.three = bf16[64,512]{1,0:T(8,128)(2,1)S(1)} collective-permute-done((bf16[64,512]{1,0:T(8,128)(2,1)S(1)}, bf16[64,512]{1,0:T(8,128)(2,1)S(1)}, u32[]{:S(2)}, u32[]{:S(2)}) %collective-permute-start.10) | collective-permute-done | bytes 65568 | tf_op jit(solution)/shard_map/ppermute | solution.py:261
  68.0 0.4 collective-permute-done.9.two
  68.4 2.4 %collective-permute-start.14 = (bf16[64,512]{1,0:T(8,128)(2,1)S(1)}, bf16[64,512]{1,0:T(8,128)(2,1)S(1)}, u32[]{:S(2)}, u32[]{:S(2)}) collective-permute-start(bf16[64,512]{1,0:T(8,128)(2,1)S(1)} %four_sum.1.own), channel_id=1, source_target_pairs={{0,9},{1,8},{2,11},{3,10},{4,13},{5,12},{6,15},{7,14},{8,1},{9,0},... | collective-permute-start | bytes 196616 | tf_op jit(solution)/shard_map/ppermute | solution.py:261
  70.8 0.4 collective-permute-start.13
  71.2 1.4 %collective-permute-start.12 = (bf16[64,512]{1,0:T(8,128)(2,1)S(1)}, bf16[64,512]{1,0:T(8,128)(2,1)S(1)}, u32[]{:S(2)}, u32[]{:S(2)}) collective-permute-start(bf16[64,512]{1,0:T(8,128)(2,1)S(1)} %four_sum.1.own), channel_id=1, source_target_pairs={{0,1},{1,0},{2,3},{3,2},{4,5},{5,4},{6,7},{7,6},{8,9},{9,8},{10,11... | collective-permute-start | bytes 196616 | tf_op jit(solution)/shard_map/ppermute | solution.py:261
  72.6 1.1 %collective-permute-done.14.by_both = bf16[64,512]{1,0:T(8,128)(2,1)S(1)} collective-permute-done((bf16[64,512]{1,0:T(8,128)(2,1)S(1)}, bf16[64,512]{1,0:T(8,128)(2,1)S(1)}, u32[]{:S(2)}, u32[]{:S(2)}) %collective-permute-start.14) | collective-permute-done | bytes 65568 | tf_op jit(solution)/shard_map/ppermute | solution.py:261
  73.7 1.4 %collective-permute-done.13.by_x = bf16[64,512]{1,0:T(8,128)(2,1)S(1)} collective-permute-done((bf16[64,512]{1,0:T(8,128)(2,1)S(1)}, bf16[64,512]{1,0:T(8,128)(2,1)S(1)}, u32[]{:S(2)}, u32[]{:S(2)}) %collective-permute-start.13) | collective-permute-done | bytes 65568 | tf_op jit(solution)/shard_map/ppermute | solution.py:261
  75.1 0.4 collective-permute-done.12.by_z
  75.5 1.3 %last_sum.1 = f32[4,32,512]{2,1,0:T(8,128)} custom-call(s32[6]{0:T(128)S(1)} %stack.41.place, bf16[64,512]{1,0:T(8,128)(2,1)S(1)} %four_sum.1.own, bf16[64,512]{1,0:T(8,128)(2,1)S(1)} %collective-permute-done.12.by_z, bf16[64,512]{1,0:T(8,128)(2,1)S(1)} %collective-permute-done.13.by_x, bf16[64,512]{1,0:T(8,128)(2,1)S(1)} %collective-permute-done.14.by_both), custom_call_target="tpu_custom_call" | custom-call | flops 131072 | bytes 524288 | tf_op jit(solution)/shard_map/last_sum/pallas_call | solution.py:265
  (2 shorter events, 0.1 us)
Async XLA Ops:
  0.6 14.1 %copy-start.6 = (s32[256,4]{0,1:T(4,128)S(1)}, s32[256,4]{0,1:T(4,128)}, u32[]{:S(2)}) copy-start(s32[256,4]{0,1:T(4,128)} %param.9) | copy-start | bytes 12292
  0.6 14.1 %copy-start.5 = (s32[256,4]{0,1:T(4,128)S(1)}, s32[256,4]{0,1:T(4,128)}, u32[]{:S(2)}) copy-start(s32[256,4]{0,1:T(4,128)} %param.8) | copy-start | bytes 12292
  0.7 14.1 %copy-start.4 = (bf16[4,256,4,4]{1,3,2,0:T(4,128)(2,1)S(1)}, bf16[4,256,4,4]{1,3,2,0:T(4,128)(2,1)}, u32[]{:S(2)}) copy-start(bf16[4,256,4,4]{1,3,2,0:T(4,128)(2,1)} %param.7) | copy-start | bytes 98308
  2.5 14.5 %collective-permute-start.1 = (bf16[2,2,32,512]{3,2,1,0:T(8,128)(2,1)S(1)}, bf16[2,2,32,512]{3,2,1,0:T(8,128)(2,1)S(1)}, u32[]{:S(2)}, u32[]{:S(2)}) collective-permute-start(bf16[2,2,32,512]{3,2,1,0:T(8,128)(2,1)S(1)} %get-tuple-element.31), channel_id=1, source_target_pairs={{0,0},{240,240},{16,32},{32,16},{48,64},{64,48},{80,96},{96,80},{1... | collective-permute-start | bytes 393224 | tf_op jit(solution)/shard_map/ppermute | solution.py:323
  3.2 13.8 %collective-permute-start = (bf16[2,2,32,512]{3,2,1,0:T(8,128)(2,1)S(1)}, bf16[2,2,32,512]{3,2,1,0:T(8,128)(2,1)S(1)}, u32[]{:S(2)}, u32[]{:S(2)}) collective-permute-start(bf16[2,2,32,512]{3,2,1,0:T(8,128)(2,1)S(1)} %get-tuple-element.32), channel_id=1, source_target_pairs={{0,16},{16,0},{32,48},{48,32},{64,80},{80,64},{96,112},{112,96},{1... | collective-permute-start | bytes 393224 | tf_op jit(solution)/shard_map/ppermute | solution.py:261
  7.8 9.2 %copy-start.1 = (bf16[16,32,512]{2,1,0:T(8,128)(2,1)S(1)}, bf16[16,32,512]{2,1,0:T(8,128)(2,1)}, u32[]{:S(2)}) copy-start(bf16[16,32,512]{2,1,0:T(8,128)(2,1)} %center.3) | copy-start | bytes 1572868
  7.8 14.1 %collective-permute-start.5 = (bf16[16,16,512]{2,1,0:T(8,128)(2,1)S(1)}, bf16[16,16,512]{2,1,0:T(8,128)(2,1)S(1)}, u32[]{:S(2)}, u32[]{:S(2)}) collective-permute-start(bf16[16,16,512]{2,1,0:T(8,128)(2,1)S(1)} %get-tuple-element.25), channel_id=1, source_target_pairs={{0,15},{1,0},{2,1},{3,2},{4,3},{5,4},{6,5},{7,6},{8,7},{9,8},{10,9... | collective-permute-start | bytes 786440 | tf_op jit(solution)/shard_map/ppermute | solution.py:257
  14.6 11.4 %collective-permute-start.4 = (bf16[16,16,512]{2,1,0:T(8,128)(2,1)S(1)}, bf16[16,16,512]{2,1,0:T(8,128)(2,1)S(1)}, u32[]{:S(2)}, u32[]{:S(2)}) collective-permute-start(bf16[16,16,512]{2,1,0:T(8,128)(2,1)S(1)} %get-tuple-element.26), channel_id=1, source_target_pairs={{0,1},{1,2},{2,3},{3,4},{4,5},{5,6},{6,7},{7,8},{8,9},{9,10},{10,1... | collective-permute-start | bytes 786440 | tf_op jit(solution)/shard_map/ppermute | solution.py:257
  14.7 14.0 %copy-start = (bf16[16,32,512]{2,1,0:T(8,128)(2,1)S(1)}, bf16[16,32,512]{2,1,0:T(8,128)(2,1)}, u32[]{:S(2)}) copy-start(bf16[16,32,512]{2,1,0:T(8,128)(2,1)} %center.2) | copy-start | bytes 1572868
  17.6 11.2 %collective-permute-start.6 = (bf16[2,2,2,16,512]{4,3,2,1,0:T(8,128)(2,1)S(1)}, bf16[2,2,2,16,512]{4,3,2,1,0:T(8,128)(2,1)S(1)}, u32[]{:S(2)}, u32[]{:S(2)}) collective-permute-start(bf16[2,2,2,16,512]{4,3,2,1,0:T(8,128)(2,1)S(1)} %get-tuple-element.16), channel_id=1, source_target_pairs={{0,1},{1,2},{2,3},{3,4},{4,5},{5,6},{6,7},{7,8},{8,9},{9,10},{10,1... | collective-permute-start | bytes 393224 | tf_op jit(solution)/shard_map/ppermute | solution.py:257
  17.7 11.1 %collective-permute-start.7 = (bf16[2,2,2,16,512]{4,3,2,1,0:T(8,128)(2,1)S(1)}, bf16[2,2,2,16,512]{4,3,2,1,0:T(8,128)(2,1)S(1)}, u32[]{:S(2)}, u32[]{:S(2)}) collective-permute-start(bf16[2,2,2,16,512]{4,3,2,1,0:T(8,128)(2,1)S(1)} %get-tuple-element.17), channel_id=1, source_target_pairs={{0,15},{1,0},{2,1},{3,2},{4,3},{5,4},{6,5},{7,6},{8,7},{9,8},{10,9... | collective-permute-start | bytes 393224 | tf_op jit(solution)/shard_map/ppermute | solution.py:257
  21.9 11.2 %collective-permute-start.2 = (bf16[16,16,512]{2,1,0:T(8,128)(2,1)S(1)}, bf16[16,16,512]{2,1,0:T(8,128)(2,1)S(1)}, u32[]{:S(2)}, u32[]{:S(2)}) collective-permute-start(bf16[16,16,512]{2,1,0:T(8,128)(2,1)S(1)} %get-tuple-element.14), channel_id=1, source_target_pairs={{0,1},{1,2},{2,3},{3,4},{4,5},{5,6},{6,7},{7,8},{8,9},{9,10},{10,1... | collective-permute-start | bytes 786440 | tf_op jit(solution)/shard_map/ppermute | solution.py:257
  21.9 11.2 %copy-start.2 = (bf16[4,512,512]{2,1,0:T(8,128)(2,1)S(1)}, bf16[4,512,512]{2,1,0:T(8,128)(2,1)}, u32[]{:S(2)}) copy-start(bf16[4,512,512]{2,1,0:T(8,128)(2,1)} %mixing.3) | copy-start | bytes 6291460
  21.9 11.2 %collective-permute-start.3 = (bf16[16,16,512]{2,1,0:T(8,128)(2,1)S(1)}, bf16[16,16,512]{2,1,0:T(8,128)(2,1)S(1)}, u32[]{:S(2)}, u32[]{:S(2)}) collective-permute-start(bf16[16,16,512]{2,1,0:T(8,128)(2,1)S(1)} %get-tuple-element.15), channel_id=1, source_target_pairs={{0,15},{1,0},{2,1},{3,2},{4,3},{5,4},{6,5},{7,6},{8,7},{9,8},{10,9... | collective-permute-start | bytes 786440 | tf_op jit(solution)/shard_map/ppermute | solution.py:257
  32.0 3.2 %collective-permute-start.8 = (bf16[16,64,512]{2,1,0:T(8,128)(2,1)S(1)}, bf16[16,64,512]{2,1,0:T(8,128)(2,1)S(1)}, u32[]{:S(2)}, u32[]{:S(2)}) collective-permute-start(bf16[16,64,512]{2,1,0:T(8,128)(2,1)S(1)} %get-tuple-element.22), channel_id=1, source_target_pairs={{0,16},{16,0},{1,17},{17,1},{2,18},{18,2},{3,19},{19,3},{4,20},{20... | collective-permute-start | bytes 3145736 | tf_op jit(solution)/shard_map/ppermute | solution.py:261
  36.4 23.0 %all-to-all-start = ((bf16[16,64,512]{2,1,0:T(8,128)(2,1)}), bf16[16,64,512]{2,1,0:T(8,128)(2,1)S(1)}, u32[]{:S(2)}, u32[]{:S(2)}) async-start(bf16[16,64,512]{2,1,0:T(8,128)(2,1)} %pair_sum.1.after), calls=%async_computation | async-start | bytes 2097152 | tf_op jit(solution)/shard_map/all_to_all | solution.py:373
  43.6 4.2 %copy-start.3 = (bf16[4,512,512]{2,1,0:T(8,128)(2,1)S(1)}, bf16[4,512,512]{2,1,0:T(8,128)(2,1)}, u32[]{:S(2)}) copy-start(bf16[4,512,512]{2,1,0:T(8,128)(2,1)} %mixing.3) | copy-start | bytes 6291460
  59.5 6.6 %collective-permute-start.11 = (bf16[64,512]{1,0:T(8,128)(2,1)S(1)}, bf16[64,512]{1,0:T(8,128)(2,1)S(1)}, u32[]{:S(2)}, u32[]{:S(2)}) collective-permute-start(bf16[64,512]{1,0:T(8,128)(2,1)S(1)} %chip_sum.1.one), channel_id=1, source_target_pairs={{0,6},{1,7},{2,4},{3,5},{4,2},{5,3},{6,0},{7,1},{8,14},{9,15},{10,... | collective-permute-start | bytes 196616 | tf_op jit(solution)/shard_map/ppermute | solution.py:261
  59.6 8.4 %collective-permute-start.10 = (bf16[64,512]{1,0:T(8,128)(2,1)S(1)}, bf16[64,512]{1,0:T(8,128)(2,1)S(1)}, u32[]{:S(2)}, u32[]{:S(2)}) collective-permute-start(bf16[64,512]{1,0:T(8,128)(2,1)S(1)} %chip_sum.1.one), channel_id=1, source_target_pairs={{0,4},{1,5},{2,6},{3,7},{4,0},{5,1},{6,2},{7,3},{8,12},{9,13},{10,... | collective-permute-start | bytes 196616 | tf_op jit(solution)/shard_map/ppermute | solution.py:261
  60.1 8.3 %collective-permute-start.9 = (bf16[64,512]{1,0:T(8,128)(2,1)S(1)}, bf16[64,512]{1,0:T(8,128)(2,1)S(1)}, u32[]{:S(2)}, u32[]{:S(2)}) collective-permute-start(bf16[64,512]{1,0:T(8,128)(2,1)S(1)} %chip_sum.1.one), channel_id=1, source_target_pairs={{0,2},{1,3},{2,0},{3,1},{4,6},{5,7},{6,4},{7,5},{8,10},{9,11},{10,... | collective-permute-start | bytes 196616 | tf_op jit(solution)/shard_map/ppermute | solution.py:261
  68.4 5.3 %collective-permute-start.14 = (bf16[64,512]{1,0:T(8,128)(2,1)S(1)}, bf16[64,512]{1,0:T(8,128)(2,1)S(1)}, u32[]{:S(2)}, u32[]{:S(2)}) collective-permute-start(bf16[64,512]{1,0:T(8,128)(2,1)S(1)} %four_sum.1.own), channel_id=1, source_target_pairs={{0,9},{1,8},{2,11},{3,10},{4,13},{5,12},{6,15},{7,14},{8,1},{9,0},... | collective-permute-start | bytes 196616 | tf_op jit(solution)/shard_map/ppermute | solution.py:261
  70.8 4.3 %collective-permute-start.13 = (bf16[64,512]{1,0:T(8,128)(2,1)S(1)}, bf16[64,512]{1,0:T(8,128)(2,1)S(1)}, u32[]{:S(2)}, u32[]{:S(2)}) collective-permute-start(bf16[64,512]{1,0:T(8,128)(2,1)S(1)} %four_sum.1.own), channel_id=1, source_target_pairs={{0,8},{8,0},{1,9},{9,1},{2,10},{10,2},{3,11},{11,3},{4,12},{12,4},... | collective-permute-start | bytes 196616 | tf_op jit(solution)/shard_map/ppermute | solution.py:261
  71.2 4.3 %collective-permute-start.12 = (bf16[64,512]{1,0:T(8,128)(2,1)S(1)}, bf16[64,512]{1,0:T(8,128)(2,1)S(1)}, u32[]{:S(2)}, u32[]{:S(2)}) collective-permute-start(bf16[64,512]{1,0:T(8,128)(2,1)S(1)} %four_sum.1.own), channel_id=1, source_target_pairs={{0,1},{1,0},{2,3},{3,2},{4,5},{5,4},{6,7},{7,6},{8,9},{9,8},{10,11... | collective-permute-start | bytes 196616 | tf_op jit(solution)/shard_map/ppermute | solution.py:261

commit v5 on v4

--- a/solution.py
+++ b/solution.py
@@ -82,7 +82,7 @@
         store_bands(forward, row, jnp.concatenate(totals, axis=1), basis_count, count, taps)
         return carry
 
-    lax.fori_loop(0, rows, one_row, 0, unroll=4)
+    lax.fori_loop(0, rows, one_row, 0, unroll=16)
 
 
 def adjoint_taps_kernel(place, after, psi, lat, lon, adjoint, near_all, adj_wide):
@@ -114,7 +114,7 @@
         store_bands(adjoint, row, total, basis_count, count, taps)
         return carry
 
-    lax.fori_loop(0, rows, one_row, 0, unroll=2)
+    lax.fori_loop(0, rows, one_row, 0, unroll=4)
 
 
 def rims_kernel(place, after, inner, outer, cot, to_east, to_west, cot_to_east, cot_to_west):
@@ -164,7 +164,7 @@
         filt_out[:, row] = filtered.reshape(basis_count, cols, channels)
         return carry
 
-    lax.fori_loop(0, rows, one_row, 0, unroll=4)
+    lax.fori_loop(0, rows, one_row, 0, unroll=16)
     cot_flat = cot[...].reshape(rows * cols, channels)
     pairs = keep.shape[0] // 2
     share = channels // (2 * pairs)
@@ -183,7 +183,7 @@
             send[2 * pair + basis // per, lines] = other[pair]
 
 
-def output_kernel(ready_w, ready_e, filt, mixing, out, token):
+def output_kernel(filt, mixing, out, token):
     token[...] = jnp.zeros_like(token)
     basis_count, rows, cols, channels = filt.shape
     total = None
@@ -209,7 +209,7 @@
         spread[:, row] = pulled.reshape(basis_count, cols, channels)
         return carry
 
-    lax.fori_loop(0, rows, one_row, 0, unroll=4)
+    lax.fori_loop(0, rows, one_row, 0, unroll=16)
     total = None
     for basis in range(basis_count):
         part = lax.dot_general(
@@ -222,7 +222,7 @@
     out[...] = total.reshape(rows, cols, channels).astype(BF16)
 
 
-def pair_sum_kernel(after, keep, recv, out):
+def pair_sum_kernel(after, ready_w, ready_e, keep, recv, out):
     out[...] = (keep[...] + recv[...].astype(F32)).astype(BF16)
 
 
@@ -355,8 +355,8 @@
     output, token_one = call(
         output_kernel,
         (shaped((rows, cols, channels), BF16), token),
-        (cot_west, cot_east, filtered, mixing),
-        [VMEM] * 4,
+        (filtered, mixing),
+        [VMEM] * 2,
         "mixed",
         flops=MIXED_COST,
         moved=4_500_000,
@@ -364,8 +364,8 @@
     summed = call(
         pair_sum_kernel,
         shaped(keep.shape, BF16),
-        (token_one, keep, recv),
-        [VMEM] * 3,
+        (token_one, cot_west, cot_east, keep, recv),
+        [VMEM] * 5,
         "pair_sum",
         flops=keep.size,
         moved=keep.size * 8,

time: 78 us -> 76.8 us (0.985)
  Pallas kernels: 20.1 us -> 16.8 us
  waiting for transfers between devices: 15.3 us -> 18 us
    pallas_call x10, Pallas kernels: 20.1 us -> 16.8 us  [call(): pl.pallas_call(kernel, out_shape=outs, in_specs=specs, out_specs=jax.tree...]
    all_to_all x1, waiting for transfers between devices: 6.33 us -> 8.39 us  [local(): parts = lax.all_to_all(summed, ('y', 'xh', 'xl'), 0, 0)]
  transfers between devices with their start and end apart: 16 -> 16, of which waited for: 8 -> 10; matrix products, arithmetic and copies ran while one was open for 1% -> 2% of each run, Pallas kernels for 23% -> 19%
where the time goes in v5:
time: 76.8 us; the launch traced here: 75.8 us
  starting transfers between devices  37.1 us (48%)
  waiting for transfers between devices  18 us (23%)
  Pallas kernels  16.8 us (22%)
  local copies, waits for them, and re-layouts  2.96 us (4%)
  between operations  0.84 us (1%)
    pallas_call x10, Pallas kernels, call(): pl.pallas_call(kernel, out_shape=outs, in_specs=specs, out_specs=jax.tree...  16.8 us
    ppermute x6, starting transfers between devices, shift(): lax.ppermute(cells, axis, [(i, (i + step) % count) for i in range(count)])  15.2 us
    ppermute x8, starting transfers between devices, swap(): return lax.ppermute(cells, axis, [(i, i ^ mask) for i in range(count)])  14 us
    all_to_all x1, waiting for transfers between devices, local(): parts = lax.all_to_all(summed, ('y', 'xh', 'xl'), 0, 0)  8.39 us
    all_to_all x1, starting transfers between devices, local(): parts = lax.all_to_all(summed, ('y', 'xh', 'xl'), 0, 0)  7.25 us
    ppermute x8, waiting for transfers between devices, swap(): return lax.ppermute(cells, axis, [(i, i ^ mask) for i in range(count)])  6.01 us
    ppermute x6, waiting for transfers between devices, shift(): lax.ppermute(cells, axis, [(i, (i + step) % count) for i in range(count)])  3.61 us
    another operation x2, local copies, waits for them, and re-layouts, local(): top = jnp.stack([cells[:HL] for cells in both])  1.78 us
  transfers between devices with their start and end apart: 16, of which 10 were waited for; matrix products, arithmetic and copies ran while one was open for 2% of the time, Pallas kernels for 19%

profile of v5, /device:TPU:2, one launch (start us, length us, event | category | flops | bytes accessed | tf_op | source)
XLA Modules:
  0.0 75.8 jit_solution(6252801206895580327)
XLA Ops:
  0.6 0.0 copy-start.6
  0.6 0.0 copy-start.5
  0.7 0.0 copy-start.4
  0.7 0.9 %slice_bitcast_fusion.3 = (bf16[1,2,32,512]{3,2,1,0:T(8,128)(2,1)S(1)}, bf16[1,2,32,512]{3,2,1,0:T(8,128)(2,1)S(1)}) fusion(bf16[16,32,512]{2,1,0:T(8,128)(2,1)} %center.2), kind=kLoop, calls=%fused_computation.7 | loop fusion | bytes 262144 | tf_op jit(solution)/shard_map/stack | solution.py:298
  1.6 0.9 %slice_bitcast_fusion.2 = (bf16[1,2,32,512]{3,2,1,0:T(8,128)(2,1)S(1)}, bf16[1,2,32,512]{3,2,1,0:T(8,128)(2,1)S(1)}) fusion(bf16[16,32,512]{2,1,0:T(8,128)(2,1)} %center.3), kind=kLoop, calls=%fused_computation.6 | loop fusion | bytes 262144 | tf_op jit(solution)/shard_map/stack | solution.py:298
  2.5 0.7 collective-permute-start.3
  3.2 3.6 %collective-permute-start.2 = (bf16[2,2,32,512]{3,2,1,0:T(8,128)(2,1)S(1)}, bf16[2,2,32,512]{3,2,1,0:T(8,128)(2,1)S(1)}, u32[]{:S(2)}, u32[]{:S(2)}) collective-permute-start(bf16[2,2,32,512]{3,2,1,0:T(8,128)(2,1)S(1)} %get-tuple-element.32), channel_id=1, source_target_pairs={{0,16},{16,0},{32,48},{48,32},{64,80},{80,64},{96,112},{112,96},{1... | collective-permute-start | bytes 393224 | tf_op jit(solution)/shard_map/ppermute | solution.py:261
  6.7 1.1 %fusion = (bf16[16,16,512]{2,1,0:T(8,128)(2,1)S(1)}, bf16[16,16,512]{2,1,0:T(8,128)(2,1)S(1)}) fusion(bf16[16,32,512]{2,1,0:T(8,128)(2,1)} %center.2), kind=kLoop, calls=%fused_computation.8 | loop fusion | bytes 1048576 | tf_op jit(solution)/shard_map/slice | solution.py:303
  7.8 0.0 copy-start.1
  7.8 6.8 %collective-permute-start.1 = (bf16[16,16,512]{2,1,0:T(8,128)(2,1)S(1)}, bf16[16,16,512]{2,1,0:T(8,128)(2,1)S(1)}, u32[]{:S(2)}, u32[]{:S(2)}) collective-permute-start(bf16[16,16,512]{2,1,0:T(8,128)(2,1)S(1)} %get-tuple-element.29), channel_id=1, source_target_pairs={{0,15},{1,0},{2,1},{3,2},{4,3},{5,4},{6,5},{7,6},{8,7},{9,8},{10,9... | collective-permute-start | bytes 786440 | tf_op jit(solution)/shard_map/ppermute | solution.py:257
  14.6 0.0 collective-permute-start
  14.6 0.1 stack.41.place
  14.7 0.0 copy-done.6
  14.7 0.0 copy-done.5
  14.7 0.0 copy-done.4
  14.7 0.0 copy-start
  14.7 1.3 %forward_taps.1.after.taps = bf16[16,128,256]{2,1,0:T(8,128)(2,1)S(1)} custom-call(s32[6]{0:T(128)S(1)} %stack.41.place, bf16[4,4,4,256]{3,2,1,0:T(4,128)(2,1)S(1)} %bitcast.16, s32[4,256]{1,0:T(4,128)S(1)} %bitcast.18, s32[4,256]{1,0:T(4,128)S(1)} %bitcast.21), custom_call_target="tpu_custom_call" | custom-call | flops 1000000000 | bytes 1000000 | tf_op jit(solution)/shard_map/forward_taps/pallas_call | solution.py:265
  16.1 0.0 collective-permute-done.3.outer
  16.1 0.0 collective-permute-done.2.inner
  16.1 0.0 copy-done.1
  16.1 0.6 rims.1
  16.7 0.1 collective-permute-start.4
  16.8 4.2 %collective-permute-start.5 = (bf16[2,2,2,16,512]{4,3,2,1,0:T(8,128)(2,1)S(1)}, bf16[2,2,2,16,512]{4,3,2,1,0:T(8,128)(2,1)S(1)}, u32[]{:S(2)}, u32[]{:S(2)}) collective-permute-start(bf16[2,2,2,16,512]{4,3,2,1,0:T(8,128)(2,1)S(1)} %get-tuple-element.15), channel_id=1, source_target_pairs={{0,15},{1,0},{2,1},{3,2},{4,3},{5,4},{6,5},{7,6},{8,7},{9,8},{10,9... | collective-permute-start | bytes 393224 | tf_op jit(solution)/shard_map/ppermute | solution.py:257
  21.0 0.0 collective-permute-start.6
  21.0 0.0 collective-permute-done.1.east
  21.0 0.0 copy-start.2
  21.0 4.1 %collective-permute-start.7 = (bf16[16,16,512]{2,1,0:T(8,128)(2,1)S(1)}, bf16[16,16,512]{2,1,0:T(8,128)(2,1)S(1)}, u32[]{:S(2)}, u32[]{:S(2)}) collective-permute-start(bf16[16,16,512]{2,1,0:T(8,128)(2,1)S(1)} %get-tuple-element.20), channel_id=1, source_target_pairs={{0,15},{1,0},{2,1},{3,2},{4,3},{5,4},{6,5},{7,6},{8,7},{9,8},{10,9... | collective-permute-start | bytes 786440 | tf_op jit(solution)/shard_map/ppermute | solution.py:257
  25.1 0.8 %collective-permute-done.west = bf16[16,16,512]{2,1,0:T(8,128)(2,1)S(1)} collective-permute-done((bf16[16,16,512]{2,1,0:T(8,128)(2,1)S(1)}, bf16[16,16,512]{2,1,0:T(8,128)(2,1)S(1)}, u32[]{:S(2)}, u32[]{:S(2)}) %collective-permute-start) | collective-permute-done | bytes 262176 | tf_op jit(solution)/shard_map/ppermute | solution.py:257
  25.9 2.8 %collective-permute-done.4.rims_w = bf16[2,2,2,16,512]{4,3,2,1,0:T(8,128)(2,1)S(1)} collective-permute-done((bf16[2,2,2,16,512]{4,3,2,1,0:T(8,128)(2,1)S(1)}, bf16[2,2,2,16,512]{4,3,2,1,0:T(8,128)(2,1)S(1)}, u32[]{:S(2)}, u32[]{:S(2)}) %collective-permute-start.4) | collective-permute-done | bytes 131104 | tf_op jit(solution)/shard_map/ppermute | solution.py:257
  28.7 0.0 collective-permute-done.5.rims_e
  28.7 0.0 copy-done
  28.7 2.5 %filtering.1 = (f32[16,64,512]{2,1,0:T(8,128)S(1)}, bf16[16,64,512]{2,1,0:T(8,128)(2,1)S(1)}, bf16[4,16,32,512]{3,2,1,0:T(8,128)(2,1)S(1)}) custom-call(s32[6]{0:T(128)S(1)} %stack.41.place, s32[4,256]{1,0:T(4,128)S(1)} %bitcast.19, bf16[16,128,256]{2,1,0:T(8,128)(2,1)S(1)} %forward_taps.1.after.taps, bf16[16,32,512]{2,1,0:T(8,128)(2,1)S(1)} %copy-done, ...), custom_call_target="tpu_custom_call" | custom-call | flops 20000000000 | bytes 8000000 | tf_op jit(solution)/shard_map/filtering/pallas_call | solution.py:265
  31.3 0.1 collective-permute-start.8
  31.4 0.0 copy-done.2
  31.4 2.0 %mixed.1 = (bf16[16,32,512]{2,1,0:T(8,128)(2,1)}, f32[8,128]{1,0:T(8,128)S(1)}) custom-call(bf16[4,16,32,512]{3,2,1,0:T(8,128)(2,1)S(1)} %get-tuple-element.16.filt, bf16[4,512,512]{2,1,0:T(8,128)(2,1)S(1)} %copy-done.2), custom_call_target="tpu_custom_call" | custom-call | flops 60000002048 | bytes 4500000 | tf_op jit(solution)/shard_map/mixed/pallas_call | solution.py:265
  33.4 0.0 collective-permute-done.6.ready_w.west
  33.4 0.0 collective-permute-done.7.ready_e.east
  33.4 0.6 collective-permute-done.8.recv
  34.0 1.2 %pair_sum.1.after = bf16[16,64,512]{2,1,0:T(8,128)(2,1)} custom-call(f32[8,128]{1,0:T(8,128)S(1)} %get-tuple-element.18.after, bf16[16,16,512]{2,1,0:T(8,128)(2,1)S(1)} %collective-permute-done.6.ready_w.west, bf16[16,16,512]{2,1,0:T(8,128)(2,1)S(1)} %collective-permute-done.7.ready_e.east, f32[16,64,512]{2,1,0:T(8,128)S(1)} %get-tuple-element.21.keep, ...), custom_call_target="tpu_custom_call" | custom-call | flops 524288 | bytes 4194304 | tf_op jit(solution)/shard_map/pair_sum/pallas_call | solution.py:265
  35.2 7.2 %all-to-all-start = ((bf16[16,64,512]{2,1,0:T(8,128)(2,1)}), bf16[16,64,512]{2,1,0:T(8,128)(2,1)S(1)}, u32[]{:S(2)}, u32[]{:S(2)}) async-start(bf16[16,64,512]{2,1,0:T(8,128)(2,1)} %pair_sum.1.after), calls=%async_computation | async-start | bytes 2097152 | tf_op jit(solution)/shard_map/all_to_all | solution.py:373
  42.5 0.0 copy-start.3
  42.5 3.2 %adjoint_taps.1.taps = bf16[16,128,320]{2,1,0:T(8,128)(2,1)S(1)} custom-call(s32[6]{0:T(128)S(1)} %stack.41.place, bf16[16,64,512]{2,1,0:T(8,128)(2,1)} %pair_sum.1.after, bf16[4,4,4,256]{3,2,1,0:T(4,128)(2,1)S(1)} %bitcast.17, s32[4,256]{1,0:T(4,128)S(1)} %bitcast.20, s32[4,256]{1,0:T(4,128)S(1)} %bitcast.22), custom_call_target="tpu_custom_call" | custom-call | flops 2000000000 | bytes 2000000 | tf_op jit(solution)/shard_map/adjoint_taps/pallas_call | solution.py:265
  45.7 0.0 copy-done.3
  45.7 4.5 %adjoint.1 = (bf16[16,32,512]{2,1,0:T(8,128)(2,1)}, f32[8,128]{1,0:T(8,128)S(1)}) custom-call(s32[6]{0:T(128)S(1)} %stack.41.place, bf16[16,64,512]{2,1,0:T(8,128)(2,1)} %pair_sum.1.after, bf16[16,128,320]{2,1,0:T(8,128)(2,1)S(1)} %adjoint_taps.1.taps, bf16[16,32,512]{2,1,0:T(8,128)(2,1)S(1)} %copy-done.1, ...), custom_call_target="tpu_custom_call" | custom-call | flops 3000000000 | bytes 6000000 | tf_op jit(solution)/shard_map/adjoint/pallas_call | solution.py:265
  50.1 8.4 %all-to-all-done.parts = bf16[16,64,512]{2,1,0:T(8,128)(2,1)S(1)} async-done(((bf16[16,64,512]{2,1,0:T(8,128)(2,1)}), bf16[16,64,512]{2,1,0:T(8,128)(2,1)S(1)}, u32[]{:S(2)}, u32[]{:S(2)}) %all-to-all-start) | async-done | bytes 1048608 | tf_op jit(solution)/shard_map/all_to_all | solution.py:373
  58.5 0.1 chip_sum.1.one
  58.7 0.3 collective-permute-start.11
  59.0 0.1 collective-permute-start.10
  59.1 6.4 %collective-permute-start.9 = (bf16[64,512]{1,0:T(8,128)(2,1)S(1)}, bf16[64,512]{1,0:T(8,128)(2,1)S(1)}, u32[]{:S(2)}, u32[]{:S(2)}) collective-permute-start(bf16[64,512]{1,0:T(8,128)(2,1)S(1)} %chip_sum.1.one), channel_id=1, source_target_pairs={{0,2},{1,3},{2,0},{3,1},{4,6},{5,7},{6,4},{7,5},{8,10},{9,11},{10,... | collective-permute-start | bytes 196616 | tf_op jit(solution)/shard_map/ppermute | solution.py:261
  65.5 0.5 collective-permute-done.11.four
  65.9 1.5 %collective-permute-done.10.three = bf16[64,512]{1,0:T(8,128)(2,1)S(1)} collective-permute-done((bf16[64,512]{1,0:T(8,128)(2,1)S(1)}, bf16[64,512]{1,0:T(8,128)(2,1)S(1)}, u32[]{:S(2)}, u32[]{:S(2)}) %collective-permute-start.10) | collective-permute-done | bytes 65568 | tf_op jit(solution)/shard_map/ppermute | solution.py:261
  67.4 1.0 %collective-permute-done.9.two = bf16[64,512]{1,0:T(8,128)(2,1)S(1)} collective-permute-done((bf16[64,512]{1,0:T(8,128)(2,1)S(1)}, bf16[64,512]{1,0:T(8,128)(2,1)S(1)}, u32[]{:S(2)}, u32[]{:S(2)}) %collective-permute-start.9) | collective-permute-done | bytes 65568 | tf_op jit(solution)/shard_map/ppermute | solution.py:261
  68.4 1.6 %collective-permute-start.14 = (bf16[64,512]{1,0:T(8,128)(2,1)S(1)}, bf16[64,512]{1,0:T(8,128)(2,1)S(1)}, u32[]{:S(2)}, u32[]{:S(2)}) collective-permute-start(bf16[64,512]{1,0:T(8,128)(2,1)S(1)} %four_sum.1.own), channel_id=1, source_target_pairs={{0,9},{1,8},{2,11},{3,10},{4,13},{5,12},{6,15},{7,14},{8,1},{9,0},... | collective-permute-start | bytes 196616 | tf_op jit(solution)/shard_map/ppermute | solution.py:261
  70.0 0.2 collective-permute-start.13
  70.2 1.7 %collective-permute-start.12 = (bf16[64,512]{1,0:T(8,128)(2,1)S(1)}, bf16[64,512]{1,0:T(8,128)(2,1)S(1)}, u32[]{:S(2)}, u32[]{:S(2)}) collective-permute-start(bf16[64,512]{1,0:T(8,128)(2,1)S(1)} %four_sum.1.own), channel_id=1, source_target_pairs={{0,1},{1,0},{2,3},{3,2},{4,5},{5,4},{6,7},{7,6},{8,9},{9,8},{10,11... | collective-permute-start | bytes 196616 | tf_op jit(solution)/shard_map/ppermute | solution.py:261
  72.0 1.7 %collective-permute-done.14.by_both = bf16[64,512]{1,0:T(8,128)(2,1)S(1)} collective-permute-done((bf16[64,512]{1,0:T(8,128)(2,1)S(1)}, bf16[64,512]{1,0:T(8,128)(2,1)S(1)}, u32[]{:S(2)}, u32[]{:S(2)}) %collective-permute-start.14) | collective-permute-done | bytes 65568 | tf_op jit(solution)/shard_map/ppermute | solution.py:261
  73.7 0.7 collective-permute-done.13.by_x
  74.3 0.1 collective-permute-done.12.by_z
  74.5 1.3 %last_sum.1 = f32[4,32,512]{2,1,0:T(8,128)} custom-call(s32[6]{0:T(128)S(1)} %stack.41.place, bf16[64,512]{1,0:T(8,128)(2,1)S(1)} %four_sum.1.own, bf16[64,512]{1,0:T(8,128)(2,1)S(1)} %collective-permute-done.12.by_z, bf16[64,512]{1,0:T(8,128)(2,1)S(1)} %collective-permute-done.13.by_x, bf16[64,512]{1,0:T(8,128)(2,1)S(1)} %collective-permute-done.14.by_both), custom_call_target="tpu_custom_call" | custom-call | flops 131072 | bytes 524288 | tf_op jit(solution)/shard_map/last_sum/pallas_call | solution.py:265
  (2 shorter events, 0.1 us)
Async XLA Ops:
  0.6 14.1 %copy-start.6 = (s32[256,4]{0,1:T(4,128)S(1)}, s32[256,4]{0,1:T(4,128)}, u32[]{:S(2)}) copy-start(s32[256,4]{0,1:T(4,128)} %param.9) | copy-start | bytes 12292
  0.6 14.1 %copy-start.5 = (s32[256,4]{0,1:T(4,128)S(1)}, s32[256,4]{0,1:T(4,128)}, u32[]{:S(2)}) copy-start(s32[256,4]{0,1:T(4,128)} %param.8) | copy-start | bytes 12292
  0.7 14.1 %copy-start.4 = (bf16[4,256,4,4]{1,3,2,0:T(4,128)(2,1)S(1)}, bf16[4,256,4,4]{1,3,2,0:T(4,128)(2,1)}, u32[]{:S(2)}) copy-start(bf16[4,256,4,4]{1,3,2,0:T(4,128)(2,1)} %param.7) | copy-start | bytes 98308
  2.5 13.6 %collective-permute-start.3 = (bf16[2,2,32,512]{3,2,1,0:T(8,128)(2,1)S(1)}, bf16[2,2,32,512]{3,2,1,0:T(8,128)(2,1)S(1)}, u32[]{:S(2)}, u32[]{:S(2)}) collective-permute-start(bf16[2,2,32,512]{3,2,1,0:T(8,128)(2,1)S(1)} %get-tuple-element.31), channel_id=1, source_target_pairs={{0,0},{240,240},{16,32},{32,16},{48,64},{64,48},{80,96},{96,80},{1... | collective-permute-start | bytes 393224 | tf_op jit(solution)/shard_map/ppermute | solution.py:323
  3.2 12.9 %collective-permute-start.2 = (bf16[2,2,32,512]{3,2,1,0:T(8,128)(2,1)S(1)}, bf16[2,2,32,512]{3,2,1,0:T(8,128)(2,1)S(1)}, u32[]{:S(2)}, u32[]{:S(2)}) collective-permute-start(bf16[2,2,32,512]{3,2,1,0:T(8,128)(2,1)S(1)} %get-tuple-element.32), channel_id=1, source_target_pairs={{0,16},{16,0},{32,48},{48,32},{64,80},{80,64},{96,112},{112,96},{1... | collective-permute-start | bytes 393224 | tf_op jit(solution)/shard_map/ppermute | solution.py:261
  7.8 8.3 %copy-start.1 = (bf16[16,32,512]{2,1,0:T(8,128)(2,1)S(1)}, bf16[16,32,512]{2,1,0:T(8,128)(2,1)}, u32[]{:S(2)}) copy-start(bf16[16,32,512]{2,1,0:T(8,128)(2,1)} %center.3) | copy-start | bytes 1572868
  7.8 13.2 %collective-permute-start.1 = (bf16[16,16,512]{2,1,0:T(8,128)(2,1)S(1)}, bf16[16,16,512]{2,1,0:T(8,128)(2,1)S(1)}, u32[]{:S(2)}, u32[]{:S(2)}) collective-permute-start(bf16[16,16,512]{2,1,0:T(8,128)(2,1)S(1)} %get-tuple-element.29), channel_id=1, source_target_pairs={{0,15},{1,0},{2,1},{3,2},{4,3},{5,4},{6,5},{7,6},{8,7},{9,8},{10,9... | collective-permute-start | bytes 786440 | tf_op jit(solution)/shard_map/ppermute | solution.py:257
  14.6 11.3 %collective-permute-start = (bf16[16,16,512]{2,1,0:T(8,128)(2,1)S(1)}, bf16[16,16,512]{2,1,0:T(8,128)(2,1)S(1)}, u32[]{:S(2)}, u32[]{:S(2)}) collective-permute-start(bf16[16,16,512]{2,1,0:T(8,128)(2,1)S(1)} %get-tuple-element.30), channel_id=1, source_target_pairs={{0,1},{1,2},{2,3},{3,4},{4,5},{5,6},{6,7},{7,8},{8,9},{9,10},{10,1... | collective-permute-start | bytes 786440 | tf_op jit(solution)/shard_map/ppermute | solution.py:257
  14.7 14.0 %copy-start = (bf16[16,32,512]{2,1,0:T(8,128)(2,1)S(1)}, bf16[16,32,512]{2,1,0:T(8,128)(2,1)}, u32[]{:S(2)}) copy-start(bf16[16,32,512]{2,1,0:T(8,128)(2,1)} %center.2) | copy-start | bytes 1572868
  16.7 12.0 %collective-permute-start.4 = (bf16[2,2,2,16,512]{4,3,2,1,0:T(8,128)(2,1)S(1)}, bf16[2,2,2,16,512]{4,3,2,1,0:T(8,128)(2,1)S(1)}, u32[]{:S(2)}, u32[]{:S(2)}) collective-permute-start(bf16[2,2,2,16,512]{4,3,2,1,0:T(8,128)(2,1)S(1)} %get-tuple-element.14), channel_id=1, source_target_pairs={{0,1},{1,2},{2,3},{3,4},{4,5},{5,6},{6,7},{7,8},{8,9},{9,10},{10,1... | collective-permute-start | bytes 393224 | tf_op jit(solution)/shard_map/ppermute | solution.py:257
  16.8 12.0 %collective-permute-start.5 = (bf16[2,2,2,16,512]{4,3,2,1,0:T(8,128)(2,1)S(1)}, bf16[2,2,2,16,512]{4,3,2,1,0:T(8,128)(2,1)S(1)}, u32[]{:S(2)}, u32[]{:S(2)}) collective-permute-start(bf16[2,2,2,16,512]{4,3,2,1,0:T(8,128)(2,1)S(1)} %get-tuple-element.15), channel_id=1, source_target_pairs={{0,15},{1,0},{2,1},{3,2},{4,3},{5,4},{6,5},{7,6},{8,7},{9,8},{10,9... | collective-permute-start | bytes 393224 | tf_op jit(solution)/shard_map/ppermute | solution.py:257
  21.0 12.4 %collective-permute-start.6 = (bf16[16,16,512]{2,1,0:T(8,128)(2,1)S(1)}, bf16[16,16,512]{2,1,0:T(8,128)(2,1)S(1)}, u32[]{:S(2)}, u32[]{:S(2)}) collective-permute-start(bf16[16,16,512]{2,1,0:T(8,128)(2,1)S(1)} %get-tuple-element.19), channel_id=1, source_target_pairs={{0,1},{1,2},{2,3},{3,4},{4,5},{5,6},{6,7},{7,8},{8,9},{9,10},{10,1... | collective-permute-start | bytes 786440 | tf_op jit(solution)/shard_map/ppermute | solution.py:257
  21.0 10.4 %copy-start.2 = (bf16[4,512,512]{2,1,0:T(8,128)(2,1)S(1)}, bf16[4,512,512]{2,1,0:T(8,128)(2,1)}, u32[]{:S(2)}) copy-start(bf16[4,512,512]{2,1,0:T(8,128)(2,1)} %mixing.3) | copy-start | bytes 6291460
  21.0 12.4 %collective-permute-start.7 = (bf16[16,16,512]{2,1,0:T(8,128)(2,1)S(1)}, bf16[16,16,512]{2,1,0:T(8,128)(2,1)S(1)}, u32[]{:S(2)}, u32[]{:S(2)}) collective-permute-start(bf16[16,16,512]{2,1,0:T(8,128)(2,1)S(1)} %get-tuple-element.20), channel_id=1, source_target_pairs={{0,15},{1,0},{2,1},{3,2},{4,3},{5,4},{6,5},{7,6},{8,7},{9,8},{10,9... | collective-permute-start | bytes 786440 | tf_op jit(solution)/shard_map/ppermute | solution.py:257
  31.3 2.7 %collective-permute-start.8 = (bf16[16,64,512]{2,1,0:T(8,128)(2,1)S(1)}, bf16[16,64,512]{2,1,0:T(8,128)(2,1)S(1)}, u32[]{:S(2)}, u32[]{:S(2)}) collective-permute-start(bf16[16,64,512]{2,1,0:T(8,128)(2,1)S(1)} %get-tuple-element.22), channel_id=1, source_target_pairs={{0,16},{16,0},{1,17},{17,1},{2,18},{18,2},{3,19},{19,3},{4,20},{20... | collective-permute-start | bytes 3145736 | tf_op jit(solution)/shard_map/ppermute | solution.py:261
  35.2 23.3 %all-to-all-start = ((bf16[16,64,512]{2,1,0:T(8,128)(2,1)}), bf16[16,64,512]{2,1,0:T(8,128)(2,1)S(1)}, u32[]{:S(2)}, u32[]{:S(2)}) async-start(bf16[16,64,512]{2,1,0:T(8,128)(2,1)} %pair_sum.1.after), calls=%async_computation | async-start | bytes 2097152 | tf_op jit(solution)/shard_map/all_to_all | solution.py:373
  42.5 3.2 %copy-start.3 = (bf16[4,512,512]{2,1,0:T(8,128)(2,1)S(1)}, bf16[4,512,512]{2,1,0:T(8,128)(2,1)}, u32[]{:S(2)}) copy-start(bf16[4,512,512]{2,1,0:T(8,128)(2,1)} %mixing.3) | copy-start | bytes 6291460
  58.7 7.2 %collective-permute-start.11 = (bf16[64,512]{1,0:T(8,128)(2,1)S(1)}, bf16[64,512]{1,0:T(8,128)(2,1)S(1)}, u32[]{:S(2)}, u32[]{:S(2)}) collective-permute-start(bf16[64,512]{1,0:T(8,128)(2,1)S(1)} %chip_sum.1.one), channel_id=1, source_target_pairs={{0,6},{1,7},{2,4},{3,5},{4,2},{5,3},{6,0},{7,1},{8,14},{9,15},{10,... | collective-permute-start | bytes 196616 | tf_op jit(solution)/shard_map/ppermute | solution.py:261
  59.0 8.4 %collective-permute-start.10 = (bf16[64,512]{1,0:T(8,128)(2,1)S(1)}, bf16[64,512]{1,0:T(8,128)(2,1)S(1)}, u32[]{:S(2)}, u32[]{:S(2)}) collective-permute-start(bf16[64,512]{1,0:T(8,128)(2,1)S(1)} %chip_sum.1.one), channel_id=1, source_target_pairs={{0,4},{1,5},{2,6},{3,7},{4,0},{5,1},{6,2},{7,3},{8,12},{9,13},{10,... | collective-permute-start | bytes 196616 | tf_op jit(solution)/shard_map/ppermute | solution.py:261
  59.1 9.3 %collective-permute-start.9 = (bf16[64,512]{1,0:T(8,128)(2,1)S(1)}, bf16[64,512]{1,0:T(8,128)(2,1)S(1)}, u32[]{:S(2)}, u32[]{:S(2)}) collective-permute-start(bf16[64,512]{1,0:T(8,128)(2,1)S(1)} %chip_sum.1.one), channel_id=1, source_target_pairs={{0,2},{1,3},{2,0},{3,1},{4,6},{5,7},{6,4},{7,5},{8,10},{9,11},{10,... | collective-permute-start | bytes 196616 | tf_op jit(solution)/shard_map/ppermute | solution.py:261
  68.4 5.3 %collective-permute-start.14 = (bf16[64,512]{1,0:T(8,128)(2,1)S(1)}, bf16[64,512]{1,0:T(8,128)(2,1)S(1)}, u32[]{:S(2)}, u32[]{:S(2)}) collective-permute-start(bf16[64,512]{1,0:T(8,128)(2,1)S(1)} %four_sum.1.own), channel_id=1, source_target_pairs={{0,9},{1,8},{2,11},{3,10},{4,13},{5,12},{6,15},{7,14},{8,1},{9,0},... | collective-permute-start | bytes 196616 | tf_op jit(solution)/shard_map/ppermute | solution.py:261
  70.0 4.4 %collective-permute-start.13 = (bf16[64,512]{1,0:T(8,128)(2,1)S(1)}, bf16[64,512]{1,0:T(8,128)(2,1)S(1)}, u32[]{:S(2)}, u32[]{:S(2)}) collective-permute-start(bf16[64,512]{1,0:T(8,128)(2,1)S(1)} %four_sum.1.own), channel_id=1, source_target_pairs={{0,8},{8,0},{1,9},{9,1},{2,10},{10,2},{3,11},{11,3},{4,12},{12,4},... | collective-permute-start | bytes 196616 | tf_op jit(solution)/shard_map/ppermute | solution.py:261
  70.2 4.3 %collective-permute-start.12 = (bf16[64,512]{1,0:T(8,128)(2,1)S(1)}, bf16[64,512]{1,0:T(8,128)(2,1)S(1)}, u32[]{:S(2)}, u32[]{:S(2)}) collective-permute-start(bf16[64,512]{1,0:T(8,128)(2,1)S(1)} %four_sum.1.own), channel_id=1, source_target_pairs={{0,1},{1,0},{2,3},{3,2},{4,5},{5,4},{6,7},{7,6},{8,9},{9,8},{10,11... | collective-permute-start | bytes 196616 | tf_op jit(solution)/shard_map/ppermute | solution.py:261

commit v6 on v3

--- a/solution.py
+++ b/solution.py
@@ -10,6 +10,8 @@
 from jax.sharding import PartitionSpec as P
 
 HL = 2
+MIXED_COST = 60_000_000_000
+FILTER_COST = 20_000_000_000
 WL = 16
 SPAN = 2 * HL + 1
 F32 = jnp.float32
@@ -60,14 +62,14 @@
 
 
 def forward_taps_kernel(place, psi, lat, lon, forward, near_all, spread):
-    rows = forward.shape[0]
+    rows = forward.shape[0] - 2 * HL
     basis_count, blocks, taps, cycles = psi.shape
     count = taps + 2
     wide = forward.shape[2] // blocks
     lines = basis_count * count
     gathered(near_all, place, psi, lat, lon, rows)
     near = near_all[...]
-    slot = iota((128, 128), 0) - HL
+    slot = iota((128, 128), 0)
     base = iota((1, wide), 1) - WL
 
     def one_row(row, carry):
@@ -80,7 +82,7 @@
         store_bands(forward, row, jnp.concatenate(totals, axis=1), basis_count, count, taps)
         return carry
 
-    lax.fori_loop(0, rows, one_row, 0, unroll=4)
+    lax.fori_loop(0, rows + 2 * HL, one_row, 0, unroll=20)
 
 
 def adjoint_taps_kernel(place, after, psi, lat, lon, adjoint, near_all, adj_wide):
@@ -112,10 +114,10 @@
         store_bands(adjoint, row, total, basis_count, count, taps)
         return carry
 
-    lax.fori_loop(0, rows, one_row, 0, unroll=2)
-
-
-def rims_kernel(place, after, inner, outer, to_east, to_west):
+    lax.fori_loop(0, rows, one_row, 0, unroll=4)
+
+
+def rims_kernel(place, inner, outer, to_east, to_west):
     cols = inner.shape[2]
     odd = place[3] == 1
     north = jnp.where(odd, inner[...], outer[...])
@@ -145,31 +147,46 @@
         extended[lines, WL + cols :] = jnp.where(inside, rims_e[side, which], none)
 
 
-def filter_kernel(
-    place, lat, taps, center, west, east, inner, outer, rims_w, rims_e, cot, keep, send, filt_out, extended
+def terms_kernel(
+    place, lat, taps, center, west, east, cot, inner, outer, keep, send, extended, filtered, around
 ):
     rows, cols, channels = center.shape
-    basis_count = filt_out.shape[0]
+    basis_count = filtered.shape[0]
     blocks = lat.shape[0]
-    assemble(0, place, extended, center, west, east, inner, outer, rims_w, rims_e)
+    wide_rows = rows + 2 * HL
+    extended[0:rows, 0:WL] = west[...]
+    extended[0:rows, WL : WL + cols] = center[...]
+    extended[0:rows, WL + cols :] = east[...]
+    extended[rows] = jnp.zeros(extended.shape[1:], BF16)
+    odd = place[3] == 1
+    around[0:HL] = jnp.where(odd, inner[1], outer[1])
+    around[HL : HL + rows] = cot[...]
+    around[HL + rows :] = jnp.where(odd, outer[1], inner[1])
 
     def one_row(row, carry):
-        slabs = [extended[row + HL + lat[block, place[0] + row]] for block in range(blocks)]
+        cycle = jnp.clip(place[0] + row - HL, 0, place[5] - 1)
+        slabs = []
+        for block in range(blocks):
+            source = row - HL + lat[block, cycle]
+            inside = (source >= 0) & (source < rows)
+            slabs.append(extended[jnp.where(inside, source, rows)])
         slab = jnp.concatenate(slabs, axis=0)
-        filtered = jnp.dot(taps[row], slab, preferred_element_type=F32).astype(BF16)
-        filt_out[:, row] = filtered.reshape(basis_count, cols, channels)
+        part = jnp.dot(taps[row], slab, preferred_element_type=F32).astype(BF16)
+        filtered[:, row] = part.reshape(basis_count, cols, channels)
         return carry
 
-    lax.fori_loop(0, rows, one_row, 0, unroll=4)
-    cot_flat = cot[...].reshape(rows * cols, channels)
+    lax.fori_loop(0, wide_rows, one_row, 0, unroll=20)
+    cot_flat = around[...].reshape(wide_rows * cols, channels)
     pairs = keep.shape[0] // 2
     share = channels // (2 * pairs)
     per = keep.shape[1] // share
     core = place[3]
     for basis in range(basis_count):
-        filtered = filt_out[basis].reshape(rows * cols, channels)
         terms = lax.dot_general(
-            filtered, cot_flat, (((0,), (0,)), ((), ())), preferred_element_type=F32
+            filtered[basis].reshape(wide_rows * cols, channels),
+            cot_flat,
+            (((0,), (0,)), ((), ())),
+            preferred_element_type=F32,
         ).reshape(pairs, 2, share, channels)
         lines = slice(basis % per * share, (basis % per + 1) * share)
         mine = jnp.where(core == 0, terms[:, 0], terms[:, 1])
@@ -179,13 +196,33 @@
             send[2 * pair + basis // per, lines] = other[pair]
 
 
-def output_kernel(filt, mixing, out, token):
+def ready_kernel(west, east, token):
     token[...] = jnp.zeros_like(token)
-    basis_count, rows, cols, channels = filt.shape
+
+
+def output_kernel(
+    place, after, lat, taps, center, west, east, inner, outer, rims_w, rims_e, mixing, out, token, extended, filtered
+):
+    token[...] = jnp.zeros_like(token)
+    rows, cols, channels = center.shape
+    basis_count = mixing.shape[0]
+    blocks = lat.shape[0]
+    assemble(0, place, extended, center, west, east, inner, outer, rims_w, rims_e)
+
+    def one_row(row, carry):
+        slabs = [extended[row + HL + lat[block, place[0] + row]] for block in range(blocks)]
+        slab = jnp.concatenate(slabs, axis=0)
+        part = jnp.dot(taps[row + HL], slab, preferred_element_type=F32).astype(BF16)
+        filtered[:, row] = part.reshape(basis_count, cols, channels)
+        return carry
+
+    lax.fori_loop(0, rows, one_row, 0, unroll=16)
     total = None
     for basis in range(basis_count):
         part = jnp.dot(
-            filt[basis].reshape(rows * cols, channels), mixing[basis], preferred_element_type=F32
+            filtered[basis].reshape(rows * cols, channels),
+            mixing[basis],
+            preferred_element_type=F32,
         )
         total = part if total is None else total + part
     out[...] = total.reshape(rows, cols, channels).astype(BF16)
@@ -205,7 +242,7 @@
         spread[:, row] = pulled.reshape(basis_count, cols, channels)
         return carry
 
-    lax.fori_loop(0, rows, one_row, 0, unroll=4)
+    lax.fori_loop(0, rows, one_row, 0, unroll=16)
     total = None
     for basis in range(basis_count):
         part = lax.dot_general(
@@ -222,7 +259,7 @@
     out[...] = (keep[...] + recv[...].astype(F32)).astype(BF16)
 
 
-def chip_sum_kernel(after, parts, out):
+def chip_sum_kernel(after_one, after_two, parts, out):
     total = parts[0].astype(F32)
     for chip in range(1, parts.shape[0]):
         total = total + parts[chip].astype(F32)
@@ -304,7 +341,7 @@
     lines = basis_count * blocks * (taps + 2)
     fwd_taps = call(
         forward_taps_kernel,
-        shaped((rows, basis_count * cols, blocks * wide), BF16),
+        shaped((rows + 2 * HL, basis_count * cols, blocks * wide), BF16),
         (place, psi, lat, lon),
         [SMEM] + [VMEM] * 3,
         "forward_taps",
@@ -319,47 +356,45 @@
     outer = lax.ppermute(outer, LAT, pairs)
     rim = shaped((2, 2, HL, WL, channels), BF16)
     rim_to_east, rim_to_west = call(
-        rims_kernel,
-        (rim, rim),
-        (place, fwd_taps, inner, outer),
-        [SMEM] + [VMEM] * 3,
-        "rims",
-        moved=1_000_000,
+        rims_kernel, (rim, rim), (place, inner, outer), [SMEM] + [VMEM] * 2, "rims", moved=1_000_000
     )
     rims_w = shift(rim_to_east, LON, lons, 1)
     rims_e = shift(rim_to_west, LON, lons, -1)
     share = basis_count * channels // lats
-    keep, send, filtered = call(
-        filter_kernel,
+    keep, send = call(
+        terms_kernel,
         (
             shaped((lats, share // 2, channels), F32),
             shaped((lats, share // 2, channels), BF16),
-            shaped((basis_count, rows, cols, channels), BF16),
         ),
-        (place, lat, fwd_taps, field, west, east, inner, outer, rims_w, rims_e, cotangent),
-        [SMEM] * 2 + [VMEM] * 9,
-        "filtering",
-        [pltpu.VMEM((rows + 2 * HL, wide, channels), BF16)],
-        flops=2_000_000_000,
+        (place, lat, fwd_taps, field, west, east, cotangent, inner, outer),
+        [SMEM] * 2 + [VMEM] * 7,
+        "terms",
+        [
+            pltpu.VMEM((rows + 1, wide, channels), BF16),
+            pltpu.VMEM((basis_count, rows + 2 * HL, cols, channels), BF16),
+            pltpu.VMEM((rows + 2 * HL, cols, channels), BF16),
+        ],
+        flops=FILTER_COST,
         moved=8_000_000,
     )
     recv = swap(send, "core", 2, 1)
     cot_west = shift(cotangent[:, cols - WL :], LON, lons, 1)
     cot_east = shift(cotangent[:, :WL], LON, lons, -1)
     token = shaped((8, 128), F32)
-    output, token_one = call(
-        output_kernel,
-        (shaped((rows, cols, channels), BF16), token),
-        (filtered, mixing),
+    ready = call(
+        ready_kernel,
+        token,
+        (cot_west, cot_east),
         [VMEM] * 2,
-        "mixed",
-        flops=1_500_000_000,
-        moved=4_500_000,
+        "ready",
+        flops=MIXED_COST,
+        moved=1_000_000,
     )
     summed = call(
         pair_sum_kernel,
         shaped(keep.shape, BF16),
-        (token_one, keep, recv),
+        (ready, keep, recv),
         [VMEM] * 3,
         "pair_sum",
         flops=keep.size,
@@ -367,6 +402,32 @@
     )
     parts = lax.all_to_all(summed, ("y", "xh", "xl"), 0, 0)
 
+    output, token_one = call(
+        output_kernel,
+        (shaped((rows, cols, channels), BF16), token),
+        (
+            place,
+            summed,
+            lat,
+            fwd_taps,
+            field,
+            west,
+            east,
+            inner,
+            outer,
+            rims_w,
+            rims_e,
+            mixing,
+        ),
+        [SMEM, VMEM, SMEM] + [VMEM] * 9,
+        "output",
+        [
+            pltpu.VMEM((rows + 2 * HL, wide, channels), BF16),
+            pltpu.VMEM((basis_count, rows, cols, channels), BF16),
+        ],
+        flops=3_000_000_000,
+        moved=6_000_000,
+    )
     adj_taps = call(
         adjoint_taps_kernel,
         shaped((rows, basis_count * cols, SPAN * wide), BF16),
@@ -410,8 +471,8 @@
     part = call(
         chip_sum_kernel,
         shaped((deep, channels), BF16),
-        (token_two, parts),
-        [VMEM] * 2,
+        (token_one, token_two, parts),
+        [VMEM] * 3,
         "chip_sum",
         flops=parts.size,
         moved=parts.size * 2,

time: 79.9 us -> 74.6 us (0.934)
  waiting for transfers between devices: 18.2 us -> 12.6 us
    ppermute x6, waiting for transfers between devices: 4.74 us -> 0.04 us  [shift(): lax.ppermute(cells, axis, [(i, (i + step) % count) for i in range(count)])]
    all_to_all x1, waiting for transfers between devices: 6.43 us -> 3.11 us  [local(): parts = lax.all_to_all(summed, ('y', 'xh', 'xl'), 0, 0)]
    ppermute x8, waiting for transfers between devices: 7.02 us -> 9.44 us  [swap(): return lax.ppermute(cells, axis, [(i, i ^ mask) for i in range(count)])]
    ppermute x1, starting transfers between devices: 0.67 us -> 1.55 us  [local(): outer = lax.ppermute(outer, LAT, pairs)]
    pallas_call x10 -> x11, Pallas kernels: 19.9 us -> 19.3 us  [call(): pl.pallas_call(kernel, out_shape=outs, in_specs=specs, out_specs=jax.tree...]
  transfers between devices with their start and end apart: 16 -> 16, of which waited for: 9 -> 7; matrix products, arithmetic and copies ran while one was open for 1% -> 2% of each run, Pallas kernels for 18% -> 22%
where the time goes in v6:
time: 74.6 us; the launch traced here: 74.2 us
  starting transfers between devices  37.7 us (51%)
  Pallas kernels  19.3 us (26%)
  waiting for transfers between devices  12.6 us (17%)
  local copies, waits for them, and re-layouts  3.04 us (4%)
  between operations  0.84 us (1%)
    pallas_call x11, Pallas kernels, call(): pl.pallas_call(kernel, out_shape=outs, in_specs=specs, out_specs=jax.tree...  19.3 us
    ppermute x6, starting transfers between devices, shift(): lax.ppermute(cells, axis, [(i, (i + step) % count) for i in range(count)])  14.4 us
    ppermute x8, starting transfers between devices, swap(): return lax.ppermute(cells, axis, [(i, i ^ mask) for i in range(count)])  12.9 us
    ppermute x8, waiting for transfers between devices, swap(): return lax.ppermute(cells, axis, [(i, i ^ mask) for i in range(count)])  9.44 us
    all_to_all x1, starting transfers between devices, local(): parts = lax.all_to_all(summed, ('y', 'xh', 'xl'), 0, 0)  8.82 us
    all_to_all x1, waiting for transfers between devices, local(): parts = lax.all_to_all(summed, ('y', 'xh', 'xl'), 0, 0)  3.11 us
    another operation x2, local copies, waits for them, and re-layouts, local(): top = jnp.stack([cells[:HL] for cells in both])  1.82 us
    ppermute x1, starting transfers between devices, local(): outer = lax.ppermute(outer, LAT, pairs)  1.55 us
  transfers between devices with their start and end apart: 16, of which 7 were waited for; matrix products, arithmetic and copies ran while one was open for 2% of the time, Pallas kernels for 22%

profile of v6, /device:TPU:2, one launch (start us, length us, event | category | flops | bytes accessed | tf_op | source)
XLA Modules:
  0.0 74.2 jit_solution(12221509030681439654)
XLA Ops:
  0.6 0.0 copy-start.1
  0.6 0.0 copy-start.5
  0.7 0.0 copy-start.3
  0.7 0.0 copy-start.4
  0.7 0.9 %slice_bitcast_fusion.3 = (bf16[1,2,32,512]{3,2,1,0:T(8,128)(2,1)S(1)}, bf16[1,2,32,512]{3,2,1,0:T(8,128)(2,1)S(1)}) fusion(bf16[16,32,512]{2,1,0:T(8,128)(2,1)} %center.4), kind=kLoop, calls=%fused_computation.7 | loop fusion | bytes 262144 | tf_op jit(solution)/shard_map/stack | solution.py:331
  1.6 0.9 %slice_bitcast_fusion.2 = (bf16[1,2,32,512]{3,2,1,0:T(8,128)(2,1)S(1)}, bf16[1,2,32,512]{3,2,1,0:T(8,128)(2,1)S(1)}) fusion(bf16[16,32,512]{2,1,0:T(8,128)(2,1)} %center.5), kind=kLoop, calls=%fused_computation.6 | loop fusion | bytes 262144 | tf_op jit(solution)/shard_map/stack | solution.py:331
  2.5 0.7 broadcast_select_fusion
  3.2 0.0 collective-permute-start.4
  3.2 1.6 %collective-permute-start.5 = (bf16[2,2,32,512]{3,2,1,0:T(8,128)(2,1)}, bf16[2,2,32,512]{3,2,1,0:T(8,128)(2,1)S(1)}, u32[]{:S(2)}, u32[]{:S(2)}) collective-permute-start(bf16[2,2,32,512]{3,2,1,0:T(8,128)(2,1)} %get-tuple-element.27), channel_id=1, source_target_pairs={{0,0},{240,240},{16,32},{32,16},{48,64},{64,48},{80,96},{96,80},{1... | collective-permute-start | bytes 393224 | tf_op jit(solution)/shard_map/ppermute | solution.py:356
  4.7 1.1 %fusion = (bf16[16,16,512]{2,1,0:T(8,128)(2,1)S(1)}, bf16[16,16,512]{2,1,0:T(8,128)(2,1)S(1)}) fusion(bf16[16,32,512]{2,1,0:T(8,128)(2,1)} %center.4), kind=kLoop, calls=%fused_computation.8 | loop fusion | bytes 1048576 | tf_op jit(solution)/shard_map/slice | solution.py:336
  5.8 2.0 %collective-permute-start.2 = (bf16[16,16,512]{2,1,0:T(8,128)(2,1)S(1)}, bf16[16,16,512]{2,1,0:T(8,128)(2,1)S(1)}, u32[]{:S(2)}, u32[]{:S(2)}) collective-permute-start(bf16[16,16,512]{2,1,0:T(8,128)(2,1)S(1)} %get-tuple-element.24), channel_id=1, source_target_pairs={{0,1},{1,2},{2,3},{3,4},{4,5},{5,6},{6,7},{7,8},{8,9},{9,10},{10,1... | collective-permute-start | bytes 786440 | tf_op jit(solution)/shard_map/ppermute | solution.py:290
  7.8 4.0 %collective-permute-start.3 = (bf16[16,16,512]{2,1,0:T(8,128)(2,1)S(1)}, bf16[16,16,512]{2,1,0:T(8,128)(2,1)S(1)}, u32[]{:S(2)}, u32[]{:S(2)}) collective-permute-start(bf16[16,16,512]{2,1,0:T(8,128)(2,1)S(1)} %get-tuple-element.23), channel_id=1, source_target_pairs={{0,15},{1,0},{2,1},{3,2},{4,3},{5,4},{6,5},{7,6},{8,7},{9,8},{10,9... | collective-permute-start | bytes 786440 | tf_op jit(solution)/shard_map/ppermute | solution.py:290
  11.8 0.0 copy-done.1
  11.8 0.0 copy-start
  11.9 0.1 collective-permute-start
  12.0 0.1 stack.41.place
  12.1 0.0 copy-done.5
  12.1 0.0 copy-done.3
  12.1 0.0 copy-done.4
  12.1 1.4 %forward_taps.1.taps = bf16[20,128,256]{2,1,0:T(8,128)(2,1)S(1)} custom-call(s32[6]{0:T(128)S(1)} %stack.41.place, bf16[4,4,4,256]{3,2,1,0:T(4,128)(2,1)S(1)} %bitcast.16, s32[4,256]{1,0:T(4,128)S(1)} %bitcast.20, s32[4,256]{1,0:T(4,128)S(1)} %bitcast.18), custom_call_target="tpu_custom_call" | custom-call | flops 1000000000 | bytes 1000000 | tf_op jit(solution)/shard_map/forward_taps/pallas_call | solution.py:298
  13.5 0.0 copy-start.6
  13.5 0.0 collective-permute-done.4.inner
  13.5 4.2 %collective-permute-start.1 = (bf16[16,16,512]{2,1,0:T(8,128)(2,1)S(1)}, bf16[16,16,512]{2,1,0:T(8,128)(2,1)S(1)}, u32[]{:S(2)}, u32[]{:S(2)}) collective-permute-start(bf16[16,16,512]{2,1,0:T(8,128)(2,1)S(1)} %get-tuple-element.25), channel_id=1, source_target_pairs={{0,15},{1,0},{2,1},{3,2},{4,3},{5,4},{6,5},{7,6},{8,7},{9,8},{10,9... | collective-permute-start | bytes 786440 | tf_op jit(solution)/shard_map/ppermute | solution.py:290
  17.7 0.0 collective-permute-done.5.outer
  17.7 0.0 collective-permute-done.2.west
  17.7 0.0 collective-permute-done.3.east
  17.7 0.0 copy-done
  17.7 3.2 %terms.1 = (f32[16,64,512]{2,1,0:T(8,128)S(1)}, bf16[16,64,512]{2,1,0:T(8,128)(2,1)S(1)}) custom-call(s32[6]{0:T(128)S(1)} %stack.41.place, s32[4,256]{1,0:T(4,128)S(1)} %bitcast.21, bf16[20,128,256]{2,1,0:T(8,128)(2,1)S(1)} %forward_taps.1.taps, bf16[16,32,512]{2,1,0:T(8,128)(2,1)S(1)} %copy-done, bf16[16,16,512]{2,1,0:T(8,128)(2,1)S(1)} %collective-permute-done.2.west, ...), custom_call_target="tpu_custom_call" | custom-call | flops 20000000000 | bytes 8000000 | tf_op jit(solution)/shard_map/terms/pallas_call | solution.py:298
  20.9 0.0 copy-done.6
  20.9 2.7 %collective-permute-start.6 = (bf16[16,64,512]{2,1,0:T(8,128)(2,1)S(1)}, bf16[16,64,512]{2,1,0:T(8,128)(2,1)S(1)}, u32[]{:S(2)}, u32[]{:S(2)}) collective-permute-start(bf16[16,64,512]{2,1,0:T(8,128)(2,1)S(1)} %get-tuple-element.12), channel_id=1, source_target_pairs={{0,16},{16,0},{1,17},{17,1},{2,18},{18,2},{3,19},{19,3},{4,20},{20... | collective-permute-start | bytes 3145736 | tf_op jit(solution)/shard_map/ppermute | solution.py:294
  23.7 0.0 collective-permute-done.west
  23.7 0.0 collective-permute-done.1.east
  23.7 2.3 %collective-permute-done.6.recv = bf16[16,64,512]{2,1,0:T(8,128)(2,1)S(1)} collective-permute-done((bf16[16,64,512]{2,1,0:T(8,128)(2,1)S(1)}, bf16[16,64,512]{2,1,0:T(8,128)(2,1)S(1)}, u32[]{:S(2)}, u32[]{:S(2)}) %collective-permute-start.6) | collective-permute-done | bytes 1048608 | tf_op jit(solution)/shard_map/ppermute | solution.py:294
  26.0 1.2 %pair_sum.1.after = bf16[16,64,512]{2,1,0:T(8,128)(2,1)} custom-call(f32[8,128]{1,0:T(8,128)S(1)} %ready.1.after, f32[16,64,512]{2,1,0:T(8,128)S(1)} %get-tuple-element.11.keep, bf16[16,64,512]{2,1,0:T(8,128)(2,1)S(1)} %collective-permute-done.6.recv), custom_call_target="tpu_custom_call" | custom-call | flops 524288 | bytes 4194304 | tf_op jit(solution)/shard_map/pair_sum/pallas_call | solution.py:298
  27.2 8.8 %all-to-all-start = ((bf16[16,64,512]{2,1,0:T(8,128)(2,1)}), bf16[16,64,512]{2,1,0:T(8,128)(2,1)S(1)}, u32[]{:S(2)}, u32[]{:S(2)}) async-start(bf16[16,64,512]{2,1,0:T(8,128)(2,1)} %pair_sum.1.after), calls=%async_computation | async-start | bytes 2097152 | tf_op jit(solution)/shard_map/all_to_all | solution.py:403
  36.0 0.6 rims.1
  36.6 0.1 collective-permute-start.7
  36.7 0.0 copy-start.2
  36.7 0.0 copy-start.7
  36.7 4.1 %collective-permute-start.8 = (bf16[2,2,2,16,512]{4,3,2,1,0:T(8,128)(2,1)S(1)}, bf16[2,2,2,16,512]{4,3,2,1,0:T(8,128)(2,1)S(1)}, u32[]{:S(2)}, u32[]{:S(2)}) collective-permute-start(bf16[2,2,2,16,512]{4,3,2,1,0:T(8,128)(2,1)S(1)} %get-tuple-element.14), channel_id=1, source_target_pairs={{0,15},{1,0},{2,1},{3,2},{4,3},{5,4},{6,5},{7,6},{8,7},{9,8},{10,9... | collective-permute-start | bytes 393224 | tf_op jit(solution)/shard_map/ppermute | solution.py:290
  40.8 3.1 %adjoint_taps.1.taps = bf16[16,128,320]{2,1,0:T(8,128)(2,1)S(1)} custom-call(s32[6]{0:T(128)S(1)} %stack.41.place, bf16[16,64,512]{2,1,0:T(8,128)(2,1)} %pair_sum.1.after, bf16[4,4,4,256]{3,2,1,0:T(4,128)(2,1)S(1)} %bitcast.17, s32[4,256]{1,0:T(4,128)S(1)} %bitcast.22, s32[4,256]{1,0:T(4,128)S(1)} %bitcast.19), custom_call_target="tpu_custom_call" | custom-call | flops 2000000000 | bytes 2000000 | tf_op jit(solution)/shard_map/adjoint_taps/pallas_call | solution.py:298
  43.9 0.0 collective-permute-done.7.rims_w
  43.9 0.0 collective-permute-done.8.rims_e
  43.9 0.0 copy-done.2
  43.9 0.0 copy-done.7
  43.9 3.9 %output.1 = (bf16[16,32,512]{2,1,0:T(8,128)(2,1)}, f32[8,128]{1,0:T(8,128)S(1)}) custom-call(s32[6]{0:T(128)S(1)} %stack.41.place, bf16[16,64,512]{2,1,0:T(8,128)(2,1)} %pair_sum.1.after, s32[4,256]{1,0:T(4,128)S(1)} %bitcast.23, bf16[20,128,256]{2,1,0:T(8,128)(2,1)S(1)} %copy-done.7, bf16[16,32,512]{2,1,0:T(8,128)(2,1)S(1)} %copy-done, ...), custom_call_target="tpu_custom_call" | custom-call | flops 3000000000 | bytes 6000000 | tf_op jit(solution)/shard_map/output/pallas_call | solution.py:298
  47.9 4.4 %adjoint.1 = (bf16[16,32,512]{2,1,0:T(8,128)(2,1)}, f32[8,128]{1,0:T(8,128)S(1)}) custom-call(s32[6]{0:T(128)S(1)} %stack.41.place, bf16[16,64,512]{2,1,0:T(8,128)(2,1)} %pair_sum.1.after, bf16[16,128,320]{2,1,0:T(8,128)(2,1)S(1)} %adjoint_taps.1.taps, bf16[16,32,512]{2,1,0:T(8,128)(2,1)S(1)} %copy-done.1, ...), custom_call_target="tpu_custom_call" | custom-call | flops 3000000000 | bytes 6000000 | tf_op jit(solution)/shard_map/adjoint/pallas_call | solution.py:298
  52.3 3.1 %all-to-all-done.parts = bf16[16,64,512]{2,1,0:T(8,128)(2,1)S(1)} async-done(((bf16[16,64,512]{2,1,0:T(8,128)(2,1)}), bf16[16,64,512]{2,1,0:T(8,128)(2,1)S(1)}, u32[]{:S(2)}, u32[]{:S(2)}) %all-to-all-start) | async-done | bytes 1048608 | tf_op jit(solution)/shard_map/all_to_all | solution.py:403
  55.4 0.1 chip_sum.1.one
  55.6 0.5 collective-permute-start.10
  56.0 2.6 %collective-permute-start.11 = (bf16[64,512]{1,0:T(8,128)(2,1)S(1)}, bf16[64,512]{1,0:T(8,128)(2,1)S(1)}, u32[]{:S(2)}, u32[]{:S(2)}) collective-permute-start(bf16[64,512]{1,0:T(8,128)(2,1)S(1)} %chip_sum.1.one), channel_id=1, source_target_pairs={{0,6},{1,7},{2,4},{3,5},{4,2},{5,3},{6,0},{7,1},{8,14},{9,15},{10,... | collective-permute-start | bytes 196616 | tf_op jit(solution)/shard_map/ppermute | solution.py:294
  58.6 3.6 %collective-permute-start.9 = (bf16[64,512]{1,0:T(8,128)(2,1)S(1)}, bf16[64,512]{1,0:T(8,128)(2,1)S(1)}, u32[]{:S(2)}, u32[]{:S(2)}) collective-permute-start(bf16[64,512]{1,0:T(8,128)(2,1)S(1)} %chip_sum.1.one), channel_id=1, source_target_pairs={{0,2},{1,3},{2,0},{3,1},{4,6},{5,7},{6,4},{7,5},{8,10},{9,11},{10,... | collective-permute-start | bytes 196616 | tf_op jit(solution)/shard_map/ppermute | solution.py:294
  62.2 2.4 %collective-permute-done.10.three = bf16[64,512]{1,0:T(8,128)(2,1)S(1)} collective-permute-done((bf16[64,512]{1,0:T(8,128)(2,1)S(1)}, bf16[64,512]{1,0:T(8,128)(2,1)S(1)}, u32[]{:S(2)}, u32[]{:S(2)}) %collective-permute-start.10) | collective-permute-done | bytes 65568 | tf_op jit(solution)/shard_map/ppermute | solution.py:294
  64.6 0.0 collective-permute-done.11.four
  64.6 1.4 %collective-permute-done.9.two = bf16[64,512]{1,0:T(8,128)(2,1)S(1)} collective-permute-done((bf16[64,512]{1,0:T(8,128)(2,1)S(1)}, bf16[64,512]{1,0:T(8,128)(2,1)S(1)}, u32[]{:S(2)}, u32[]{:S(2)}) %collective-permute-start.9) | collective-permute-done | bytes 65568 | tf_op jit(solution)/shard_map/ppermute | solution.py:294
  66.0 0.1 collective-permute-start.12
  66.1 1.7 %collective-permute-start.13 = (bf16[64,512]{1,0:T(8,128)(2,1)S(1)}, bf16[64,512]{1,0:T(8,128)(2,1)S(1)}, u32[]{:S(2)}, u32[]{:S(2)}) collective-permute-start(bf16[64,512]{1,0:T(8,128)(2,1)S(1)} %four_sum.1.own), channel_id=1, source_target_pairs={{0,8},{8,0},{1,9},{9,1},{2,10},{10,2},{3,11},{11,3},{4,12},{12,4},... | collective-permute-start | bytes 196616 | tf_op jit(solution)/shard_map/ppermute | solution.py:294
  67.8 1.8 %collective-permute-start.14 = (bf16[64,512]{1,0:T(8,128)(2,1)S(1)}, bf16[64,512]{1,0:T(8,128)(2,1)S(1)}, u32[]{:S(2)}, u32[]{:S(2)}) collective-permute-start(bf16[64,512]{1,0:T(8,128)(2,1)S(1)} %four_sum.1.own), channel_id=1, source_target_pairs={{0,9},{1,8},{2,11},{3,10},{4,13},{5,12},{6,15},{7,14},{8,1},{9,0},... | collective-permute-start | bytes 196616 | tf_op jit(solution)/shard_map/ppermute | solution.py:294
  69.6 0.8 %collective-permute-done.12.by_z = bf16[64,512]{1,0:T(8,128)(2,1)S(1)} collective-permute-done((bf16[64,512]{1,0:T(8,128)(2,1)S(1)}, bf16[64,512]{1,0:T(8,128)(2,1)S(1)}, u32[]{:S(2)}, u32[]{:S(2)}) %collective-permute-start.12) | collective-permute-done | bytes 65568 | tf_op jit(solution)/shard_map/ppermute | solution.py:294
  70.3 0.1 collective-permute-done.13.by_x
  70.4 2.5 %collective-permute-done.14.by_both = bf16[64,512]{1,0:T(8,128)(2,1)S(1)} collective-permute-done((bf16[64,512]{1,0:T(8,128)(2,1)S(1)}, bf16[64,512]{1,0:T(8,128)(2,1)S(1)}, u32[]{:S(2)}, u32[]{:S(2)}) %collective-permute-start.14) | collective-permute-done | bytes 65568 | tf_op jit(solution)/shard_map/ppermute | solution.py:294
  72.9 1.3 %last_sum.1 = f32[4,32,512]{2,1,0:T(8,128)} custom-call(s32[6]{0:T(128)S(1)} %stack.41.place, bf16[64,512]{1,0:T(8,128)(2,1)S(1)} %four_sum.1.own, bf16[64,512]{1,0:T(8,128)(2,1)S(1)} %collective-permute-done.12.by_z, bf16[64,512]{1,0:T(8,128)(2,1)S(1)} %collective-permute-done.13.by_x, bf16[64,512]{1,0:T(8,128)(2,1)S(1)} %collective-permute-done.14.by_both), custom_call_target="tpu_custom_call" | custom-call | flops 131072 | bytes 524288 | tf_op jit(solution)/shard_map/last_sum/pallas_call | solution.py:298
  (3 shorter events, 0.1 us)
Async XLA Ops:
  0.6 11.2 %copy-start.1 = (bf16[16,32,512]{2,1,0:T(8,128)(2,1)S(1)}, bf16[16,32,512]{2,1,0:T(8,128)(2,1)}, u32[]{:S(2)}) copy-start(bf16[16,32,512]{2,1,0:T(8,128)(2,1)} %center.5) | copy-start | bytes 1572868
  0.6 11.4 %copy-start.5 = (s32[256,4]{0,1:T(4,128)S(1)}, s32[256,4]{0,1:T(4,128)}, u32[]{:S(2)}) copy-start(s32[256,4]{0,1:T(4,128)} %param.8) | copy-start | bytes 12292
  0.7 11.4 %copy-start.3 = (bf16[4,256,4,4]{1,3,2,0:T(4,128)(2,1)S(1)}, bf16[4,256,4,4]{1,3,2,0:T(4,128)(2,1)}, u32[]{:S(2)}) copy-start(bf16[4,256,4,4]{1,3,2,0:T(4,128)(2,1)} %param.7) | copy-start | bytes 98308
  0.7 11.4 %copy-start.4 = (s32[256,4]{0,1:T(4,128)S(1)}, s32[256,4]{0,1:T(4,128)}, u32[]{:S(2)}) copy-start(s32[256,4]{0,1:T(4,128)} %param.9) | copy-start | bytes 12292
  3.2 10.3 %collective-permute-start.4 = (bf16[2,2,32,512]{3,2,1,0:T(8,128)(2,1)S(1)}, bf16[2,2,32,512]{3,2,1,0:T(8,128)(2,1)S(1)}, u32[]{:S(2)}, u32[]{:S(2)}) collective-permute-start(bf16[2,2,32,512]{3,2,1,0:T(8,128)(2,1)S(1)} %get-tuple-element.28), channel_id=1, source_target_pairs={{0,16},{16,0},{32,48},{48,32},{64,80},{80,64},{96,112},{112,96},{1... | collective-permute-start | bytes 393224 | tf_op jit(solution)/shard_map/ppermute | solution.py:294
  3.2 14.5 %collective-permute-start.5 = (bf16[2,2,32,512]{3,2,1,0:T(8,128)(2,1)}, bf16[2,2,32,512]{3,2,1,0:T(8,128)(2,1)S(1)}, u32[]{:S(2)}, u32[]{:S(2)}) collective-permute-start(bf16[2,2,32,512]{3,2,1,0:T(8,128)(2,1)} %get-tuple-element.27), channel_id=1, source_target_pairs={{0,0},{240,240},{16,32},{32,16},{48,64},{64,48},{80,96},{96,80},{1... | collective-permute-start | bytes 393224 | tf_op jit(solution)/shard_map/ppermute | solution.py:356
  5.8 11.9 %collective-permute-start.2 = (bf16[16,16,512]{2,1,0:T(8,128)(2,1)S(1)}, bf16[16,16,512]{2,1,0:T(8,128)(2,1)S(1)}, u32[]{:S(2)}, u32[]{:S(2)}) collective-permute-start(bf16[16,16,512]{2,1,0:T(8,128)(2,1)S(1)} %get-tuple-element.24), channel_id=1, source_target_pairs={{0,1},{1,2},{2,3},{3,4},{4,5},{5,6},{6,7},{7,8},{8,9},{9,10},{10,1... | collective-permute-start | bytes 786440 | tf_op jit(solution)/shard_map/ppermute | solution.py:290
  7.8 9.9 %collective-permute-start.3 = (bf16[16,16,512]{2,1,0:T(8,128)(2,1)S(1)}, bf16[16,16,512]{2,1,0:T(8,128)(2,1)S(1)}, u32[]{:S(2)}, u32[]{:S(2)}) collective-permute-start(bf16[16,16,512]{2,1,0:T(8,128)(2,1)S(1)} %get-tuple-element.23), channel_id=1, source_target_pairs={{0,15},{1,0},{2,1},{3,2},{4,3},{5,4},{6,5},{7,6},{8,7},{9,8},{10,9... | collective-permute-start | bytes 786440 | tf_op jit(solution)/shard_map/ppermute | solution.py:290
  11.8 5.9 %copy-start = (bf16[16,32,512]{2,1,0:T(8,128)(2,1)S(1)}, bf16[16,32,512]{2,1,0:T(8,128)(2,1)}, u32[]{:S(2)}) copy-start(bf16[16,32,512]{2,1,0:T(8,128)(2,1)} %center.4) | copy-start | bytes 1572868
  11.9 11.8 %collective-permute-start = (bf16[16,16,512]{2,1,0:T(8,128)(2,1)S(1)}, bf16[16,16,512]{2,1,0:T(8,128)(2,1)S(1)}, u32[]{:S(2)}, u32[]{:S(2)}) collective-permute-start(bf16[16,16,512]{2,1,0:T(8,128)(2,1)S(1)} %get-tuple-element.26), channel_id=1, source_target_pairs={{0,1},{1,2},{2,3},{3,4},{4,5},{5,6},{6,7},{7,8},{8,9},{9,10},{10,1... | collective-permute-start | bytes 786440 | tf_op jit(solution)/shard_map/ppermute | solution.py:290
  13.5 7.4 %copy-start.6 = (bf16[20,128,256]{2,1,0:T(8,128)(2,1)}, bf16[20,128,256]{2,1,0:T(8,128)(2,1)S(1)}, u32[]{:S(2)}) copy-start(bf16[20,128,256]{2,1,0:T(8,128)(2,1)S(1)} %forward_taps.1.taps) | copy-start | bytes 3932164
  13.5 10.2 %collective-permute-start.1 = (bf16[16,16,512]{2,1,0:T(8,128)(2,1)S(1)}, bf16[16,16,512]{2,1,0:T(8,128)(2,1)S(1)}, u32[]{:S(2)}, u32[]{:S(2)}) collective-permute-start(bf16[16,16,512]{2,1,0:T(8,128)(2,1)S(1)} %get-tuple-element.25), channel_id=1, source_target_pairs={{0,15},{1,0},{2,1},{3,2},{4,3},{5,4},{6,5},{7,6},{8,7},{9,8},{10,9... | collective-permute-start | bytes 786440 | tf_op jit(solution)/shard_map/ppermute | solution.py:290
  20.9 5.0 %collective-permute-start.6 = (bf16[16,64,512]{2,1,0:T(8,128)(2,1)S(1)}, bf16[16,64,512]{2,1,0:T(8,128)(2,1)S(1)}, u32[]{:S(2)}, u32[]{:S(2)}) collective-permute-start(bf16[16,64,512]{2,1,0:T(8,128)(2,1)S(1)} %get-tuple-element.12), channel_id=1, source_target_pairs={{0,16},{16,0},{1,17},{17,1},{2,18},{18,2},{3,19},{19,3},{4,20},{20... | collective-permute-start | bytes 3145736 | tf_op jit(solution)/shard_map/ppermute | solution.py:294
  27.2 28.2 %all-to-all-start = ((bf16[16,64,512]{2,1,0:T(8,128)(2,1)}), bf16[16,64,512]{2,1,0:T(8,128)(2,1)S(1)}, u32[]{:S(2)}, u32[]{:S(2)}) async-start(bf16[16,64,512]{2,1,0:T(8,128)(2,1)} %pair_sum.1.after), calls=%async_computation | async-start | bytes 2097152 | tf_op jit(solution)/shard_map/all_to_all | solution.py:403
  36.6 7.3 %collective-permute-start.7 = (bf16[2,2,2,16,512]{4,3,2,1,0:T(8,128)(2,1)S(1)}, bf16[2,2,2,16,512]{4,3,2,1,0:T(8,128)(2,1)S(1)}, u32[]{:S(2)}, u32[]{:S(2)}) collective-permute-start(bf16[2,2,2,16,512]{4,3,2,1,0:T(8,128)(2,1)S(1)} %get-tuple-element.13), channel_id=1, source_target_pairs={{0,1},{1,2},{2,3},{3,4},{4,5},{5,6},{6,7},{7,8},{8,9},{9,10},{10,1... | collective-permute-start | bytes 393224 | tf_op jit(solution)/shard_map/ppermute | solution.py:290
  36.7 7.2 %copy-start.2 = (bf16[4,512,512]{2,1,0:T(8,128)(2,1)S(1)}, bf16[4,512,512]{2,1,0:T(8,128)(2,1)}, u32[]{:S(2)}) copy-start(bf16[4,512,512]{2,1,0:T(8,128)(2,1)} %mixing.3) | copy-start | bytes 6291460
  36.7 7.2 %copy-start.7 = (bf16[20,128,256]{2,1,0:T(8,128)(2,1)S(1)}, bf16[20,128,256]{2,1,0:T(8,128)(2,1)}, u32[]{:S(2)}) copy-start(bf16[20,128,256]{2,1,0:T(8,128)(2,1)} %copy-done.6) | copy-start | bytes 3932164
  36.7 7.2 %collective-permute-start.8 = (bf16[2,2,2,16,512]{4,3,2,1,0:T(8,128)(2,1)S(1)}, bf16[2,2,2,16,512]{4,3,2,1,0:T(8,128)(2,1)S(1)}, u32[]{:S(2)}, u32[]{:S(2)}) collective-permute-start(bf16[2,2,2,16,512]{4,3,2,1,0:T(8,128)(2,1)S(1)} %get-tuple-element.14), channel_id=1, source_target_pairs={{0,15},{1,0},{2,1},{3,2},{4,3},{5,4},{6,5},{7,6},{8,7},{9,8},{10,9... | collective-permute-start | bytes 393224 | tf_op jit(solution)/shard_map/ppermute | solution.py:290
  55.6 9.0 %collective-permute-start.10 = (bf16[64,512]{1,0:T(8,128)(2,1)S(1)}, bf16[64,512]{1,0:T(8,128)(2,1)S(1)}, u32[]{:S(2)}, u32[]{:S(2)}) collective-permute-start(bf16[64,512]{1,0:T(8,128)(2,1)S(1)} %chip_sum.1.one), channel_id=1, source_target_pairs={{0,4},{1,5},{2,6},{3,7},{4,0},{5,1},{6,2},{7,3},{8,12},{9,13},{10,... | collective-permute-start | bytes 196616 | tf_op jit(solution)/shard_map/ppermute | solution.py:294
  56.0 8.5 %collective-permute-start.11 = (bf16[64,512]{1,0:T(8,128)(2,1)S(1)}, bf16[64,512]{1,0:T(8,128)(2,1)S(1)}, u32[]{:S(2)}, u32[]{:S(2)}) collective-permute-start(bf16[64,512]{1,0:T(8,128)(2,1)S(1)} %chip_sum.1.one), channel_id=1, source_target_pairs={{0,6},{1,7},{2,4},{3,5},{4,2},{5,3},{6,0},{7,1},{8,14},{9,15},{10,... | collective-permute-start | bytes 196616 | tf_op jit(solution)/shard_map/ppermute | solution.py:294
  58.6 7.4 %collective-permute-start.9 = (bf16[64,512]{1,0:T(8,128)(2,1)S(1)}, bf16[64,512]{1,0:T(8,128)(2,1)S(1)}, u32[]{:S(2)}, u32[]{:S(2)}) collective-permute-start(bf16[64,512]{1,0:T(8,128)(2,1)S(1)} %chip_sum.1.one), channel_id=1, source_target_pairs={{0,2},{1,3},{2,0},{3,1},{4,6},{5,7},{6,4},{7,5},{8,10},{9,11},{10,... | collective-permute-start | bytes 196616 | tf_op jit(solution)/shard_map/ppermute | solution.py:294
  66.0 4.4 %collective-permute-start.12 = (bf16[64,512]{1,0:T(8,128)(2,1)S(1)}, bf16[64,512]{1,0:T(8,128)(2,1)S(1)}, u32[]{:S(2)}, u32[]{:S(2)}) collective-permute-start(bf16[64,512]{1,0:T(8,128)(2,1)S(1)} %four_sum.1.own), channel_id=1, source_target_pairs={{0,1},{1,0},{2,3},{3,2},{4,5},{5,4},{6,7},{7,6},{8,9},{9,8},{10,11... | collective-permute-start | bytes 196616 | tf_op jit(solution)/shard_map/ppermute | solution.py:294
  66.1 4.3 %collective-permute-start.13 = (bf16[64,512]{1,0:T(8,128)(2,1)S(1)}, bf16[64,512]{1,0:T(8,128)(2,1)S(1)}, u32[]{:S(2)}, u32[]{:S(2)}) collective-permute-start(bf16[64,512]{1,0:T(8,128)(2,1)S(1)} %four_sum.1.own), channel_id=1, source_target_pairs={{0,8},{8,0},{1,9},{9,1},{2,10},{10,2},{3,11},{11,3},{4,12},{12,4},... | collective-permute-start | bytes 196616 | tf_op jit(solution)/shard_map/ppermute | solution.py:294
  67.8 5.2 %collective-permute-start.14 = (bf16[64,512]{1,0:T(8,128)(2,1)S(1)}, bf16[64,512]{1,0:T(8,128)(2,1)S(1)}, u32[]{:S(2)}, u32[]{:S(2)}) collective-permute-start(bf16[64,512]{1,0:T(8,128)(2,1)S(1)} %four_sum.1.own), channel_id=1, source_target_pairs={{0,9},{1,8},{2,11},{3,10},{4,13},{5,12},{6,15},{7,14},{8,1},{9,0},... | collective-permute-start | bytes 196616 | tf_op jit(solution)/shard_map/ppermute | solution.py:294

commit v7 on v6

--- a/solution.py
+++ b/solution.py
@@ -114,7 +114,7 @@
         store_bands(adjoint, row, total, basis_count, count, taps)
         return carry
 
-    lax.fori_loop(0, rows, one_row, 0, unroll=4)
+    lax.fori_loop(0, rows, one_row, 0, unroll=16)
 
 
 def rims_kernel(place, inner, outer, to_east, to_west):

time: 74.6 us -> 74.6 us (level)
  transfers between devices with their start and end apart: 16 -> 16, of which waited for: 7 -> 8; matrix products, arithmetic and copies ran while one was open for 2% -> 2% of each run, Pallas kernels for 22% -> 22%
where the time goes in v7:
time: 74.6 us; the launch traced here: 74.2 us
  starting transfers between devices  37.7 us (51%)
  Pallas kernels  18.7 us (25%)
  waiting for transfers between devices  13.2 us (18%)
  local copies, waits for them, and re-layouts  3.04 us (4%)
  between operations  0.84 us (1%)
    pallas_call x11, Pallas kernels, call(): pl.pallas_call(kernel, out_shape=outs, in_specs=specs, out_specs=jax.tree...  18.7 us
    ppermute x6, starting transfers between devices, shift(): lax.ppermute(cells, axis, [(i, (i + step) % count) for i in range(count)])  14.4 us
    ppermute x8, starting transfers between devices, swap(): return lax.ppermute(cells, axis, [(i, i ^ mask) for i in range(count)])  12.9 us
    ppermute x8, waiting for transfers between devices, swap(): return lax.ppermute(cells, axis, [(i, i ^ mask) for i in range(count)])  9.44 us
    all_to_all x1, starting transfers between devices, local(): parts = lax.all_to_all(summed, ('y', 'xh', 'xl'), 0, 0)  8.82 us
    all_to_all x1, waiting for transfers between devices, local(): parts = lax.all_to_all(summed, ('y', 'xh', 'xl'), 0, 0)  3.11 us
    another operation x2, local copies, waits for them, and re-layouts, local(): top = jnp.stack([cells[:HL] for cells in both])  1.82 us
    ppermute x1, starting transfers between devices, local(): outer = lax.ppermute(outer, LAT, pairs)  1.55 us
  transfers between devices with their start and end apart: 16, of which 8 were waited for; matrix products, arithmetic and copies ran while one was open for 2% of the time, Pallas kernels for 22%

profile of v7, /device:TPU:2, one launch (start us, length us, event | category | flops | bytes accessed | tf_op | source)
XLA Modules:
  0.0 74.2 jit_solution(11948019598486771327)
XLA Ops:
  0.6 0.0 copy-start.1
  0.6 0.0 copy-start.5
  0.7 0.0 copy-start.3
  0.7 0.0 copy-start.4
  0.7 0.9 %slice_bitcast_fusion.3 = (bf16[1,2,32,512]{3,2,1,0:T(8,128)(2,1)S(1)}, bf16[1,2,32,512]{3,2,1,0:T(8,128)(2,1)S(1)}) fusion(bf16[16,32,512]{2,1,0:T(8,128)(2,1)} %center.4), kind=kLoop, calls=%fused_computation.7 | loop fusion | bytes 262144 | tf_op jit(solution)/shard_map/stack | solution.py:331
  1.6 0.9 %slice_bitcast_fusion.2 = (bf16[1,2,32,512]{3,2,1,0:T(8,128)(2,1)S(1)}, bf16[1,2,32,512]{3,2,1,0:T(8,128)(2,1)S(1)}) fusion(bf16[16,32,512]{2,1,0:T(8,128)(2,1)} %center.5), kind=kLoop, calls=%fused_computation.6 | loop fusion | bytes 262144 | tf_op jit(solution)/shard_map/stack | solution.py:331
  2.5 0.7 broadcast_select_fusion
  3.2 0.0 collective-permute-start.4
  3.2 1.6 %collective-permute-start.5 = (bf16[2,2,32,512]{3,2,1,0:T(8,128)(2,1)}, bf16[2,2,32,512]{3,2,1,0:T(8,128)(2,1)S(1)}, u32[]{:S(2)}, u32[]{:S(2)}) collective-permute-start(bf16[2,2,32,512]{3,2,1,0:T(8,128)(2,1)} %get-tuple-element.27), channel_id=1, source_target_pairs={{0,0},{240,240},{16,32},{32,16},{48,64},{64,48},{80,96},{96,80},{1... | collective-permute-start | bytes 393224 | tf_op jit(solution)/shard_map/ppermute | solution.py:356
  4.7 1.1 %fusion = (bf16[16,16,512]{2,1,0:T(8,128)(2,1)S(1)}, bf16[16,16,512]{2,1,0:T(8,128)(2,1)S(1)}) fusion(bf16[16,32,512]{2,1,0:T(8,128)(2,1)} %center.4), kind=kLoop, calls=%fused_computation.8 | loop fusion | bytes 1048576 | tf_op jit(solution)/shard_map/slice | solution.py:336
  5.8 2.0 %collective-permute-start.2 = (bf16[16,16,512]{2,1,0:T(8,128)(2,1)S(1)}, bf16[16,16,512]{2,1,0:T(8,128)(2,1)S(1)}, u32[]{:S(2)}, u32[]{:S(2)}) collective-permute-start(bf16[16,16,512]{2,1,0:T(8,128)(2,1)S(1)} %get-tuple-element.24), channel_id=1, source_target_pairs={{0,1},{1,2},{2,3},{3,4},{4,5},{5,6},{6,7},{7,8},{8,9},{9,10},{10,1... | collective-permute-start | bytes 786440 | tf_op jit(solution)/shard_map/ppermute | solution.py:290
  7.8 4.0 %collective-permute-start.3 = (bf16[16,16,512]{2,1,0:T(8,128)(2,1)S(1)}, bf16[16,16,512]{2,1,0:T(8,128)(2,1)S(1)}, u32[]{:S(2)}, u32[]{:S(2)}) collective-permute-start(bf16[16,16,512]{2,1,0:T(8,128)(2,1)S(1)} %get-tuple-element.23), channel_id=1, source_target_pairs={{0,15},{1,0},{2,1},{3,2},{4,3},{5,4},{6,5},{7,6},{8,7},{9,8},{10,9... | collective-permute-start | bytes 786440 | tf_op jit(solution)/shard_map/ppermute | solution.py:290
  11.8 0.0 copy-done.1
  11.8 0.0 copy-start
  11.9 0.1 collective-permute-start
  12.0 0.1 stack.41.place
  12.1 0.0 copy-done.5
  12.1 0.0 copy-done.3
  12.1 0.0 copy-done.4
  12.1 1.4 %forward_taps.1.taps = bf16[20,128,256]{2,1,0:T(8,128)(2,1)S(1)} custom-call(s32[6]{0:T(128)S(1)} %stack.41.place, bf16[4,4,4,256]{3,2,1,0:T(4,128)(2,1)S(1)} %bitcast.16, s32[4,256]{1,0:T(4,128)S(1)} %bitcast.20, s32[4,256]{1,0:T(4,128)S(1)} %bitcast.18), custom_call_target="tpu_custom_call" | custom-call | flops 1000000000 | bytes 1000000 | tf_op jit(solution)/shard_map/forward_taps/pallas_call | solution.py:298
  13.5 0.0 copy-start.6
  13.5 0.0 collective-permute-done.4.inner
  13.5 4.2 %collective-permute-start.1 = (bf16[16,16,512]{2,1,0:T(8,128)(2,1)S(1)}, bf16[16,16,512]{2,1,0:T(8,128)(2,1)S(1)}, u32[]{:S(2)}, u32[]{:S(2)}) collective-permute-start(bf16[16,16,512]{2,1,0:T(8,128)(2,1)S(1)} %get-tuple-element.25), channel_id=1, source_target_pairs={{0,15},{1,0},{2,1},{3,2},{4,3},{5,4},{6,5},{7,6},{8,7},{9,8},{10,9... | collective-permute-start | bytes 786440 | tf_op jit(solution)/shard_map/ppermute | solution.py:290
  17.7 0.0 collective-permute-done.5.outer
  17.7 0.0 collective-permute-done.2.west
  17.7 0.0 collective-permute-done.3.east
  17.7 0.0 copy-done
  17.7 3.2 %terms.1 = (f32[16,64,512]{2,1,0:T(8,128)S(1)}, bf16[16,64,512]{2,1,0:T(8,128)(2,1)S(1)}) custom-call(s32[6]{0:T(128)S(1)} %stack.41.place, s32[4,256]{1,0:T(4,128)S(1)} %bitcast.21, bf16[20,128,256]{2,1,0:T(8,128)(2,1)S(1)} %forward_taps.1.taps, bf16[16,32,512]{2,1,0:T(8,128)(2,1)S(1)} %copy-done, bf16[16,16,512]{2,1,0:T(8,128)(2,1)S(1)} %collective-permute-done.2.west, ...), custom_call_target="tpu_custom_call" | custom-call | flops 20000000000 | bytes 8000000 | tf_op jit(solution)/shard_map/terms/pallas_call | solution.py:298
  20.9 0.0 copy-done.6
  20.9 2.7 %collective-permute-start.6 = (bf16[16,64,512]{2,1,0:T(8,128)(2,1)S(1)}, bf16[16,64,512]{2,1,0:T(8,128)(2,1)S(1)}, u32[]{:S(2)}, u32[]{:S(2)}) collective-permute-start(bf16[16,64,512]{2,1,0:T(8,128)(2,1)S(1)} %get-tuple-element.12), channel_id=1, source_target_pairs={{0,16},{16,0},{1,17},{17,1},{2,18},{18,2},{3,19},{19,3},{4,20},{20... | collective-permute-start | bytes 3145736 | tf_op jit(solution)/shard_map/ppermute | solution.py:294
  23.7 0.0 collective-permute-done.west
  23.7 0.0 collective-permute-done.1.east
  23.7 2.3 %collective-permute-done.6.recv = bf16[16,64,512]{2,1,0:T(8,128)(2,1)S(1)} collective-permute-done((bf16[16,64,512]{2,1,0:T(8,128)(2,1)S(1)}, bf16[16,64,512]{2,1,0:T(8,128)(2,1)S(1)}, u32[]{:S(2)}, u32[]{:S(2)}) %collective-permute-start.6) | collective-permute-done | bytes 1048608 | tf_op jit(solution)/shard_map/ppermute | solution.py:294
  26.0 1.2 %pair_sum.1.after = bf16[16,64,512]{2,1,0:T(8,128)(2,1)} custom-call(f32[8,128]{1,0:T(8,128)S(1)} %ready.1.after, f32[16,64,512]{2,1,0:T(8,128)S(1)} %get-tuple-element.11.keep, bf16[16,64,512]{2,1,0:T(8,128)(2,1)S(1)} %collective-permute-done.6.recv), custom_call_target="tpu_custom_call" | custom-call | flops 524288 | bytes 4194304 | tf_op jit(solution)/shard_map/pair_sum/pallas_call | solution.py:298
  27.2 8.8 %all-to-all-start = ((bf16[16,64,512]{2,1,0:T(8,128)(2,1)}), bf16[16,64,512]{2,1,0:T(8,128)(2,1)S(1)}, u32[]{:S(2)}, u32[]{:S(2)}) async-start(bf16[16,64,512]{2,1,0:T(8,128)(2,1)} %pair_sum.1.after), calls=%async_computation | async-start | bytes 2097152 | tf_op jit(solution)/shard_map/all_to_all | solution.py:403
  36.0 0.6 rims.1
  36.6 0.1 collective-permute-start.7
  36.7 0.0 copy-start.2
  36.7 0.0 copy-start.7
  36.7 4.1 %collective-permute-start.8 = (bf16[2,2,2,16,512]{4,3,2,1,0:T(8,128)(2,1)S(1)}, bf16[2,2,2,16,512]{4,3,2,1,0:T(8,128)(2,1)S(1)}, u32[]{:S(2)}, u32[]{:S(2)}) collective-permute-start(bf16[2,2,2,16,512]{4,3,2,1,0:T(8,128)(2,1)S(1)} %get-tuple-element.14), channel_id=1, source_target_pairs={{0,15},{1,0},{2,1},{3,2},{4,3},{5,4},{6,5},{7,6},{8,7},{9,8},{10,9... | collective-permute-start | bytes 393224 | tf_op jit(solution)/shard_map/ppermute | solution.py:290
  40.8 2.5 %adjoint_taps.1.taps = bf16[16,128,320]{2,1,0:T(8,128)(2,1)S(1)} custom-call(s32[6]{0:T(128)S(1)} %stack.41.place, bf16[16,64,512]{2,1,0:T(8,128)(2,1)} %pair_sum.1.after, bf16[4,4,4,256]{3,2,1,0:T(4,128)(2,1)S(1)} %bitcast.17, s32[4,256]{1,0:T(4,128)S(1)} %bitcast.22, s32[4,256]{1,0:T(4,128)S(1)} %bitcast.19), custom_call_target="tpu_custom_call" | custom-call | flops 2000000000 | bytes 2000000 | tf_op jit(solution)/shard_map/adjoint_taps/pallas_call | solution.py:298
  43.3 0.6 collective-permute-done.7.rims_w
  43.9 0.0 collective-permute-done.8.rims_e
  43.9 0.0 copy-done.2
  43.9 0.0 copy-done.7
  43.9 3.9 %output.1 = (bf16[16,32,512]{2,1,0:T(8,128)(2,1)}, f32[8,128]{1,0:T(8,128)S(1)}) custom-call(s32[6]{0:T(128)S(1)} %stack.41.place, bf16[16,64,512]{2,1,0:T(8,128)(2,1)} %pair_sum.1.after, s32[4,256]{1,0:T(4,128)S(1)} %bitcast.23, bf16[20,128,256]{2,1,0:T(8,128)(2,1)S(1)} %copy-done.7, bf16[16,32,512]{2,1,0:T(8,128)(2,1)S(1)} %copy-done, ...), custom_call_target="tpu_custom_call" | custom-call | flops 3000000000 | bytes 6000000 | tf_op jit(solution)/shard_map/output/pallas_call | solution.py:298
  47.9 4.4 %adjoint.1 = (bf16[16,32,512]{2,1,0:T(8,128)(2,1)}, f32[8,128]{1,0:T(8,128)S(1)}) custom-call(s32[6]{0:T(128)S(1)} %stack.41.place, bf16[16,64,512]{2,1,0:T(8,128)(2,1)} %pair_sum.1.after, bf16[16,128,320]{2,1,0:T(8,128)(2,1)S(1)} %adjoint_taps.1.taps, bf16[16,32,512]{2,1,0:T(8,128)(2,1)S(1)} %copy-done.1, ...), custom_call_target="tpu_custom_call" | custom-call | flops 3000000000 | bytes 6000000 | tf_op jit(solution)/shard_map/adjoint/pallas_call | solution.py:298
  52.3 3.1 %all-to-all-done.parts = bf16[16,64,512]{2,1,0:T(8,128)(2,1)S(1)} async-done(((bf16[16,64,512]{2,1,0:T(8,128)(2,1)}), bf16[16,64,512]{2,1,0:T(8,128)(2,1)S(1)}, u32[]{:S(2)}, u32[]{:S(2)}) %all-to-all-start) | async-done | bytes 1048608 | tf_op jit(solution)/shard_map/all_to_all | solution.py:403
  55.4 0.1 chip_sum.1.one
  55.6 0.5 collective-permute-start.10
  56.0 2.6 %collective-permute-start.11 = (bf16[64,512]{1,0:T(8,128)(2,1)S(1)}, bf16[64,512]{1,0:T(8,128)(2,1)S(1)}, u32[]{:S(2)}, u32[]{:S(2)}) collective-permute-start(bf16[64,512]{1,0:T(8,128)(2,1)S(1)} %chip_sum.1.one), channel_id=1, source_target_pairs={{0,6},{1,7},{2,4},{3,5},{4,2},{5,3},{6,0},{7,1},{8,14},{9,15},{10,... | collective-permute-start | bytes 196616 | tf_op jit(solution)/shard_map/ppermute | solution.py:294
  58.6 3.6 %collective-permute-start.9 = (bf16[64,512]{1,0:T(8,128)(2,1)S(1)}, bf16[64,512]{1,0:T(8,128)(2,1)S(1)}, u32[]{:S(2)}, u32[]{:S(2)}) collective-permute-start(bf16[64,512]{1,0:T(8,128)(2,1)S(1)} %chip_sum.1.one), channel_id=1, source_target_pairs={{0,2},{1,3},{2,0},{3,1},{4,6},{5,7},{6,4},{7,5},{8,10},{9,11},{10,... | collective-permute-start | bytes 196616 | tf_op jit(solution)/shard_map/ppermute | solution.py:294
  62.2 2.4 %collective-permute-done.10.three = bf16[64,512]{1,0:T(8,128)(2,1)S(1)} collective-permute-done((bf16[64,512]{1,0:T(8,128)(2,1)S(1)}, bf16[64,512]{1,0:T(8,128)(2,1)S(1)}, u32[]{:S(2)}, u32[]{:S(2)}) %collective-permute-start.10) | collective-permute-done | bytes 65568 | tf_op jit(solution)/shard_map/ppermute | solution.py:294
  64.6 0.0 collective-permute-done.11.four
  64.6 1.4 %collective-permute-done.9.two = bf16[64,512]{1,0:T(8,128)(2,1)S(1)} collective-permute-done((bf16[64,512]{1,0:T(8,128)(2,1)S(1)}, bf16[64,512]{1,0:T(8,128)(2,1)S(1)}, u32[]{:S(2)}, u32[]{:S(2)}) %collective-permute-start.9) | collective-permute-done | bytes 65568 | tf_op jit(solution)/shard_map/ppermute | solution.py:294
  66.0 0.1 collective-permute-start.12
  66.1 1.7 %collective-permute-start.13 = (bf16[64,512]{1,0:T(8,128)(2,1)S(1)}, bf16[64,512]{1,0:T(8,128)(2,1)S(1)}, u32[]{:S(2)}, u32[]{:S(2)}) collective-permute-start(bf16[64,512]{1,0:T(8,128)(2,1)S(1)} %four_sum.1.own), channel_id=1, source_target_pairs={{0,8},{8,0},{1,9},{9,1},{2,10},{10,2},{3,11},{11,3},{4,12},{12,4},... | collective-permute-start | bytes 196616 | tf_op jit(solution)/shard_map/ppermute | solution.py:294
  67.8 1.8 %collective-permute-start.14 = (bf16[64,512]{1,0:T(8,128)(2,1)S(1)}, bf16[64,512]{1,0:T(8,128)(2,1)S(1)}, u32[]{:S(2)}, u32[]{:S(2)}) collective-permute-start(bf16[64,512]{1,0:T(8,128)(2,1)S(1)} %four_sum.1.own), channel_id=1, source_target_pairs={{0,9},{1,8},{2,11},{3,10},{4,13},{5,12},{6,15},{7,14},{8,1},{9,0},... | collective-permute-start | bytes 196616 | tf_op jit(solution)/shard_map/ppermute | solution.py:294
  69.6 0.8 %collective-permute-done.12.by_z = bf16[64,512]{1,0:T(8,128)(2,1)S(1)} collective-permute-done((bf16[64,512]{1,0:T(8,128)(2,1)S(1)}, bf16[64,512]{1,0:T(8,128)(2,1)S(1)}, u32[]{:S(2)}, u32[]{:S(2)}) %collective-permute-start.12) | collective-permute-done | bytes 65568 | tf_op jit(solution)/shard_map/ppermute | solution.py:294
  70.3 0.1 collective-permute-done.13.by_x
  70.4 2.5 %collective-permute-done.14.by_both = bf16[64,512]{1,0:T(8,128)(2,1)S(1)} collective-permute-done((bf16[64,512]{1,0:T(8,128)(2,1)S(1)}, bf16[64,512]{1,0:T(8,128)(2,1)S(1)}, u32[]{:S(2)}, u32[]{:S(2)}) %collective-permute-start.14) | collective-permute-done | bytes 65568 | tf_op jit(solution)/shard_map/ppermute | solution.py:294
  72.9 1.3 %last_sum.1 = f32[4,32,512]{2,1,0:T(8,128)} custom-call(s32[6]{0:T(128)S(1)} %stack.41.place, bf16[64,512]{1,0:T(8,128)(2,1)S(1)} %four_sum.1.own, bf16[64,512]{1,0:T(8,128)(2,1)S(1)} %collective-permute-done.12.by_z, bf16[64,512]{1,0:T(8,128)(2,1)S(1)} %collective-permute-done.13.by_x, bf16[64,512]{1,0:T(8,128)(2,1)S(1)} %collective-permute-done.14.by_both), custom_call_target="tpu_custom_call" | custom-call | flops 131072 | bytes 524288 | tf_op jit(solution)/shard_map/last_sum/pallas_call | solution.py:298
  (3 shorter events, 0.1 us)
Async XLA Ops:
  0.6 11.2 %copy-start.1 = (bf16[16,32,512]{2,1,0:T(8,128)(2,1)S(1)}, bf16[16,32,512]{2,1,0:T(8,128)(2,1)}, u32[]{:S(2)}) copy-start(bf16[16,32,512]{2,1,0:T(8,128)(2,1)} %center.5) | copy-start | bytes 1572868
  0.6 11.4 %copy-start.5 = (s32[256,4]{0,1:T(4,128)S(1)}, s32[256,4]{0,1:T(4,128)}, u32[]{:S(2)}) copy-start(s32[256,4]{0,1:T(4,128)} %param.8) | copy-start | bytes 12292
  0.7 11.4 %copy-start.3 = (bf16[4,256,4,4]{1,3,2,0:T(4,128)(2,1)S(1)}, bf16[4,256,4,4]{1,3,2,0:T(4,128)(2,1)}, u32[]{:S(2)}) copy-start(bf16[4,256,4,4]{1,3,2,0:T(4,128)(2,1)} %param.7) | copy-start | bytes 98308
  0.7 11.4 %copy-start.4 = (s32[256,4]{0,1:T(4,128)S(1)}, s32[256,4]{0,1:T(4,128)}, u32[]{:S(2)}) copy-start(s32[256,4]{0,1:T(4,128)} %param.9) | copy-start | bytes 12292
  3.2 10.3 %collective-permute-start.4 = (bf16[2,2,32,512]{3,2,1,0:T(8,128)(2,1)S(1)}, bf16[2,2,32,512]{3,2,1,0:T(8,128)(2,1)S(1)}, u32[]{:S(2)}, u32[]{:S(2)}) collective-permute-start(bf16[2,2,32,512]{3,2,1,0:T(8,128)(2,1)S(1)} %get-tuple-element.28), channel_id=1, source_target_pairs={{0,16},{16,0},{32,48},{48,32},{64,80},{80,64},{96,112},{112,96},{1... | collective-permute-start | bytes 393224 | tf_op jit(solution)/shard_map/ppermute | solution.py:294
  3.2 14.5 %collective-permute-start.5 = (bf16[2,2,32,512]{3,2,1,0:T(8,128)(2,1)}, bf16[2,2,32,512]{3,2,1,0:T(8,128)(2,1)S(1)}, u32[]{:S(2)}, u32[]{:S(2)}) collective-permute-start(bf16[2,2,32,512]{3,2,1,0:T(8,128)(2,1)} %get-tuple-element.27), channel_id=1, source_target_pairs={{0,0},{240,240},{16,32},{32,16},{48,64},{64,48},{80,96},{96,80},{1... | collective-permute-start | bytes 393224 | tf_op jit(solution)/shard_map/ppermute | solution.py:356
  5.8 11.9 %collective-permute-start.2 = (bf16[16,16,512]{2,1,0:T(8,128)(2,1)S(1)}, bf16[16,16,512]{2,1,0:T(8,128)(2,1)S(1)}, u32[]{:S(2)}, u32[]{:S(2)}) collective-permute-start(bf16[16,16,512]{2,1,0:T(8,128)(2,1)S(1)} %get-tuple-element.24), channel_id=1, source_target_pairs={{0,1},{1,2},{2,3},{3,4},{4,5},{5,6},{6,7},{7,8},{8,9},{9,10},{10,1... | collective-permute-start | bytes 786440 | tf_op jit(solution)/shard_map/ppermute | solution.py:290
  7.8 9.9 %collective-permute-start.3 = (bf16[16,16,512]{2,1,0:T(8,128)(2,1)S(1)}, bf16[16,16,512]{2,1,0:T(8,128)(2,1)S(1)}, u32[]{:S(2)}, u32[]{:S(2)}) collective-permute-start(bf16[16,16,512]{2,1,0:T(8,128)(2,1)S(1)} %get-tuple-element.23), channel_id=1, source_target_pairs={{0,15},{1,0},{2,1},{3,2},{4,3},{5,4},{6,5},{7,6},{8,7},{9,8},{10,9... | collective-permute-start | bytes 786440 | tf_op jit(solution)/shard_map/ppermute | solution.py:290
  11.8 5.9 %copy-start = (bf16[16,32,512]{2,1,0:T(8,128)(2,1)S(1)}, bf16[16,32,512]{2,1,0:T(8,128)(2,1)}, u32[]{:S(2)}) copy-start(bf16[16,32,512]{2,1,0:T(8,128)(2,1)} %center.4) | copy-start | bytes 1572868
  11.9 11.8 %collective-permute-start = (bf16[16,16,512]{2,1,0:T(8,128)(2,1)S(1)}, bf16[16,16,512]{2,1,0:T(8,128)(2,1)S(1)}, u32[]{:S(2)}, u32[]{:S(2)}) collective-permute-start(bf16[16,16,512]{2,1,0:T(8,128)(2,1)S(1)} %get-tuple-element.26), channel_id=1, source_target_pairs={{0,1},{1,2},{2,3},{3,4},{4,5},{5,6},{6,7},{7,8},{8,9},{9,10},{10,1... | collective-permute-start | bytes 786440 | tf_op jit(solution)/shard_map/ppermute | solution.py:290
  13.5 7.4 %copy-start.6 = (bf16[20,128,256]{2,1,0:T(8,128)(2,1)}, bf16[20,128,256]{2,1,0:T(8,128)(2,1)S(1)}, u32[]{:S(2)}) copy-start(bf16[20,128,256]{2,1,0:T(8,128)(2,1)S(1)} %forward_taps.1.taps) | copy-start | bytes 3932164
  13.5 10.2 %collective-permute-start.1 = (bf16[16,16,512]{2,1,0:T(8,128)(2,1)S(1)}, bf16[16,16,512]{2,1,0:T(8,128)(2,1)S(1)}, u32[]{:S(2)}, u32[]{:S(2)}) collective-permute-start(bf16[16,16,512]{2,1,0:T(8,128)(2,1)S(1)} %get-tuple-element.25), channel_id=1, source_target_pairs={{0,15},{1,0},{2,1},{3,2},{4,3},{5,4},{6,5},{7,6},{8,7},{9,8},{10,9... | collective-permute-start | bytes 786440 | tf_op jit(solution)/shard_map/ppermute | solution.py:290
  20.9 5.0 %collective-permute-start.6 = (bf16[16,64,512]{2,1,0:T(8,128)(2,1)S(1)}, bf16[16,64,512]{2,1,0:T(8,128)(2,1)S(1)}, u32[]{:S(2)}, u32[]{:S(2)}) collective-permute-start(bf16[16,64,512]{2,1,0:T(8,128)(2,1)S(1)} %get-tuple-element.12), channel_id=1, source_target_pairs={{0,16},{16,0},{1,17},{17,1},{2,18},{18,2},{3,19},{19,3},{4,20},{20... | collective-permute-start | bytes 3145736 | tf_op jit(solution)/shard_map/ppermute | solution.py:294
  27.2 28.2 %all-to-all-start = ((bf16[16,64,512]{2,1,0:T(8,128)(2,1)}), bf16[16,64,512]{2,1,0:T(8,128)(2,1)S(1)}, u32[]{:S(2)}, u32[]{:S(2)}) async-start(bf16[16,64,512]{2,1,0:T(8,128)(2,1)} %pair_sum.1.after), calls=%async_computation | async-start | bytes 2097152 | tf_op jit(solution)/shard_map/all_to_all | solution.py:403
  36.6 7.3 %collective-permute-start.7 = (bf16[2,2,2,16,512]{4,3,2,1,0:T(8,128)(2,1)S(1)}, bf16[2,2,2,16,512]{4,3,2,1,0:T(8,128)(2,1)S(1)}, u32[]{:S(2)}, u32[]{:S(2)}) collective-permute-start(bf16[2,2,2,16,512]{4,3,2,1,0:T(8,128)(2,1)S(1)} %get-tuple-element.13), channel_id=1, source_target_pairs={{0,1},{1,2},{2,3},{3,4},{4,5},{5,6},{6,7},{7,8},{8,9},{9,10},{10,1... | collective-permute-start | bytes 393224 | tf_op jit(solution)/shard_map/ppermute | solution.py:290
  36.7 7.2 %copy-start.2 = (bf16[4,512,512]{2,1,0:T(8,128)(2,1)S(1)}, bf16[4,512,512]{2,1,0:T(8,128)(2,1)}, u32[]{:S(2)}) copy-start(bf16[4,512,512]{2,1,0:T(8,128)(2,1)} %mixing.3) | copy-start | bytes 6291460
  36.7 7.2 %copy-start.7 = (bf16[20,128,256]{2,1,0:T(8,128)(2,1)S(1)}, bf16[20,128,256]{2,1,0:T(8,128)(2,1)}, u32[]{:S(2)}) copy-start(bf16[20,128,256]{2,1,0:T(8,128)(2,1)} %copy-done.6) | copy-start | bytes 3932164
  36.7 7.2 %collective-permute-start.8 = (bf16[2,2,2,16,512]{4,3,2,1,0:T(8,128)(2,1)S(1)}, bf16[2,2,2,16,512]{4,3,2,1,0:T(8,128)(2,1)S(1)}, u32[]{:S(2)}, u32[]{:S(2)}) collective-permute-start(bf16[2,2,2,16,512]{4,3,2,1,0:T(8,128)(2,1)S(1)} %get-tuple-element.14), channel_id=1, source_target_pairs={{0,15},{1,0},{2,1},{3,2},{4,3},{5,4},{6,5},{7,6},{8,7},{9,8},{10,9... | collective-permute-start | bytes 393224 | tf_op jit(solution)/shard_map/ppermute | solution.py:290
  55.6 9.0 %collective-permute-start.10 = (bf16[64,512]{1,0:T(8,128)(2,1)S(1)}, bf16[64,512]{1,0:T(8,128)(2,1)S(1)}, u32[]{:S(2)}, u32[]{:S(2)}) collective-permute-start(bf16[64,512]{1,0:T(8,128)(2,1)S(1)} %chip_sum.1.one), channel_id=1, source_target_pairs={{0,4},{1,5},{2,6},{3,7},{4,0},{5,1},{6,2},{7,3},{8,12},{9,13},{10,... | collective-permute-start | bytes 196616 | tf_op jit(solution)/shard_map/ppermute | solution.py:294
  56.0 8.5 %collective-permute-start.11 = (bf16[64,512]{1,0:T(8,128)(2,1)S(1)}, bf16[64,512]{1,0:T(8,128)(2,1)S(1)}, u32[]{:S(2)}, u32[]{:S(2)}) collective-permute-start(bf16[64,512]{1,0:T(8,128)(2,1)S(1)} %chip_sum.1.one), channel_id=1, source_target_pairs={{0,6},{1,7},{2,4},{3,5},{4,2},{5,3},{6,0},{7,1},{8,14},{9,15},{10,... | collective-permute-start | bytes 196616 | tf_op jit(solution)/shard_map/ppermute | solution.py:294
  58.6 7.4 %collective-permute-start.9 = (bf16[64,512]{1,0:T(8,128)(2,1)S(1)}, bf16[64,512]{1,0:T(8,128)(2,1)S(1)}, u32[]{:S(2)}, u32[]{:S(2)}) collective-permute-start(bf16[64,512]{1,0:T(8,128)(2,1)S(1)} %chip_sum.1.one), channel_id=1, source_target_pairs={{0,2},{1,3},{2,0},{3,1},{4,6},{5,7},{6,4},{7,5},{8,10},{9,11},{10,... | collective-permute-start | bytes 196616 | tf_op jit(solution)/shard_map/ppermute | solution.py:294
  66.0 4.4 %collective-permute-start.12 = (bf16[64,512]{1,0:T(8,128)(2,1)S(1)}, bf16[64,512]{1,0:T(8,128)(2,1)S(1)}, u32[]{:S(2)}, u32[]{:S(2)}) collective-permute-start(bf16[64,512]{1,0:T(8,128)(2,1)S(1)} %four_sum.1.own), channel_id=1, source_target_pairs={{0,1},{1,0},{2,3},{3,2},{4,5},{5,4},{6,7},{7,6},{8,9},{9,8},{10,11... | collective-permute-start | bytes 196616 | tf_op jit(solution)/shard_map/ppermute | solution.py:294
  66.1 4.3 %collective-permute-start.13 = (bf16[64,512]{1,0:T(8,128)(2,1)S(1)}, bf16[64,512]{1,0:T(8,128)(2,1)S(1)}, u32[]{:S(2)}, u32[]{:S(2)}) collective-permute-start(bf16[64,512]{1,0:T(8,128)(2,1)S(1)} %four_sum.1.own), channel_id=1, source_target_pairs={{0,8},{8,0},{1,9},{9,1},{2,10},{10,2},{3,11},{11,3},{4,12},{12,4},... | collective-permute-start | bytes 196616 | tf_op jit(solution)/shard_map/ppermute | solution.py:294
  67.8 5.2 %collective-permute-start.14 = (bf16[64,512]{1,0:T(8,128)(2,1)S(1)}, bf16[64,512]{1,0:T(8,128)(2,1)S(1)}, u32[]{:S(2)}, u32[]{:S(2)}) collective-permute-start(bf16[64,512]{1,0:T(8,128)(2,1)S(1)} %four_sum.1.own), channel_id=1, source_target_pairs={{0,9},{1,8},{2,11},{3,10},{4,13},{5,12},{6,15},{7,14},{8,1},{9,0},... | collective-permute-start | bytes 196616 | tf_op jit(solution)/shard_map/ppermute | solution.py:294

commit v8 on v7

--- a/solution.py
+++ b/solution.py
@@ -18,7 +18,7 @@
 BF16 = jnp.bfloat16
 VMEM = pl.BlockSpec(memory_space=pltpu.VMEM)
 SMEM = pl.BlockSpec(memory_space=pltpu.SMEM)
-PARAMS = pltpu.CompilerParams(vmem_limit_bytes=24 * 1024 * 1024)
+PARAMS = pltpu.CompilerParams(vmem_limit_bytes=16 * 1024 * 1024)
 
 
 def iota(shape, axis):

time: 74.6 us -> 74.6 us (level)
  no operation moved by 1% of the time
where the time goes in v8:
time: 74.6 us; the launch traced here: 74.2 us
  starting transfers between devices  37.7 us (51%)
  Pallas kernels  18.7 us (25%)
  waiting for transfers between devices  13.2 us (18%)
  local copies, waits for them, and re-layouts  3.04 us (4%)
  between operations  0.84 us (1%)
    pallas_call x11, Pallas kernels, call(): pl.pallas_call(kernel, out_shape=outs, in_specs=specs, out_specs=jax.tree...  18.7 us
    ppermute x6, starting transfers between devices, shift(): lax.ppermute(cells, axis, [(i, (i + step) % count) for i in range(count)])  14.4 us
    ppermute x8, starting transfers between devices, swap(): return lax.ppermute(cells, axis, [(i, i ^ mask) for i in range(count)])  12.9 us
    ppermute x8, waiting for transfers between devices, swap(): return lax.ppermute(cells, axis, [(i, i ^ mask) for i in range(count)])  9.44 us
    all_to_all x1, starting transfers between devices, local(): parts = lax.all_to_all(summed, ('y', 'xh', 'xl'), 0, 0)  8.82 us
    all_to_all x1, waiting for transfers between devices, local(): parts = lax.all_to_all(summed, ('y', 'xh', 'xl'), 0, 0)  3.11 us
    another operation x2, local copies, waits for them, and re-layouts, local(): top = jnp.stack([cells[:HL] for cells in both])  1.82 us
    ppermute x1, starting transfers between devices, local(): outer = lax.ppermute(outer, LAT, pairs)  1.55 us
  transfers between devices with their start and end apart: 16, of which 8 were waited for; matrix products, arithmetic and copies ran while one was open for 2% of the time, Pallas kernels for 22%

profile of v8, /device:TPU:2, one launch (start us, length us, event | category | flops | bytes accessed | tf_op | source)
XLA Modules:
  0.0 74.2 jit_solution(15791103325243929247)
XLA Ops:
  0.6 0.0 copy-start.1
  0.6 0.0 copy-start.5
  0.7 0.0 copy-start.3
  0.7 0.0 copy-start.4
  0.7 0.9 %slice_bitcast_fusion.3 = (bf16[1,2,32,512]{3,2,1,0:T(8,128)(2,1)S(1)}, bf16[1,2,32,512]{3,2,1,0:T(8,128)(2,1)S(1)}) fusion(bf16[16,32,512]{2,1,0:T(8,128)(2,1)} %center.4), kind=kLoop, calls=%fused_computation.7 | loop fusion | bytes 262144 | tf_op jit(solution)/shard_map/stack | solution.py:331
  1.6 0.9 %slice_bitcast_fusion.2 = (bf16[1,2,32,512]{3,2,1,0:T(8,128)(2,1)S(1)}, bf16[1,2,32,512]{3,2,1,0:T(8,128)(2,1)S(1)}) fusion(bf16[16,32,512]{2,1,0:T(8,128)(2,1)} %center.5), kind=kLoop, calls=%fused_computation.6 | loop fusion | bytes 262144 | tf_op jit(solution)/shard_map/stack | solution.py:331
  2.5 0.7 broadcast_select_fusion
  3.2 0.0 collective-permute-start.4
  3.2 1.6 %collective-permute-start.5 = (bf16[2,2,32,512]{3,2,1,0:T(8,128)(2,1)}, bf16[2,2,32,512]{3,2,1,0:T(8,128)(2,1)S(1)}, u32[]{:S(2)}, u32[]{:S(2)}) collective-permute-start(bf16[2,2,32,512]{3,2,1,0:T(8,128)(2,1)} %get-tuple-element.27), channel_id=1, source_target_pairs={{0,0},{240,240},{16,32},{32,16},{48,64},{64,48},{80,96},{96,80},{1... | collective-permute-start | bytes 393224 | tf_op jit(solution)/shard_map/ppermute | solution.py:356
  4.7 1.1 %fusion = (bf16[16,16,512]{2,1,0:T(8,128)(2,1)S(1)}, bf16[16,16,512]{2,1,0:T(8,128)(2,1)S(1)}) fusion(bf16[16,32,512]{2,1,0:T(8,128)(2,1)} %center.4), kind=kLoop, calls=%fused_computation.8 | loop fusion | bytes 1048576 | tf_op jit(solution)/shard_map/slice | solution.py:336
  5.8 2.0 %collective-permute-start.2 = (bf16[16,16,512]{2,1,0:T(8,128)(2,1)S(1)}, bf16[16,16,512]{2,1,0:T(8,128)(2,1)S(1)}, u32[]{:S(2)}, u32[]{:S(2)}) collective-permute-start(bf16[16,16,512]{2,1,0:T(8,128)(2,1)S(1)} %get-tuple-element.24), channel_id=1, source_target_pairs={{0,1},{1,2},{2,3},{3,4},{4,5},{5,6},{6,7},{7,8},{8,9},{9,10},{10,1... | collective-permute-start | bytes 786440 | tf_op jit(solution)/shard_map/ppermute | solution.py:290
  7.8 4.0 %collective-permute-start.3 = (bf16[16,16,512]{2,1,0:T(8,128)(2,1)S(1)}, bf16[16,16,512]{2,1,0:T(8,128)(2,1)S(1)}, u32[]{:S(2)}, u32[]{:S(2)}) collective-permute-start(bf16[16,16,512]{2,1,0:T(8,128)(2,1)S(1)} %get-tuple-element.23), channel_id=1, source_target_pairs={{0,15},{1,0},{2,1},{3,2},{4,3},{5,4},{6,5},{7,6},{8,7},{9,8},{10,9... | collective-permute-start | bytes 786440 | tf_op jit(solution)/shard_map/ppermute | solution.py:290
  11.8 0.0 copy-done.1
  11.8 0.0 copy-start
  11.9 0.1 collective-permute-start
  12.0 0.1 stack.41.place
  12.1 0.0 copy-done.5
  12.1 0.0 copy-done.3
  12.1 0.0 copy-done.4
  12.1 1.4 %forward_taps.1.taps = bf16[20,128,256]{2,1,0:T(8,128)(2,1)S(1)} custom-call(s32[6]{0:T(128)S(1)} %stack.41.place, bf16[4,4,4,256]{3,2,1,0:T(4,128)(2,1)S(1)} %bitcast.16, s32[4,256]{1,0:T(4,128)S(1)} %bitcast.20, s32[4,256]{1,0:T(4,128)S(1)} %bitcast.18), custom_call_target="tpu_custom_call" | custom-call | flops 1000000000 | bytes 1000000 | tf_op jit(solution)/shard_map/forward_taps/pallas_call | solution.py:298
  13.5 0.0 copy-start.6
  13.5 0.0 collective-permute-done.4.inner
  13.5 4.2 %collective-permute-start.1 = (bf16[16,16,512]{2,1,0:T(8,128)(2,1)S(1)}, bf16[16,16,512]{2,1,0:T(8,128)(2,1)S(1)}, u32[]{:S(2)}, u32[]{:S(2)}) collective-permute-start(bf16[16,16,512]{2,1,0:T(8,128)(2,1)S(1)} %get-tuple-element.25), channel_id=1, source_target_pairs={{0,15},{1,0},{2,1},{3,2},{4,3},{5,4},{6,5},{7,6},{8,7},{9,8},{10,9... | collective-permute-start | bytes 786440 | tf_op jit(solution)/shard_map/ppermute | solution.py:290
  17.7 0.0 collective-permute-done.5.outer
  17.7 0.0 collective-permute-done.2.west
  17.7 0.0 collective-permute-done.3.east
  17.7 0.0 copy-done
  17.7 3.2 %terms.1 = (f32[16,64,512]{2,1,0:T(8,128)S(1)}, bf16[16,64,512]{2,1,0:T(8,128)(2,1)S(1)}) custom-call(s32[6]{0:T(128)S(1)} %stack.41.place, s32[4,256]{1,0:T(4,128)S(1)} %bitcast.21, bf16[20,128,256]{2,1,0:T(8,128)(2,1)S(1)} %forward_taps.1.taps, bf16[16,32,512]{2,1,0:T(8,128)(2,1)S(1)} %copy-done, bf16[16,16,512]{2,1,0:T(8,128)(2,1)S(1)} %collective-permute-done.2.west, ...), custom_call_target="tpu_custom_call" | custom-call | flops 20000000000 | bytes 8000000 | tf_op jit(solution)/shard_map/terms/pallas_call | solution.py:298
  20.9 0.0 copy-done.6
  20.9 2.7 %collective-permute-start.6 = (bf16[16,64,512]{2,1,0:T(8,128)(2,1)S(1)}, bf16[16,64,512]{2,1,0:T(8,128)(2,1)S(1)}, u32[]{:S(2)}, u32[]{:S(2)}) collective-permute-start(bf16[16,64,512]{2,1,0:T(8,128)(2,1)S(1)} %get-tuple-element.12), channel_id=1, source_target_pairs={{0,16},{16,0},{1,17},{17,1},{2,18},{18,2},{3,19},{19,3},{4,20},{20... | collective-permute-start | bytes 3145736 | tf_op jit(solution)/shard_map/ppermute | solution.py:294
  23.7 0.0 collective-permute-done.west
  23.7 0.0 collective-permute-done.1.east
  23.7 2.3 %collective-permute-done.6.recv = bf16[16,64,512]{2,1,0:T(8,128)(2,1)S(1)} collective-permute-done((bf16[16,64,512]{2,1,0:T(8,128)(2,1)S(1)}, bf16[16,64,512]{2,1,0:T(8,128)(2,1)S(1)}, u32[]{:S(2)}, u32[]{:S(2)}) %collective-permute-start.6) | collective-permute-done | bytes 1048608 | tf_op jit(solution)/shard_map/ppermute | solution.py:294
  26.0 1.2 %pair_sum.1.after = bf16[16,64,512]{2,1,0:T(8,128)(2,1)} custom-call(f32[8,128]{1,0:T(8,128)S(1)} %ready.1.after, f32[16,64,512]{2,1,0:T(8,128)S(1)} %get-tuple-element.11.keep, bf16[16,64,512]{2,1,0:T(8,128)(2,1)S(1)} %collective-permute-done.6.recv), custom_call_target="tpu_custom_call" | custom-call | flops 524288 | bytes 4194304 | tf_op jit(solution)/shard_map/pair_sum/pallas_call | solution.py:298
  27.2 8.8 %all-to-all-start = ((bf16[16,64,512]{2,1,0:T(8,128)(2,1)}), bf16[16,64,512]{2,1,0:T(8,128)(2,1)S(1)}, u32[]{:S(2)}, u32[]{:S(2)}) async-start(bf16[16,64,512]{2,1,0:T(8,128)(2,1)} %pair_sum.1.after), calls=%async_computation | async-start | bytes 2097152 | tf_op jit(solution)/shard_map/all_to_all | solution.py:403
  36.0 0.6 rims.1
  36.6 0.1 collective-permute-start.7
  36.7 0.0 copy-start.2
  36.7 0.0 copy-start.7
  36.7 4.1 %collective-permute-start.8 = (bf16[2,2,2,16,512]{4,3,2,1,0:T(8,128)(2,1)S(1)}, bf16[2,2,2,16,512]{4,3,2,1,0:T(8,128)(2,1)S(1)}, u32[]{:S(2)}, u32[]{:S(2)}) collective-permute-start(bf16[2,2,2,16,512]{4,3,2,1,0:T(8,128)(2,1)S(1)} %get-tuple-element.14), channel_id=1, source_target_pairs={{0,15},{1,0},{2,1},{3,2},{4,3},{5,4},{6,5},{7,6},{8,7},{9,8},{10,9... | collective-permute-start | bytes 393224 | tf_op jit(solution)/shard_map/ppermute | solution.py:290
  40.8 2.5 %adjoint_taps.1.taps = bf16[16,128,320]{2,1,0:T(8,128)(2,1)S(1)} custom-call(s32[6]{0:T(128)S(1)} %stack.41.place, bf16[16,64,512]{2,1,0:T(8,128)(2,1)} %pair_sum.1.after, bf16[4,4,4,256]{3,2,1,0:T(4,128)(2,1)S(1)} %bitcast.17, s32[4,256]{1,0:T(4,128)S(1)} %bitcast.22, s32[4,256]{1,0:T(4,128)S(1)} %bitcast.19), custom_call_target="tpu_custom_call" | custom-call | flops 2000000000 | bytes 2000000 | tf_op jit(solution)/shard_map/adjoint_taps/pallas_call | solution.py:298
  43.3 0.6 collective-permute-done.7.rims_w
  43.9 0.0 collective-permute-done.8.rims_e
  43.9 0.0 copy-done.2
  43.9 0.0 copy-done.7
  43.9 3.9 %output.1 = (bf16[16,32,512]{2,1,0:T(8,128)(2,1)}, f32[8,128]{1,0:T(8,128)S(1)}) custom-call(s32[6]{0:T(128)S(1)} %stack.41.place, bf16[16,64,512]{2,1,0:T(8,128)(2,1)} %pair_sum.1.after, s32[4,256]{1,0:T(4,128)S(1)} %bitcast.23, bf16[20,128,256]{2,1,0:T(8,128)(2,1)S(1)} %copy-done.7, bf16[16,32,512]{2,1,0:T(8,128)(2,1)S(1)} %copy-done, ...), custom_call_target="tpu_custom_call" | custom-call | flops 3000000000 | bytes 6000000 | tf_op jit(solution)/shard_map/output/pallas_call | solution.py:298
  47.9 4.4 %adjoint.1 = (bf16[16,32,512]{2,1,0:T(8,128)(2,1)}, f32[8,128]{1,0:T(8,128)S(1)}) custom-call(s32[6]{0:T(128)S(1)} %stack.41.place, bf16[16,64,512]{2,1,0:T(8,128)(2,1)} %pair_sum.1.after, bf16[16,128,320]{2,1,0:T(8,128)(2,1)S(1)} %adjoint_taps.1.taps, bf16[16,32,512]{2,1,0:T(8,128)(2,1)S(1)} %copy-done.1, ...), custom_call_target="tpu_custom_call" | custom-call | flops 3000000000 | bytes 6000000 | tf_op jit(solution)/shard_map/adjoint/pallas_call | solution.py:298
  52.3 3.1 %all-to-all-done.parts = bf16[16,64,512]{2,1,0:T(8,128)(2,1)S(1)} async-done(((bf16[16,64,512]{2,1,0:T(8,128)(2,1)}), bf16[16,64,512]{2,1,0:T(8,128)(2,1)S(1)}, u32[]{:S(2)}, u32[]{:S(2)}) %all-to-all-start) | async-done | bytes 1048608 | tf_op jit(solution)/shard_map/all_to_all | solution.py:403
  55.4 0.1 chip_sum.1.one
  55.6 0.5 collective-permute-start.10
  56.0 2.6 %collective-permute-start.11 = (bf16[64,512]{1,0:T(8,128)(2,1)S(1)}, bf16[64,512]{1,0:T(8,128)(2,1)S(1)}, u32[]{:S(2)}, u32[]{:S(2)}) collective-permute-start(bf16[64,512]{1,0:T(8,128)(2,1)S(1)} %chip_sum.1.one), channel_id=1, source_target_pairs={{0,6},{1,7},{2,4},{3,5},{4,2},{5,3},{6,0},{7,1},{8,14},{9,15},{10,... | collective-permute-start | bytes 196616 | tf_op jit(solution)/shard_map/ppermute | solution.py:294
  58.6 3.6 %collective-permute-start.9 = (bf16[64,512]{1,0:T(8,128)(2,1)S(1)}, bf16[64,512]{1,0:T(8,128)(2,1)S(1)}, u32[]{:S(2)}, u32[]{:S(2)}) collective-permute-start(bf16[64,512]{1,0:T(8,128)(2,1)S(1)} %chip_sum.1.one), channel_id=1, source_target_pairs={{0,2},{1,3},{2,0},{3,1},{4,6},{5,7},{6,4},{7,5},{8,10},{9,11},{10,... | collective-permute-start | bytes 196616 | tf_op jit(solution)/shard_map/ppermute | solution.py:294
  62.2 2.4 %collective-permute-done.10.three = bf16[64,512]{1,0:T(8,128)(2,1)S(1)} collective-permute-done((bf16[64,512]{1,0:T(8,128)(2,1)S(1)}, bf16[64,512]{1,0:T(8,128)(2,1)S(1)}, u32[]{:S(2)}, u32[]{:S(2)}) %collective-permute-start.10) | collective-permute-done | bytes 65568 | tf_op jit(solution)/shard_map/ppermute | solution.py:294
  64.6 0.0 collective-permute-done.11.four
  64.6 1.4 %collective-permute-done.9.two = bf16[64,512]{1,0:T(8,128)(2,1)S(1)} collective-permute-done((bf16[64,512]{1,0:T(8,128)(2,1)S(1)}, bf16[64,512]{1,0:T(8,128)(2,1)S(1)}, u32[]{:S(2)}, u32[]{:S(2)}) %collective-permute-start.9) | collective-permute-done | bytes 65568 | tf_op jit(solution)/shard_map/ppermute | solution.py:294
  66.0 0.1 collective-permute-start.12
  66.1 1.7 %collective-permute-start.13 = (bf16[64,512]{1,0:T(8,128)(2,1)S(1)}, bf16[64,512]{1,0:T(8,128)(2,1)S(1)}, u32[]{:S(2)}, u32[]{:S(2)}) collective-permute-start(bf16[64,512]{1,0:T(8,128)(2,1)S(1)} %four_sum.1.own), channel_id=1, source_target_pairs={{0,8},{8,0},{1,9},{9,1},{2,10},{10,2},{3,11},{11,3},{4,12},{12,4},... | collective-permute-start | bytes 196616 | tf_op jit(solution)/shard_map/ppermute | solution.py:294
  67.8 1.8 %collective-permute-start.14 = (bf16[64,512]{1,0:T(8,128)(2,1)S(1)}, bf16[64,512]{1,0:T(8,128)(2,1)S(1)}, u32[]{:S(2)}, u32[]{:S(2)}) collective-permute-start(bf16[64,512]{1,0:T(8,128)(2,1)S(1)} %four_sum.1.own), channel_id=1, source_target_pairs={{0,9},{1,8},{2,11},{3,10},{4,13},{5,12},{6,15},{7,14},{8,1},{9,0},... | collective-permute-start | bytes 196616 | tf_op jit(solution)/shard_map/ppermute | solution.py:294
  69.6 0.8 %collective-permute-done.12.by_z = bf16[64,512]{1,0:T(8,128)(2,1)S(1)} collective-permute-done((bf16[64,512]{1,0:T(8,128)(2,1)S(1)}, bf16[64,512]{1,0:T(8,128)(2,1)S(1)}, u32[]{:S(2)}, u32[]{:S(2)}) %collective-permute-start.12) | collective-permute-done | bytes 65568 | tf_op jit(solution)/shard_map/ppermute | solution.py:294
  70.3 0.1 collective-permute-done.13.by_x
  70.4 2.5 %collective-permute-done.14.by_both = bf16[64,512]{1,0:T(8,128)(2,1)S(1)} collective-permute-done((bf16[64,512]{1,0:T(8,128)(2,1)S(1)}, bf16[64,512]{1,0:T(8,128)(2,1)S(1)}, u32[]{:S(2)}, u32[]{:S(2)}) %collective-permute-start.14) | collective-permute-done | bytes 65568 | tf_op jit(solution)/shard_map/ppermute | solution.py:294
  72.9 1.3 %last_sum.1 = f32[4,32,512]{2,1,0:T(8,128)} custom-call(s32[6]{0:T(128)S(1)} %stack.41.place, bf16[64,512]{1,0:T(8,128)(2,1)S(1)} %four_sum.1.own, bf16[64,512]{1,0:T(8,128)(2,1)S(1)} %collective-permute-done.12.by_z, bf16[64,512]{1,0:T(8,128)(2,1)S(1)} %collective-permute-done.13.by_x, bf16[64,512]{1,0:T(8,128)(2,1)S(1)} %collective-permute-done.14.by_both), custom_call_target="tpu_custom_call" | custom-call | flops 131072 | bytes 524288 | tf_op jit(solution)/shard_map/last_sum/pallas_call | solution.py:298
  (3 shorter events, 0.1 us)
Async XLA Ops:
  0.6 11.2 %copy-start.1 = (bf16[16,32,512]{2,1,0:T(8,128)(2,1)S(1)}, bf16[16,32,512]{2,1,0:T(8,128)(2,1)}, u32[]{:S(2)}) copy-start(bf16[16,32,512]{2,1,0:T(8,128)(2,1)} %center.5) | copy-start | bytes 1572868
  0.6 11.4 %copy-start.5 = (s32[256,4]{0,1:T(4,128)S(1)}, s32[256,4]{0,1:T(4,128)}, u32[]{:S(2)}) copy-start(s32[256,4]{0,1:T(4,128)} %param.8) | copy-start | bytes 12292
  0.7 11.4 %copy-start.3 = (bf16[4,256,4,4]{1,3,2,0:T(4,128)(2,1)S(1)}, bf16[4,256,4,4]{1,3,2,0:T(4,128)(2,1)}, u32[]{:S(2)}) copy-start(bf16[4,256,4,4]{1,3,2,0:T(4,128)(2,1)} %param.7) | copy-start | bytes 98308
  0.7 11.4 %copy-start.4 = (s32[256,4]{0,1:T(4,128)S(1)}, s32[256,4]{0,1:T(4,128)}, u32[]{:S(2)}) copy-start(s32[256,4]{0,1:T(4,128)} %param.9) | copy-start | bytes 12292
  3.2 10.3 %collective-permute-start.4 = (bf16[2,2,32,512]{3,2,1,0:T(8,128)(2,1)S(1)}, bf16[2,2,32,512]{3,2,1,0:T(8,128)(2,1)S(1)}, u32[]{:S(2)}, u32[]{:S(2)}) collective-permute-start(bf16[2,2,32,512]{3,2,1,0:T(8,128)(2,1)S(1)} %get-tuple-element.28), channel_id=1, source_target_pairs={{0,16},{16,0},{32,48},{48,32},{64,80},{80,64},{96,112},{112,96},{1... | collective-permute-start | bytes 393224 | tf_op jit(solution)/shard_map/ppermute | solution.py:294
  3.2 14.5 %collective-permute-start.5 = (bf16[2,2,32,512]{3,2,1,0:T(8,128)(2,1)}, bf16[2,2,32,512]{3,2,1,0:T(8,128)(2,1)S(1)}, u32[]{:S(2)}, u32[]{:S(2)}) collective-permute-start(bf16[2,2,32,512]{3,2,1,0:T(8,128)(2,1)} %get-tuple-element.27), channel_id=1, source_target_pairs={{0,0},{240,240},{16,32},{32,16},{48,64},{64,48},{80,96},{96,80},{1... | collective-permute-start | bytes 393224 | tf_op jit(solution)/shard_map/ppermute | solution.py:356
  5.8 11.9 %collective-permute-start.2 = (bf16[16,16,512]{2,1,0:T(8,128)(2,1)S(1)}, bf16[16,16,512]{2,1,0:T(8,128)(2,1)S(1)}, u32[]{:S(2)}, u32[]{:S(2)}) collective-permute-start(bf16[16,16,512]{2,1,0:T(8,128)(2,1)S(1)} %get-tuple-element.24), channel_id=1, source_target_pairs={{0,1},{1,2},{2,3},{3,4},{4,5},{5,6},{6,7},{7,8},{8,9},{9,10},{10,1... | collective-permute-start | bytes 786440 | tf_op jit(solution)/shard_map/ppermute | solution.py:290
  7.8 9.9 %collective-permute-start.3 = (bf16[16,16,512]{2,1,0:T(8,128)(2,1)S(1)}, bf16[16,16,512]{2,1,0:T(8,128)(2,1)S(1)}, u32[]{:S(2)}, u32[]{:S(2)}) collective-permute-start(bf16[16,16,512]{2,1,0:T(8,128)(2,1)S(1)} %get-tuple-element.23), channel_id=1, source_target_pairs={{0,15},{1,0},{2,1},{3,2},{4,3},{5,4},{6,5},{7,6},{8,7},{9,8},{10,9... | collective-permute-start | bytes 786440 | tf_op jit(solution)/shard_map/ppermute | solution.py:290
  11.8 5.9 %copy-start = (bf16[16,32,512]{2,1,0:T(8,128)(2,1)S(1)}, bf16[16,32,512]{2,1,0:T(8,128)(2,1)}, u32[]{:S(2)}) copy-start(bf16[16,32,512]{2,1,0:T(8,128)(2,1)} %center.4) | copy-start | bytes 1572868
  11.9 11.8 %collective-permute-start = (bf16[16,16,512]{2,1,0:T(8,128)(2,1)S(1)}, bf16[16,16,512]{2,1,0:T(8,128)(2,1)S(1)}, u32[]{:S(2)}, u32[]{:S(2)}) collective-permute-start(bf16[16,16,512]{2,1,0:T(8,128)(2,1)S(1)} %get-tuple-element.26), channel_id=1, source_target_pairs={{0,1},{1,2},{2,3},{3,4},{4,5},{5,6},{6,7},{7,8},{8,9},{9,10},{10,1... | collective-permute-start | bytes 786440 | tf_op jit(solution)/shard_map/ppermute | solution.py:290
  13.5 7.4 %copy-start.6 = (bf16[20,128,256]{2,1,0:T(8,128)(2,1)}, bf16[20,128,256]{2,1,0:T(8,128)(2,1)S(1)}, u32[]{:S(2)}) copy-start(bf16[20,128,256]{2,1,0:T(8,128)(2,1)S(1)} %forward_taps.1.taps) | copy-start | bytes 3932164
  13.5 10.2 %collective-permute-start.1 = (bf16[16,16,512]{2,1,0:T(8,128)(2,1)S(1)}, bf16[16,16,512]{2,1,0:T(8,128)(2,1)S(1)}, u32[]{:S(2)}, u32[]{:S(2)}) collective-permute-start(bf16[16,16,512]{2,1,0:T(8,128)(2,1)S(1)} %get-tuple-element.25), channel_id=1, source_target_pairs={{0,15},{1,0},{2,1},{3,2},{4,3},{5,4},{6,5},{7,6},{8,7},{9,8},{10,9... | collective-permute-start | bytes 786440 | tf_op jit(solution)/shard_map/ppermute | solution.py:290
  20.9 5.0 %collective-permute-start.6 = (bf16[16,64,512]{2,1,0:T(8,128)(2,1)S(1)}, bf16[16,64,512]{2,1,0:T(8,128)(2,1)S(1)}, u32[]{:S(2)}, u32[]{:S(2)}) collective-permute-start(bf16[16,64,512]{2,1,0:T(8,128)(2,1)S(1)} %get-tuple-element.12), channel_id=1, source_target_pairs={{0,16},{16,0},{1,17},{17,1},{2,18},{18,2},{3,19},{19,3},{4,20},{20... | collective-permute-start | bytes 3145736 | tf_op jit(solution)/shard_map/ppermute | solution.py:294
  27.2 28.2 %all-to-all-start = ((bf16[16,64,512]{2,1,0:T(8,128)(2,1)}), bf16[16,64,512]{2,1,0:T(8,128)(2,1)S(1)}, u32[]{:S(2)}, u32[]{:S(2)}) async-start(bf16[16,64,512]{2,1,0:T(8,128)(2,1)} %pair_sum.1.after), calls=%async_computation | async-start | bytes 2097152 | tf_op jit(solution)/shard_map/all_to_all | solution.py:403
  36.6 7.3 %collective-permute-start.7 = (bf16[2,2,2,16,512]{4,3,2,1,0:T(8,128)(2,1)S(1)}, bf16[2,2,2,16,512]{4,3,2,1,0:T(8,128)(2,1)S(1)}, u32[]{:S(2)}, u32[]{:S(2)}) collective-permute-start(bf16[2,2,2,16,512]{4,3,2,1,0:T(8,128)(2,1)S(1)} %get-tuple-element.13), channel_id=1, source_target_pairs={{0,1},{1,2},{2,3},{3,4},{4,5},{5,6},{6,7},{7,8},{8,9},{9,10},{10,1... | collective-permute-start | bytes 393224 | tf_op jit(solution)/shard_map/ppermute | solution.py:290
  36.7 7.2 %copy-start.2 = (bf16[4,512,512]{2,1,0:T(8,128)(2,1)S(1)}, bf16[4,512,512]{2,1,0:T(8,128)(2,1)}, u32[]{:S(2)}) copy-start(bf16[4,512,512]{2,1,0:T(8,128)(2,1)} %mixing.3) | copy-start | bytes 6291460
  36.7 7.2 %copy-start.7 = (bf16[20,128,256]{2,1,0:T(8,128)(2,1)S(1)}, bf16[20,128,256]{2,1,0:T(8,128)(2,1)}, u32[]{:S(2)}) copy-start(bf16[20,128,256]{2,1,0:T(8,128)(2,1)} %copy-done.6) | copy-start | bytes 3932164
  36.7 7.2 %collective-permute-start.8 = (bf16[2,2,2,16,512]{4,3,2,1,0:T(8,128)(2,1)S(1)}, bf16[2,2,2,16,512]{4,3,2,1,0:T(8,128)(2,1)S(1)}, u32[]{:S(2)}, u32[]{:S(2)}) collective-permute-start(bf16[2,2,2,16,512]{4,3,2,1,0:T(8,128)(2,1)S(1)} %get-tuple-element.14), channel_id=1, source_target_pairs={{0,15},{1,0},{2,1},{3,2},{4,3},{5,4},{6,5},{7,6},{8,7},{9,8},{10,9... | collective-permute-start | bytes 393224 | tf_op jit(solution)/shard_map/ppermute | solution.py:290
  55.6 9.0 %collective-permute-start.10 = (bf16[64,512]{1,0:T(8,128)(2,1)S(1)}, bf16[64,512]{1,0:T(8,128)(2,1)S(1)}, u32[]{:S(2)}, u32[]{:S(2)}) collective-permute-start(bf16[64,512]{1,0:T(8,128)(2,1)S(1)} %chip_sum.1.one), channel_id=1, source_target_pairs={{0,4},{1,5},{2,6},{3,7},{4,0},{5,1},{6,2},{7,3},{8,12},{9,13},{10,... | collective-permute-start | bytes 196616 | tf_op jit(solution)/shard_map/ppermute | solution.py:294
  56.0 8.5 %collective-permute-start.11 = (bf16[64,512]{1,0:T(8,128)(2,1)S(1)}, bf16[64,512]{1,0:T(8,128)(2,1)S(1)}, u32[]{:S(2)}, u32[]{:S(2)}) collective-permute-start(bf16[64,512]{1,0:T(8,128)(2,1)S(1)} %chip_sum.1.one), channel_id=1, source_target_pairs={{0,6},{1,7},{2,4},{3,5},{4,2},{5,3},{6,0},{7,1},{8,14},{9,15},{10,... | collective-permute-start | bytes 196616 | tf_op jit(solution)/shard_map/ppermute | solution.py:294
  58.6 7.4 %collective-permute-start.9 = (bf16[64,512]{1,0:T(8,128)(2,1)S(1)}, bf16[64,512]{1,0:T(8,128)(2,1)S(1)}, u32[]{:S(2)}, u32[]{:S(2)}) collective-permute-start(bf16[64,512]{1,0:T(8,128)(2,1)S(1)} %chip_sum.1.one), channel_id=1, source_target_pairs={{0,2},{1,3},{2,0},{3,1},{4,6},{5,7},{6,4},{7,5},{8,10},{9,11},{10,... | collective-permute-start | bytes 196616 | tf_op jit(solution)/shard_map/ppermute | solution.py:294
  66.0 4.4 %collective-permute-start.12 = (bf16[64,512]{1,0:T(8,128)(2,1)S(1)}, bf16[64,512]{1,0:T(8,128)(2,1)S(1)}, u32[]{:S(2)}, u32[]{:S(2)}) collective-permute-start(bf16[64,512]{1,0:T(8,128)(2,1)S(1)} %four_sum.1.own), channel_id=1, source_target_pairs={{0,1},{1,0},{2,3},{3,2},{4,5},{5,4},{6,7},{7,6},{8,9},{9,8},{10,11... | collective-permute-start | bytes 196616 | tf_op jit(solution)/shard_map/ppermute | solution.py:294
  66.1 4.3 %collective-permute-start.13 = (bf16[64,512]{1,0:T(8,128)(2,1)S(1)}, bf16[64,512]{1,0:T(8,128)(2,1)S(1)}, u32[]{:S(2)}, u32[]{:S(2)}) collective-permute-start(bf16[64,512]{1,0:T(8,128)(2,1)S(1)} %four_sum.1.own), channel_id=1, source_target_pairs={{0,8},{8,0},{1,9},{9,1},{2,10},{10,2},{3,11},{11,3},{4,12},{12,4},... | collective-permute-start | bytes 196616 | tf_op jit(solution)/shard_map/ppermute | solution.py:294
  67.8 5.2 %collective-permute-start.14 = (bf16[64,512]{1,0:T(8,128)(2,1)S(1)}, bf16[64,512]{1,0:T(8,128)(2,1)S(1)}, u32[]{:S(2)}, u32[]{:S(2)}) collective-permute-start(bf16[64,512]{1,0:T(8,128)(2,1)S(1)} %four_sum.1.own), channel_id=1, source_target_pairs={{0,9},{1,8},{2,11},{3,10},{4,13},{5,12},{6,15},{7,14},{8,1},{9,0},... | collective-permute-start | bytes 196616 | tf_op jit(solution)/shard_map/ppermute | solution.py:294
